TPU v7x, 256 devices: a whole 4x4x8 slice. The times are simulated.
256 devices in a mesh: wide: 16 (over z, x_lo), narrow: 16 (over x_hi, y, core).
Axes of the slice: x: 4 (x_hi: 2, x_lo: 2; x = x_hi * 2 + x_lo), y: 4, z: 8, core: 2. Of those that a mesh axis runs over, the one named last changes fastest.
Arguments:
- panel: float32 [32, 4194304], P(None, ('wide', 'narrow'))
- signs: int32 [4194304], P(('wide', 'narrow')), may hold values from -1 to 1, as said below
- sample_rows: int32 [262144], P(('wide', 'narrow')), may hold values from 0 to 16383, as said below
- counts: int32 [256], P(('wide', 'narrow')), may hold values from 256 to 1024, as said below
Outputs:
- mixed: float32 [32, 4194304], P(None, ('wide', 'narrow'))
- gram: float32 [32, 32], replicated
Inputs may be any that keep to these rules, and one draw needn't show every extreme that they name: `sample_rows`: within each block's 1024 slots the indices are distinct and increasing, each below 16384. `counts`: some block has all 1024 slots live. `signs`: each entry is +1 or -1.
All inputs are finite; a program needn't handle non-finite values.
Results may differ from a plain program's by a relative error of at most 0.000098.
Values sent between devices are 32-bit elements; how exact they have to be, the bound alone decides.
No kernel may reach another device: no remote copies, remote signals or barrier semaphores. Data moves between devices by JAX's collectives and lax.ppermute only.
A program may use at most 64 MiB of HBM per device.

v0:
```python
import math

import jax
import jax.numpy as jnp
from jax import lax
from jax.sharding import PartitionSpec as P

LOW = 32
HIGH = 128


def from_partner(array, axis, stride):
    return lax.ppermute(array, axis, [(i, i ^ 1 << stride) for i in range(lax.axis_size(axis))])


def table(n):
    idx = jnp.arange(n)
    both = jnp.bitwise_and(idx[:, None], idx[None, :])
    total = jnp.zeros((n, n), jnp.int32)
    for bit in range(max(n.bit_length(), 1)):
        total = total + jnp.bitwise_and(jnp.right_shift(both, bit), 1)
    return (1 - 2 * jnp.bitwise_and(total, 1)).astype(jnp.float32)


def narrow_section(field, bit):
    partner = from_partner(field, "narrow", bit)
    upper = jnp.bitwise_and(jnp.right_shift(lax.axis_index("narrow"), bit), 1)
    return partner + (1 - 2 * upper).astype(jnp.float32) * field


def wide_section(field, bit):
    partner = from_partner(field, "wide", bit)
    upper = jnp.bitwise_and(jnp.right_shift(lax.axis_index("wide"), bit), 1)
    return partner + (1 - 2 * upper).astype(jnp.float32) * field


def shards(panel, signs, sample_rows, counts):
    width, length = panel.shape
    signed = panel * signs.astype(jnp.float32)[None, :]
    work = signed.reshape(width, length // (LOW * HIGH), LOW, HIGH)
    work = jnp.einsum("pslh,hk->pslk", work, table(HIGH), precision=lax.Precision.HIGHEST)
    work = jnp.einsum("pslk,lm->psmk", work, table(LOW), precision=lax.Precision.HIGHEST)
    work = work.reshape(width, length)
    for bit in range(lax.axis_size("narrow").bit_length() - 1):
        work = narrow_section(work, bit)
    for bit in range(lax.axis_size("wide").bit_length() - 1):
        work = wide_section(work, bit)
    blocks = lax.axis_size("wide") * lax.axis_size("narrow")
    mixed = work * (1.0 / math.sqrt(LOW * HIGH * blocks))
    live = (jnp.arange(sample_rows.shape[0], dtype=jnp.int32) < counts[0]).astype(jnp.float32)
    picked = mixed[:, sample_rows] * live[None, :]
    outer = jnp.einsum("pk,qk->pq", picked, picked, precision=lax.Precision.HIGHEST)
    summed, total = lax.psum((outer, jnp.sum(counts.astype(jnp.float32))), ("wide", "narrow"))
    return (mixed, summed / total)


def solution(mesh):
    placed = (
        P(None, ("wide", "narrow")),
        P(("wide", "narrow")),
        P(("wide", "narrow")),
        P(("wide", "narrow")),
    )
    return jax.shard_map(
        shards,
        mesh=mesh,
        in_specs=placed,
        out_specs=(P(None, ("wide", "narrow")), P()),
        check_vma=False,
    )
```

profile of v0, /device:TPU:2, one launch (start us, length us, event | category | flops | bytes accessed | tf_op | source)
XLA Modules:
  0.0 549.4 jit_solution(11714708065232532249)
XLA Ops:
  0.6 0.8 convert_element_type.44
  1.5 1.8 multiply_bitcast_fusion
  3.2 0.4 copy.29
  3.6 1.9 fusion.3
  5.6 1.9 fusion.43
  7.5 2.5 copy.34
  10.0 0.0 collective-permute-start
  10.0 4.5 collective-permute-done
  14.5 4.2 multiply_add_fusion.6
  18.7 1.6 collective-permute-start.1
  20.3 46.4 %collective-permute-done.1 = f32[32,16384]{1,0:T(8,128)} collective-permute-done((f32[32,16384]{1,0:T(8,128)}, f32[32,16384]{1,0:T(8,128)}, u32[]{:S(2)}, u32[]{:S(2)}) %collective-permute-start.1) | collective-permute-done | bytes 2097184 | tf_op jit(solution)/shard_map/ppermute | solution.py:13
  66.7 2.4 multiply_add_fusion.5
  69.1 0.0 copy-start.1
  69.1 3.3 collective-permute-start.2
  72.4 0.0 copy-done.1
  72.4 45.3 %collective-permute-done.2 = f32[32,16384]{1,0:T(8,128)} collective-permute-done((f32[32,16384]{1,0:T(8,128)S(1)}, f32[32,16384]{1,0:T(8,128)}, u32[]{:S(2)}, u32[]{:S(2)}) %collective-permute-start.2) | collective-permute-done | bytes 2097184 | tf_op jit(solution)/shard_map/ppermute | solution.py:13
  117.7 2.4 multiply_add_fusion.4
  120.1 0.0 copy-start
  120.1 2.2 collective-permute-start.3
  122.3 0.0 copy-done
  122.3 45.4 %collective-permute-done.3 = f32[32,16384]{1,0:T(8,128)} collective-permute-done((f32[32,16384]{1,0:T(8,128)S(1)}, f32[32,16384]{1,0:T(8,128)}, u32[]{:S(2)}, u32[]{:S(2)}) %collective-permute-start.3) | collective-permute-done | bytes 2097184 | tf_op jit(solution)/shard_map/ppermute | solution.py:13
  167.7 2.4 multiply_add_fusion.3
  170.2 2.4 collective-permute-start.4
  172.5 43.4 %collective-permute-done.4 = f32[32,16384]{1,0:T(8,128)} collective-permute-done((f32[32,16384]{1,0:T(8,128)S(1)}, f32[32,16384]{1,0:T(8,128)}, u32[]{:S(2)}, u32[]{:S(2)}) %collective-permute-start.4) | collective-permute-done | bytes 2097184 | tf_op jit(solution)/shard_map/ppermute | solution.py:13
  215.9 3.1 multiply_add_fusion.2
  219.0 1.4 collective-permute-start.5
  220.4 43.3 %collective-permute-done.5 = f32[32,16384]{1,0:T(8,128)} collective-permute-done((f32[32,16384]{1,0:T(8,128)}, f32[32,16384]{1,0:T(8,128)}, u32[]{:S(2)}, u32[]{:S(2)}) %collective-permute-start.5) | collective-permute-done | bytes 2097184 | tf_op jit(solution)/shard_map/ppermute | solution.py:13
  263.7 2.4 multiply_add_fusion.1
  266.1 0.0 copy-start.2
  266.1 2.9 collective-permute-start.6
  269.0 0.0 copy-done.2
  269.0 0.0 copy-start.3
  269.0 86.7 %collective-permute-done.6 = f32[32,16384]{1,0:T(8,128)} collective-permute-done((f32[32,16384]{1,0:T(8,128)S(1)}, f32[32,16384]{1,0:T(8,128)}, u32[]{:S(2)}, u32[]{:S(2)}) %collective-permute-start.6) | collective-permute-done | bytes 2097184 | tf_op jit(solution)/shard_map/ppermute | solution.py:13
  355.8 2.4 multiply_add_fusion
  358.2 6.2 %collective-permute-start.7 = (f32[32,16384]{1,0:T(8,128)S(1)}, f32[32,16384]{1,0:T(8,128)}, u32[]{:S(2)}, u32[]{:S(2)}) collective-permute-start(f32[32,16384]{1,0:T(8,128)S(1)} %multiply_add_fusion), channel_id=1, source_target_pairs={{0,128},{16,144},{32,160},{48,176},{64,192},{80,208},{96,224},{112... | collective-permute-start | bytes 6291464 | tf_op jit(solution)/shard_map/ppermute | solution.py:13
  365.1 0.0 copy-done.3
  365.1 90.2 %collective-permute-done.7 = f32[32,16384]{1,0:T(8,128)} collective-permute-done((f32[32,16384]{1,0:T(8,128)S(1)}, f32[32,16384]{1,0:T(8,128)}, u32[]{:S(2)}, u32[]{:S(2)}) %collective-permute-start.7) | collective-permute-done | bytes 2097184 | tf_op jit(solution)/shard_map/ppermute | solution.py:13
  455.2 3.1 add_multiply_fusion
  458.4 6.3 %copy.26 = f32[32,16384]{0,1:T(8,128)} copy(f32[32,16384]{1,0:T(8,128)} %add_multiply_fusion) | data formatting | bytes 4194304 | tf_op jit(solution)/shard_map/mul | solution.py:49
  464.6 6.2 %gather_fusion = f32[1024,32]{1,0:T(8,128)S(1)} fusion(f32[32,16384]{0,1:T(8,128)} %copy.26, s32[1024]{0:T(1024)S(1)} %fusion.75), kind=kCustom, calls=%fused_computation | custom fusion | bytes 266240 | tf_op jit(solution)/shard_map/gather | solution.py:51
  470.8 1.3 fusion
  472.1 76.1 %all-reduce = (f32[32,32]{1,0:T(8,128)S(1)}, f32[]{:T(128)}) all-reduce(f32[32,32]{1,0:T(8,128)S(1)} %fusion, f32[]{:T(128)} %bitcast.6), channel_id=1, replica_groups=mesh['wide'=16,'narrow'=16] {'wide','narrow'}, use_global_device_ids=true, to_apply=%region_0.0 | all-reduce | flops 1025 | bytes 8200 | tf_op jit(solution)/shard_map/psum | solution.py:53
  548.2 1.2 broadcast_divide_fusion
  (2 shorter events, 0.0 us)
Async XLA Ops:
  10.0 4.5 collective-permute-start
  18.7 48.0 %collective-permute-start.1 = (f32[32,16384]{1,0:T(8,128)}, f32[32,16384]{1,0:T(8,128)}, u32[]{:S(2)}, u32[]{:S(2)}) collective-permute-start(f32[32,16384]{1,0:T(8,128)} %multiply_add_fusion.6), channel_id=1, source_target_pairs={{0,2},{1,3},{2,0},{3,1},{4,6},{5,7},{6,4},{7,5},{8,10},{9,11},{10,... | collective-permute-start | bytes 6291464 | tf_op jit(solution)/shard_map/ppermute | solution.py:13
  69.1 3.3 copy-start.1
  69.1 48.5 %collective-permute-start.2 = (f32[32,16384]{1,0:T(8,128)S(1)}, f32[32,16384]{1,0:T(8,128)}, u32[]{:S(2)}, u32[]{:S(2)}) collective-permute-start(f32[32,16384]{1,0:T(8,128)S(1)} %multiply_add_fusion.5), channel_id=1, source_target_pairs={{0,4},{1,5},{2,6},{3,7},{4,0},{5,1},{6,2},{7,3},{8,12},{9,13},{10,... | collective-permute-start | bytes 6291464 | tf_op jit(solution)/shard_map/ppermute | solution.py:13
  120.1 2.2 copy-start
  120.1 47.6 %collective-permute-start.3 = (f32[32,16384]{1,0:T(8,128)S(1)}, f32[32,16384]{1,0:T(8,128)}, u32[]{:S(2)}, u32[]{:S(2)}) collective-permute-start(f32[32,16384]{1,0:T(8,128)S(1)} %multiply_add_fusion.4), channel_id=1, source_target_pairs={{0,8},{1,9},{2,10},{3,11},{4,12},{5,13},{6,14},{7,15},{8,0},{9,1},... | collective-permute-start | bytes 6291464 | tf_op jit(solution)/shard_map/ppermute | solution.py:13
  170.2 45.7 %collective-permute-start.4 = (f32[32,16384]{1,0:T(8,128)S(1)}, f32[32,16384]{1,0:T(8,128)}, u32[]{:S(2)}, u32[]{:S(2)}) collective-permute-start(f32[32,16384]{1,0:T(8,128)S(1)} %multiply_add_fusion.3), channel_id=1, source_target_pairs={{0,16},{16,0},{32,48},{48,32},{64,80},{80,64},{96,112},{112,96},{1... | collective-permute-start | bytes 6291464 | tf_op jit(solution)/shard_map/ppermute | solution.py:13
  219.0 44.7 %collective-permute-start.5 = (f32[32,16384]{1,0:T(8,128)}, f32[32,16384]{1,0:T(8,128)}, u32[]{:S(2)}, u32[]{:S(2)}) collective-permute-start(f32[32,16384]{1,0:T(8,128)} %multiply_add_fusion.2), channel_id=1, source_target_pairs={{0,32},{16,48},{32,0},{48,16},{64,96},{80,112},{96,64},{112,80},{1... | collective-permute-start | bytes 6291464 | tf_op jit(solution)/shard_map/ppermute | solution.py:13
  266.1 2.9 copy-start.2
  266.1 89.7 %collective-permute-start.6 = (f32[32,16384]{1,0:T(8,128)S(1)}, f32[32,16384]{1,0:T(8,128)}, u32[]{:S(2)}, u32[]{:S(2)}) collective-permute-start(f32[32,16384]{1,0:T(8,128)S(1)} %multiply_add_fusion.1), channel_id=1, source_target_pairs={{0,64},{16,80},{32,96},{48,112},{64,0},{80,16},{96,32},{112,48},{1... | collective-permute-start | bytes 6291464 | tf_op jit(solution)/shard_map/ppermute | solution.py:13
  269.0 96.0 %copy-start.3 = (s32[1024]{0:T(1024)S(1)}, s32[1024]{0:T(1024)}, u32[]{:S(2)}) copy-start(s32[1024]{0:T(1024)} %param.6) | copy-start | bytes 12292
  358.2 97.0 %collective-permute-start.7 = (f32[32,16384]{1,0:T(8,128)S(1)}, f32[32,16384]{1,0:T(8,128)}, u32[]{:S(2)}, u32[]{:S(2)}) collective-permute-start(f32[32,16384]{1,0:T(8,128)S(1)} %multiply_add_fusion), channel_id=1, source_target_pairs={{0,128},{16,144},{32,160},{48,176},{64,192},{80,208},{96,224},{112... | collective-permute-start | bytes 6291464 | tf_op jit(solution)/shard_map/ppermute | solution.py:13
where the time goes:
time: 553 us; the launch traced here: 549 us
  waiting for transfers between devices  405 us (73%)
  blocking collectives  76.1 us (14%)
  other arithmetic  26.4 us (5%)
  starting transfers between devices  19.9 us (4%)
  local copies, waits for them, and re-layouts  15.4 us (3%)
    ppermute x8, waiting for transfers between devices, from_partner(): lax.ppermute(array, axis, [(i, i ^ 1 << stride) for i in range(lax.axis_s...  405 us
    psum x1, blocking collectives, shards(): lax.psum((outer, jnp.sum(counts.astype(jnp.float32))), ('wide', 'narrow'))  76.1 us
    ppermute x8, starting transfers between devices, from_partner(): lax.ppermute(array, axis, [(i, i ^ 1 << stride) for i in range(lax.axis_s...  19.9 us
    add x4, other arithmetic, narrow_section(): return partner + (1 - 2 * upper).astype(jnp.float32) * field  11.5 us
  transfers between devices with their start and end apart: 8, of which 8 were waited for; matrix products, arithmetic and copies ran while one was open for 0% of the time, Pallas kernels for 0%

commit v1 on v0

v1 whole, which is shorter than its diff:
```python
import math

import jax
import jax.numpy as jnp
from jax import lax
from jax.experimental import pallas as pl
from jax.experimental.pallas import tpu as pltpu
from jax.sharding import PartitionSpec as P

LOW = 32
HIGH = 128
LANES = 128
HALF = 64
AXES = ("wide", "narrow")


def signs_of(i, j, n):
    v = jnp.bitwise_and(i, j)
    shift = 1
    while shift < n.bit_length():
        v = jnp.bitwise_xor(v, jnp.right_shift(v, shift))
        shift *= 2
    return (1 - 2 * jnp.bitwise_and(v, 1)).astype(jnp.float32)


def split(x):
    hi = x.astype(jnp.bfloat16)
    lo = (x - hi.astype(jnp.float32)).astype(jnp.bfloat16)
    return hi, lo


def dot(a, b):
    return jnp.dot(a, b, preferred_element_type=jnp.float32)


def butterfly(vs):
    step = 1
    while step < len(vs):
        out = list(vs)
        for i in range(len(vs)):
            if not i & step:
                out[i] = vs[i] + vs[i | step]
                out[i | step] = vs[i] - vs[i | step]
        vs = out
        step *= 2
    return vs


def local_kernel(scale, counts_ref, panel_ref, signs_ref, rows_ref, out_ref, table_ref, even_ref, odd_ref, x_ref):
    s = pl.program_id(0)
    width = panel_ref.shape[0]
    lane = lax.broadcasted_iota(jnp.int32, (16, LANES), 1)

    @pl.when(s == 0)
    def _():
        i = lax.broadcasted_iota(jnp.int32, (HIGH, 2 * HIGH), 0)
        j = lax.broadcasted_iota(jnp.int32, (HIGH, 2 * HIGH), 1)
        j = jnp.where(j < HIGH, j, jnp.bitwise_and(j + HALF, HIGH - 1))
        table_ref[...] = (signs_of(i, j, HIGH) * scale).astype(jnp.bfloat16)
        rows = rows_ref[...]
        samples = rows.shape[1]
        slot = lax.broadcasted_iota(jnp.int32, (1, samples), 1)
        rows = jnp.where(slot < counts_ref[0], rows, -1)
        at = lax.broadcasted_iota(jnp.int32, (HIGH, samples), 0)
        tile = (jnp.right_shift(rows, 7) == at).astype(jnp.float32).astype(jnp.bfloat16)
        inner = (jnp.bitwise_and(rows, HIGH - 1) == at).astype(jnp.float32).astype(jnp.bfloat16)
        mask = lax.dot_general(tile, inner, (((1,), (1,)), ((), ())), preferred_element_type=jnp.float32)
        other = pltpu.roll(mask, HALF, 1)
        low = lax.broadcasted_iota(jnp.int32, (HIGH, LANES), 1) < HALF
        even_ref[...] = jnp.where(low, mask, other)
        odd_ref[...] = jnp.where(low, other, mask)

    for g in range(width // 8):
        vs = [
            panel_ref[8 * g : 8 * g + 8, LANES * a : LANES * (a + 1)]
            * signs_ref[:, LANES * a : LANES * (a + 1)].astype(jnp.float32)
            for a in range(LOW)
        ]
        for a, v in enumerate(butterfly(vs)):
            x_ref[width * a + 8 * g : width * a + 8 * g + 8, :] = v

    table = table_ref[...]
    per = 8
    for c in range(LOW // per):
        hi, lo = split(x_ref[width * per * c : width * per * (c + 1), :])
        z = dot(hi, table) + dot(lo, table)
        for k in range(per):
            a = per * c + k
            y = z[width * k : width * (k + 1), :LANES]
            r = z[width * k : width * (k + 1), LANES:]
            row = 34 * a
            out_ref[row : row + 16, :] = jnp.where(lane < HALF, y[:16], r[16:])
            out_ref[row + 16 : row + 17, :] = even_ref[pl.ds(LOW * s + a, 1), :]
            out_ref[row + 17 : row + 33, :] = jnp.where(lane < HALF, r[:16], y[16:])
            out_ref[row + 33 : row + 34, :] = odd_ref[pl.ds(LOW * s + a, 1), :]


def across_kernel(blocks, in_ref, out_ref, mask_ref):
    i = lax.broadcasted_iota(jnp.int32, (blocks, blocks), 0)
    j = lax.broadcasted_iota(jnp.int32, (blocks, blocks), 1)
    table = signs_of(i, j, blocks).astype(jnp.bfloat16)
    for k in range(0, 16, 2):
        x = jnp.concatenate(
            [in_ref[pl.ds(k, blocks, stride=17), :], in_ref[pl.ds(k + 1, blocks, stride=17), :]], axis=1
        )
        hi, lo = split(x)
        y = dot(table, hi) + dot(table, lo)
        out_ref[pl.ds(k, blocks, stride=16), :] = y[:, :LANES]
        out_ref[pl.ds(k + 1, blocks, stride=16), :] = y[:, LANES:]
    mask_ref[...] = in_ref[pl.ds(16, blocks, stride=17), :]


def gram_kernel(counts_ref, y_ref, mask_ref, out_ref):
    blocks = mask_ref.shape[0]
    low = lax.broadcasted_iota(jnp.int32, (16, LANES), 1) < HALF
    low1 = lax.broadcasted_iota(jnp.int32, (1, LANES), 1) < HALF
    pairs = 8

    def body(c, total):
        plain, masked = [], []
        for k in range(pairs):
            d = 2 * pairs * c + 2 * k
            first = y_ref[pl.ds(pl.multiple_of(d * 16, 32), 16), :]
            second = y_ref[pl.ds(pl.multiple_of(d * 16, 32) + 16, 16), :]
            both = jnp.concatenate(
                [
                    jnp.where(low, first, pltpu.roll(second, HALF, 1)),
                    jnp.where(low, pltpu.roll(first, HALF, 1), second),
                ],
                axis=0,
            )
            m = jnp.where(low1, mask_ref[pl.ds(d, 1), :], mask_ref[pl.ds(d + 1, 1), :])
            plain.append(both)
            masked.append(both * m)
        a_hi, a_lo = split(jnp.concatenate(masked, axis=1))
        b_hi, b_lo = split(jnp.concatenate(plain, axis=1))
        nt = (((1,), (1,)), ((), ()))
        for a, b in ((a_hi, b_hi), (a_hi, b_lo), (a_lo, b_hi)):
            total = total + lax.dot_general(a, b, nt, preferred_element_type=jnp.float32)
        return total

    total = lax.fori_loop(0, blocks // (2 * pairs), body, jnp.zeros((32, 32), jnp.float32))
    out_ref[:32, :] = total
    out_ref[32:, :] = jnp.full((8, 32), counts_ref[0].astype(jnp.float32))


def unpack_kernel(in_ref, out_ref):
    low = lax.broadcasted_iota(jnp.int32, (16, LANES), 1) < HALF
    for t in range(out_ref.shape[1] // LANES):
        even = in_ref[32 * t : 32 * t + 16, :]
        odd = in_ref[32 * t + 16 : 32 * t + 32, :]
        out_ref[:16, LANES * t : LANES * (t + 1)] = jnp.where(low, even, pltpu.roll(odd, HALF, 1))
        out_ref[16:, LANES * t : LANES * (t + 1)] = jnp.where(low, pltpu.roll(even, HALF, 1), odd)


def everywhere_sum(x):
    for axis, bits in (("narrow", (1, 2, 4, 8)), ("wide", (1, 2, 4, 8))):
        for bit in bits:
            x = x + lax.ppermute(x, axis, [(i, i ^ bit) for i in range(lax.axis_size(axis))])
    return x


SMEM = pl.BlockSpec(memory_space=pltpu.SMEM)


def shards(panel, signs, sample_rows, counts):
    width, length = panel.shape
    slab = LOW * HIGH
    slabs = length // slab
    blocks = lax.axis_size("wide") * lax.axis_size("narrow")
    samples = sample_rows.shape[0]
    scale = 1.0 / math.sqrt(slab * blocks)
    f32 = jnp.float32

    sent = pl.pallas_call(
        lambda *refs: local_kernel(scale, *refs),
        grid=(slabs,),
        in_specs=[
            SMEM,
            pl.BlockSpec((width, slab), lambda s: (0, s)),
            pl.BlockSpec((1, slab), lambda s: (0, s)),
            pl.BlockSpec((1, samples), lambda s: (0, 0)),
        ],
        out_specs=pl.BlockSpec((34 * LOW, LANES), lambda s: (s, 0)),
        out_shape=jax.ShapeDtypeStruct((34 * LOW * slabs, LANES), f32),
        scratch_shapes=[
            pltpu.VMEM((HIGH, 2 * HIGH), jnp.bfloat16),
            pltpu.VMEM((HIGH, LANES), f32),
            pltpu.VMEM((HIGH, LANES), f32),
            pltpu.VMEM((width * LOW, LANES), f32),
        ],
        compiler_params=pltpu.CompilerParams(vmem_limit_bytes=32 * 2**20),
    )(counts, panel, signs.reshape(1, length), sample_rows.reshape(1, samples))

    got = lax.all_to_all(sent.reshape(17 * blocks, 1, LANES), AXES, 0, 0, tiled=True).reshape(17 * blocks, LANES)

    mixed, mask = pl.pallas_call(
        lambda *refs: across_kernel(blocks, *refs),
        out_shape=(jax.ShapeDtypeStruct((16 * blocks, LANES), f32), jax.ShapeDtypeStruct((blocks, LANES), f32)),
        compiler_params=pltpu.CompilerParams(vmem_limit_bytes=32 * 2**20),
    )(got)

    back = lax.all_to_all(mixed, AXES, 0, 0, tiled=True)

    part = pl.pallas_call(
        gram_kernel,
        in_specs=[SMEM, pl.BlockSpec(memory_space=pltpu.VMEM), pl.BlockSpec(memory_space=pltpu.VMEM)],
        out_shape=jax.ShapeDtypeStruct((40, 32), f32),
        compiler_params=pltpu.CompilerParams(vmem_limit_bytes=32 * 2**20),
    )(counts, mixed, mask)
    total = everywhere_sum(part)
    gram = total[:32] / total[32, 0]

    out = pl.pallas_call(
        unpack_kernel,
        grid=(slabs,),
        in_specs=[pl.BlockSpec((32 * LOW, LANES), lambda s: (s, 0))],
        out_specs=pl.BlockSpec((width, slab), lambda s: (0, s)),
        out_shape=jax.ShapeDtypeStruct((width, length), f32),
        compiler_params=pltpu.CompilerParams(vmem_limit_bytes=32 * 2**20),
    )(back)
    return out, gram


def solution(mesh):
    placed = (P(None, AXES), P(AXES), P(AXES), P(AXES))
    return jax.shard_map(
        shards,
        mesh=mesh,
        in_specs=placed,
        out_specs=(P(None, AXES), P()),
        check_vma=False,
    )
```

time: 553 us -> 151 us (0.27)
  waiting for transfers between devices: 405 us -> 35.8 us
  other arithmetic: 26.4 us -> 1.27 us
  Pallas kernels: 0 us -> 10.5 us
  local copies, waits for them, and re-layouts: 15.4 us -> 6.62 us
    ppermute x8, waiting for transfers between devices: 405 us -> 35.8 us  [everywhere_sum(): lax.ppermute(x, axis, [(i, i ^ bit) for i in range(lax.axis_size(axis))])]
    psum x1 -> x0, blocking collectives: 76.1 us -> none  [shards(): lax.psum((outer, jnp.sum(counts.astype(jnp.float32))), ('wide', 'narrow'))]
    all_to_all x0 -> x1, blocking collectives: none -> 71.6 us  [shards(): lax.all_to_all(sent.reshape(17 * blocks, 1, LANES), AXES, 0, 0, tiled=True)]
    add x7 -> x8, other arithmetic: 19.4 us -> 0.03 us  [everywhere_sum(): x + lax.ppermute(x, axis, [(i, i ^ bit) for i in range(lax.axis_size(axis...]
    pallas_call x0 -> x4, Pallas kernels: none -> 10.5 us  [the longest x1 4.5 us: shards(): pl.pallas_call(gram_kernel, in_specs=[SMEM, pl.BlockSpec(memory_space=plt...]
    all_to_all x0 -> x1, starting transfers between devices: none -> 6.45 us  [shards(): back = lax.all_to_all(mixed, AXES, 0, 0, tiled=True)]
    mul x1 -> x0, local copies, waits for them, and re-layouts: 6.26 us -> none  [shards(): mixed = work * (1.0 / math.sqrt(LOW * HIGH * blocks))]
    gather x1 -> x0, local copies, waits for them, and re-layouts: 6.19 us -> none  [shards(): picked = mixed[:, sample_rows] * live[None, :]]
  transfers between devices with their start and end apart: 8 -> 9, of which waited for: 8 -> 8; matrix products, arithmetic and copies ran while one was open for 0% -> 1% of each run, Pallas kernels for 0% -> 3%
where the time goes in v1:
time: 151 us; the launch traced here: 150 us
  blocking collectives  71.6 us (47%)
  waiting for transfers between devices  35.8 us (24%)
  starting transfers between devices  23.4 us (15%)
  Pallas kernels  10.5 us (7%)
  local copies, waits for them, and re-layouts  6.62 us (4%)
    all_to_all x1, blocking collectives, shards(): lax.all_to_all(sent.reshape(17 * blocks, 1, LANES), AXES, 0, 0, tiled=True)  71.6 us
    ppermute x8, waiting for transfers between devices, everywhere_sum(): lax.ppermute(x, axis, [(i, i ^ bit) for i in range(lax.axis_size(axis))])  35.8 us
    ppermute x8, starting transfers between devices, everywhere_sum(): lax.ppermute(x, axis, [(i, i ^ bit) for i in range(lax.axis_size(axis))])  16.9 us
    all_to_all x1, starting transfers between devices, shards(): back = lax.all_to_all(mixed, AXES, 0, 0, tiled=True)  6.45 us
    unnamed x10, local copies, waits for them, and re-layouts  6.04 us
    pallas_call x1, Pallas kernels, shards(): pl.pallas_call(gram_kernel, in_specs=[SMEM, pl.BlockSpec(memory_space=plt...  4.5 us
  transfers between devices with their start and end apart: 9, of which 8 were waited for; matrix products, arithmetic and copies ran while one was open for 1% of the time, Pallas kernels for 3%

profile of v1, /device:TPU:2, one launch (start us, length us, event | category | flops | bytes accessed | tf_op | source)
XLA Modules:
  0.0 150.5 jit_solution(12629936001890599154)
XLA Ops:
  1.3 0.0 copy-start.2
  1.3 1.6 %copy-done.2 = f32[32,16384]{1,0:T(8,128)S(1)} copy-done((f32[32,16384]{1,0:T(8,128)S(1)}, f32[32,16384]{1,0:T(8,128)}, u32[]{:S(2)}) %copy-start.2) | copy-done | bytes 2097176
  2.9 0.0 copy-start.3
  2.9 0.8 copy-done.3
  3.7 0.0 copy-start.4
  3.7 0.7 copy-done.4
  4.4 2.6 %shard_map.59 = f32[4352,128]{1,0:T(8,128)S(1)} custom-call(s32[1]{0:T(128)S(6)} %copy.7.refs_0_.counts_ref, f32[32,16384]{1,0:T(8,128)S(1)} %copy-done.2, s32[1,16384]{1,0:T(1,128)S(1)} %bitcast.13, s32[1,1024]{1,0:T(1,128)S(1)} %bitcast.14), custom_call_target="tpu_custom_call" | custom-call | tf_op jit(solution)/shard_map/pallas_call | solution.py:175
  7.0 71.6 %all_to_all.16 = f32[4352,1,128]{2,1,0:T(1,128)S(1)} all-to-all(f32[4352,1,128]{2,1,0:T(1,128)S(1)} %bitcast.10), channel_id=1, replica_groups=mesh['wide'=16,'narrow'=16] {'wide','narrow'}, dimensions={0} | all-to-all | bytes 4456448 | tf_op jit(solution)/shard_map/all_to_all | solution.py:195
  78.6 1.1 shard_map.60
  79.8 0.0 copy-start
  79.8 1.3 copy-done
  81.1 6.5 %all-to-all-start.1 = ((f32[256,16,128]{2,1,0:T(8,128)}), f32[256,16,128]{2,1,0:T(8,128)S(1)}, u32[]{:S(2)}, u32[]{:S(2)}) async-start(f32[256,16,128]{2,1,0:T(8,128)} %bitcast.12), calls=%async_computation.1 | async-start | bytes 4194304 | tf_op jit(solution)/shard_map/all_to_all | solution.py:203
  87.5 0.0 copy-start.1
  87.5 1.6 %copy-done.1 = f32[4096,128]{1,0:T(8,128)S(1)} copy-done((f32[4096,128]{1,0:T(8,128)S(1)}, f32[4096,128]{1,0:T(8,128)}, u32[]{:S(2)}) %copy-start.1) | copy-done | bytes 2097176
  89.2 4.5 %shard_map.62 = f32[40,32]{1,0:T(8,128)S(1)} custom-call(s32[1]{0:T(128)S(6)} %copy.7.refs_0_.counts_ref, f32[4096,128]{1,0:T(8,128)S(1)} %copy-done.1, f32[256,128]{1,0:T(8,128)S(1)} %get-tuple-element.5.mask_ref), custom_call_target="tpu_custom_call" | custom-call | tf_op jit(solution)/shard_map/pallas_call | solution.py:205
  93.7 0.2 collective-permute-start
  93.8 1.0 collective-permute-done
  94.9 1.6 %collective-permute-start.1 = (f32[40,32]{1,0:T(8,128)S(1)}, f32[40,32]{1,0:T(8,128)S(1)}, u32[]{:S(2)}, u32[]{:S(2)}) collective-permute-start(f32[40,32]{1,0:T(8,128)S(1)} %add.24), channel_id=1, source_target_pairs={{0,2},{1,3},{2,0},{3,1},{4,6},{5,7},{6,4},{7,5},{8,10},{9,11},{10,... | collective-permute-start | bytes 15368 | tf_op jit(solution)/shard_map/ppermute | solution.py:159
  96.4 2.3 %collective-permute-done.1 = f32[40,32]{1,0:T(8,128)S(1)} collective-permute-done((f32[40,32]{1,0:T(8,128)S(1)}, f32[40,32]{1,0:T(8,128)S(1)}, u32[]{:S(2)}, u32[]{:S(2)}) %collective-permute-start.1) | collective-permute-done | bytes 5152 | tf_op jit(solution)/shard_map/ppermute | solution.py:159
  98.7 3.2 %collective-permute-start.2 = (f32[40,32]{1,0:T(8,128)S(1)}, f32[40,32]{1,0:T(8,128)S(1)}, u32[]{:S(2)}, u32[]{:S(2)}) collective-permute-start(f32[40,32]{1,0:T(8,128)S(1)} %add.25), channel_id=1, source_target_pairs={{0,4},{1,5},{2,6},{3,7},{4,0},{5,1},{6,2},{7,3},{8,12},{9,13},{10,... | collective-permute-start | bytes 15368 | tf_op jit(solution)/shard_map/ppermute | solution.py:159
  102.0 2.3 %collective-permute-done.2 = f32[40,32]{1,0:T(8,128)S(1)} collective-permute-done((f32[40,32]{1,0:T(8,128)S(1)}, f32[40,32]{1,0:T(8,128)S(1)}, u32[]{:S(2)}, u32[]{:S(2)}) %collective-permute-start.2) | collective-permute-done | bytes 5152 | tf_op jit(solution)/shard_map/ppermute | solution.py:159
  104.2 1.9 %collective-permute-start.3 = (f32[40,32]{1,0:T(8,128)S(1)}, f32[40,32]{1,0:T(8,128)S(1)}, u32[]{:S(2)}, u32[]{:S(2)}) collective-permute-start(f32[40,32]{1,0:T(8,128)S(1)} %add.26), channel_id=1, source_target_pairs={{0,8},{1,9},{2,10},{3,11},{4,12},{5,13},{6,14},{7,15},{8,0},{9,1},... | collective-permute-start | bytes 15368 | tf_op jit(solution)/shard_map/ppermute | solution.py:159
  106.1 3.8 %collective-permute-done.3 = f32[40,32]{1,0:T(8,128)S(1)} collective-permute-done((f32[40,32]{1,0:T(8,128)S(1)}, f32[40,32]{1,0:T(8,128)S(1)}, u32[]{:S(2)}, u32[]{:S(2)}) %collective-permute-start.3) | collective-permute-done | bytes 5152 | tf_op jit(solution)/shard_map/ppermute | solution.py:159
  109.9 2.4 %collective-permute-start.4 = (f32[40,32]{1,0:T(8,128)S(1)}, f32[40,32]{1,0:T(8,128)S(1)}, u32[]{:S(2)}, u32[]{:S(2)}) collective-permute-start(f32[40,32]{1,0:T(8,128)S(1)} %add.27), channel_id=1, source_target_pairs={{0,16},{16,0},{32,48},{48,32},{64,80},{80,64},{96,112},{112,96},{1... | collective-permute-start | bytes 15368 | tf_op jit(solution)/shard_map/ppermute | solution.py:159
  112.3 2.0 %collective-permute-done.4 = f32[40,32]{1,0:T(8,128)S(1)} collective-permute-done((f32[40,32]{1,0:T(8,128)S(1)}, f32[40,32]{1,0:T(8,128)S(1)}, u32[]{:S(2)}, u32[]{:S(2)}) %collective-permute-start.4) | collective-permute-done | bytes 5152 | tf_op jit(solution)/shard_map/ppermute | solution.py:159
  114.3 1.4 collective-permute-start.5
  115.7 18.3 %collective-permute-done.5 = f32[40,32]{1,0:T(8,128)S(1)} collective-permute-done((f32[40,32]{1,0:T(8,128)S(1)}, f32[40,32]{1,0:T(8,128)S(1)}, u32[]{:S(2)}, u32[]{:S(2)}) %collective-permute-start.5) | collective-permute-done | bytes 5152 | tf_op jit(solution)/shard_map/ppermute | solution.py:159
  134.0 0.9 collective-permute-start.6
  134.8 3.9 %collective-permute-done.6 = f32[40,32]{1,0:T(8,128)S(1)} collective-permute-done((f32[40,32]{1,0:T(8,128)S(1)}, f32[40,32]{1,0:T(8,128)S(1)}, u32[]{:S(2)}, u32[]{:S(2)}) %collective-permute-start.6) | collective-permute-done | bytes 5152 | tf_op jit(solution)/shard_map/ppermute | solution.py:159
  138.7 5.5 %collective-permute-start.7 = (f32[40,32]{1,0:T(8,128)S(1)}, f32[40,32]{1,0:T(8,128)S(1)}, u32[]{:S(2)}, u32[]{:S(2)}) collective-permute-start(f32[40,32]{1,0:T(8,128)S(1)} %add.30), channel_id=1, source_target_pairs={{0,128},{16,144},{32,160},{48,176},{64,192},{80,208},{96,224},{112... | collective-permute-start | bytes 15368 | tf_op jit(solution)/shard_map/ppermute | solution.py:159
  144.2 2.2 %collective-permute-done.7 = f32[40,32]{1,0:T(8,128)S(1)} collective-permute-done((f32[40,32]{1,0:T(8,128)S(1)}, f32[40,32]{1,0:T(8,128)S(1)}, u32[]{:S(2)}, u32[]{:S(2)}) %collective-permute-start.7) | collective-permute-done | bytes 5152 | tf_op jit(solution)/shard_map/ppermute | solution.py:159
  146.4 0.6 slice.9
  147.0 1.2 slice_divide_fusion
  148.3 0.0 all-to-all-done.1
  148.3 2.2 %shard_map.61 = f32[32,16384]{1,0:T(8,128)} custom-call(f32[4096,128]{1,0:T(8,128)S(1)} %bitcast.11), custom_call_target="tpu_custom_call" | custom-call | tf_op jit(solution)/shard_map/pallas_call | solution.py:214
  (8 shorter events, 0.0 us)
Async XLA Ops:
  1.3 1.6 %copy-start.2 = (f32[32,16384]{1,0:T(8,128)S(1)}, f32[32,16384]{1,0:T(8,128)}, u32[]{:S(2)}) copy-start(f32[32,16384]{1,0:T(8,128)} %refs_1_.1) | copy-start | bytes 6291460
  2.9 0.8 copy-start.3
  3.7 0.7 copy-start.4
  79.8 1.3 copy-start
  81.1 67.2 %all-to-all-start.1 = ((f32[256,16,128]{2,1,0:T(8,128)}), f32[256,16,128]{2,1,0:T(8,128)S(1)}, u32[]{:S(2)}, u32[]{:S(2)}) async-start(f32[256,16,128]{2,1,0:T(8,128)} %bitcast.12), calls=%async_computation.1 | async-start | bytes 4194304 | tf_op jit(solution)/shard_map/all_to_all | solution.py:203
  87.5 1.6 %copy-start.1 = (f32[4096,128]{1,0:T(8,128)S(1)}, f32[4096,128]{1,0:T(8,128)}, u32[]{:S(2)}) copy-start(f32[4096,128]{1,0:T(8,128)} %copy-done) | copy-start | bytes 6291460
  93.7 1.2 collective-permute-start
  94.9 3.8 %collective-permute-start.1 = (f32[40,32]{1,0:T(8,128)S(1)}, f32[40,32]{1,0:T(8,128)S(1)}, u32[]{:S(2)}, u32[]{:S(2)}) collective-permute-start(f32[40,32]{1,0:T(8,128)S(1)} %add.24), channel_id=1, source_target_pairs={{0,2},{1,3},{2,0},{3,1},{4,6},{5,7},{6,4},{7,5},{8,10},{9,11},{10,... | collective-permute-start | bytes 15368 | tf_op jit(solution)/shard_map/ppermute | solution.py:159
  98.7 5.5 %collective-permute-start.2 = (f32[40,32]{1,0:T(8,128)S(1)}, f32[40,32]{1,0:T(8,128)S(1)}, u32[]{:S(2)}, u32[]{:S(2)}) collective-permute-start(f32[40,32]{1,0:T(8,128)S(1)} %add.25), channel_id=1, source_target_pairs={{0,4},{1,5},{2,6},{3,7},{4,0},{5,1},{6,2},{7,3},{8,12},{9,13},{10,... | collective-permute-start | bytes 15368 | tf_op jit(solution)/shard_map/ppermute | solution.py:159
  104.2 5.6 %collective-permute-start.3 = (f32[40,32]{1,0:T(8,128)S(1)}, f32[40,32]{1,0:T(8,128)S(1)}, u32[]{:S(2)}, u32[]{:S(2)}) collective-permute-start(f32[40,32]{1,0:T(8,128)S(1)} %add.26), channel_id=1, source_target_pairs={{0,8},{1,9},{2,10},{3,11},{4,12},{5,13},{6,14},{7,15},{8,0},{9,1},... | collective-permute-start | bytes 15368 | tf_op jit(solution)/shard_map/ppermute | solution.py:159
  109.9 4.4 %collective-permute-start.4 = (f32[40,32]{1,0:T(8,128)S(1)}, f32[40,32]{1,0:T(8,128)S(1)}, u32[]{:S(2)}, u32[]{:S(2)}) collective-permute-start(f32[40,32]{1,0:T(8,128)S(1)} %add.27), channel_id=1, source_target_pairs={{0,16},{16,0},{32,48},{48,32},{64,80},{80,64},{96,112},{112,96},{1... | collective-permute-start | bytes 15368 | tf_op jit(solution)/shard_map/ppermute | solution.py:159
  114.3 19.7 %collective-permute-start.5 = (f32[40,32]{1,0:T(8,128)S(1)}, f32[40,32]{1,0:T(8,128)S(1)}, u32[]{:S(2)}, u32[]{:S(2)}) collective-permute-start(f32[40,32]{1,0:T(8,128)S(1)} %add.28), channel_id=1, source_target_pairs={{0,32},{16,48},{32,0},{48,16},{64,96},{80,112},{96,64},{112,80},{1... | collective-permute-start | bytes 15368 | tf_op jit(solution)/shard_map/ppermute | solution.py:159
  134.0 4.8 %collective-permute-start.6 = (f32[40,32]{1,0:T(8,128)S(1)}, f32[40,32]{1,0:T(8,128)S(1)}, u32[]{:S(2)}, u32[]{:S(2)}) collective-permute-start(f32[40,32]{1,0:T(8,128)S(1)} %add.29), channel_id=1, source_target_pairs={{0,64},{16,80},{32,96},{48,112},{64,0},{80,16},{96,32},{112,48},{1... | collective-permute-start | bytes 15368 | tf_op jit(solution)/shard_map/ppermute | solution.py:159
  138.7 7.7 %collective-permute-start.7 = (f32[40,32]{1,0:T(8,128)S(1)}, f32[40,32]{1,0:T(8,128)S(1)}, u32[]{:S(2)}, u32[]{:S(2)}) collective-permute-start(f32[40,32]{1,0:T(8,128)S(1)} %add.30), channel_id=1, source_target_pairs={{0,128},{16,144},{32,160},{48,176},{64,192},{80,208},{96,224},{112... | collective-permute-start | bytes 15368 | tf_op jit(solution)/shard_map/ppermute | solution.py:159

commit v2 on v1

v2 whole, which is shorter than its diff:
```python
import math

import jax
import jax.numpy as jnp
from jax import lax
from jax.experimental import pallas as pl
from jax.experimental.pallas import tpu as pltpu
from jax.sharding import PartitionSpec as P

LOW = 32
HIGH = 128
LANES = 128
HALF = 64
AXES = ("wide", "narrow")


def signs_of(i, j, n):
    v = jnp.bitwise_and(i, j)
    shift = 1
    while shift < n.bit_length():
        v = jnp.bitwise_xor(v, jnp.right_shift(v, shift))
        shift *= 2
    return (1 - 2 * jnp.bitwise_and(v, 1)).astype(jnp.float32)


def split(x):
    hi = x.astype(jnp.bfloat16)
    lo = (x - hi.astype(jnp.float32)).astype(jnp.bfloat16)
    return hi, lo


def dot(a, b):
    return jnp.dot(a, b, preferred_element_type=jnp.float32)


def butterfly(vs):
    step = 1
    while step < len(vs):
        out = list(vs)
        for i in range(len(vs)):
            if not i & step:
                out[i] = vs[i] + vs[i | step]
                out[i | step] = vs[i] - vs[i | step]
        vs = out
        step *= 2
    return vs


def local_kernel(
    scale, counts_ref, panel_hbm, signs_hbm, rows_hbm, out_hbm,
    panel_ref, signs_ref, rows_ref, table_ref, even_ref, odd_ref, x_ref, out_ref, sems, out_sems,
):
    slabs, width, slab = panel_ref.shape
    small = [
        pltpu.make_async_copy(rows_hbm, rows_ref, sems.at[slabs]),
        pltpu.make_async_copy(signs_hbm, signs_ref, sems.at[slabs + 1]),
    ]
    big = [
        pltpu.make_async_copy(panel_hbm.at[:, slab * s : slab * (s + 1)], panel_ref.at[s], sems.at[s])
        for s in range(slabs)
    ]
    for copy in small + big:
        copy.start()
    i = lax.broadcasted_iota(jnp.int32, (2 * HIGH, 2 * HIGH), 0)
    j = lax.broadcasted_iota(jnp.int32, (2 * HIGH, 2 * HIGH), 1)
    i = jnp.bitwise_and(i, HIGH - 1)
    j = jnp.where(j < HIGH, j, jnp.bitwise_and(j + HALF, HIGH - 1))
    table_ref[...] = (signs_of(i, j, HIGH) * scale).astype(jnp.bfloat16)
    small[0].wait()
    rows = rows_ref[...]
    samples = rows.shape[1]
    slot = lax.broadcasted_iota(jnp.int32, (1, samples), 1)
    rows = jnp.where(slot < counts_ref[0], rows, -1)
    at = lax.broadcasted_iota(jnp.int32, (HIGH, samples), 0)
    tile = (jnp.right_shift(rows, 7) == at).astype(jnp.float32).astype(jnp.bfloat16)
    inner = (jnp.bitwise_and(rows, HIGH - 1) == at).astype(jnp.float32).astype(jnp.bfloat16)
    mask = lax.dot_general(tile, inner, (((1,), (1,)), ((), ())), preferred_element_type=jnp.float32)
    other = pltpu.roll(mask, HALF, 1)
    low = lax.broadcasted_iota(jnp.int32, (HIGH, LANES), 1) < HALF
    even_ref[...] = jnp.where(low, mask, other)
    odd_ref[...] = jnp.where(low, other, mask)
    small[1].wait()
    table = table_ref[...]
    low = lax.broadcasted_iota(jnp.int32, (16, LANES), 1) < HALF
    per = 8
    outs = []
    for s in range(slabs):
        big[s].wait()
        for g in range(width // 8):
            vs = [
                panel_ref[s, 8 * g : 8 * g + 8, LANES * a : LANES * (a + 1)]
                * signs_ref[:, slab * s + LANES * a : slab * s + LANES * (a + 1)].astype(jnp.float32)
                for a in range(LOW)
            ]
            for a, v in enumerate(butterfly(vs)):
                x_ref[s % 2, width * a + 8 * g : width * a + 8 * g + 8, :] = v
        for c in range(LOW // per):
            hi, lo = split(x_ref[s % 2, width * per * c : width * per * (c + 1), :])
            z = dot(jnp.concatenate([hi, lo], axis=1), table)
            for k in range(per):
                t = LOW * s + per * c + k
                y = z[width * k : width * (k + 1), :LANES]
                r = z[width * k : width * (k + 1), LANES:]
                row = 34 * t
                out_ref[row : row + 16, :] = jnp.where(low, y[:16], r[16:])
                out_ref[row + 16 : row + 17, :] = even_ref[t : t + 1, :]
                out_ref[row + 17 : row + 33, :] = jnp.where(low, r[:16], y[16:])
                out_ref[row + 33 : row + 34, :] = odd_ref[t : t + 1, :]
        rows = pl.ds(34 * LOW * s, 34 * LOW)
        outs.append(pltpu.make_async_copy(out_ref.at[rows, :], out_hbm.at[rows, :], out_sems.at[s]))
        outs[-1].start()
    for copy in outs:
        copy.wait()


def across_kernel(blocks, in_ref, out_hbm, mask_hbm, keep_ref, mask_ref, sems):
    i = lax.broadcasted_iota(jnp.int32, (blocks, blocks), 0)
    j = lax.broadcasted_iota(jnp.int32, (blocks, blocks), 1)
    table = signs_of(i, j, blocks).astype(jnp.bfloat16)
    tiles = keep_ref.reshape(blocks, 16, LANES)
    mask_ref[...] = in_ref[pl.ds(16, blocks, stride=17), :]
    copies = [pltpu.make_async_copy(mask_ref, mask_hbm, sems.at[2])]
    copies[0].start()
    for part in range(2):
        for k in range(8 * part, 8 * part + 8, 2):
            x = jnp.concatenate(
                [in_ref[pl.ds(k, blocks, stride=17), :], in_ref[pl.ds(k + 1, blocks, stride=17), :]], axis=1
            )
            hi, lo = split(x)
            y = dot(table, hi) + dot(table, lo)
            keep_ref[pl.ds(k, blocks, stride=16), :] = y[:, :LANES]
            keep_ref[pl.ds(k + 1, blocks, stride=16), :] = y[:, LANES:]
        rows = pl.ds(8 * part, 8)
        copies.append(pltpu.make_async_copy(tiles.at[:, rows, :], out_hbm.at[:, rows, :], sems.at[part]))
        copies[-1].start()
    for copy in copies:
        copy.wait()


def gram_kernel(counts_ref, y_ref, mask_ref, out_ref):
    blocks = mask_ref.shape[0]
    low = lax.broadcasted_iota(jnp.int32, (16, LANES), 1) < HALF
    low1 = lax.broadcasted_iota(jnp.int32, (1, LANES), 1) < HALF
    pairs = 8

    @pl.when(pl.program_id(0) == 0)
    def _():
        out_ref[:32, :] = jnp.zeros((32, 32), jnp.float32)
        out_ref[32:, :] = jnp.full((8, 32), counts_ref[0].astype(jnp.float32))

    total = out_ref[:32, :]
    for c in range(blocks // (2 * pairs)):
        plain, masked = [], []
        for k in range(pairs):
            d = 2 * pairs * c + 2 * k
            first = y_ref[d]
            second = y_ref[d + 1]
            both = jnp.concatenate(
                [
                    jnp.where(low, first, pltpu.roll(second, HALF, 1)),
                    jnp.where(low, pltpu.roll(first, HALF, 1), second),
                ],
                axis=0,
            )
            m = jnp.where(low1, mask_ref[d : d + 1, :], mask_ref[d + 1 : d + 2, :])
            plain.append(both)
            masked.append(both * m)
        a_hi, a_lo = split(jnp.concatenate(masked, axis=1))
        b_hi, b_lo = split(jnp.concatenate(plain, axis=1))
        nt = (((1,), (1,)), ((), ()))
        for a, b in ((a_hi, b_hi), (a_hi, b_lo), (a_lo, b_hi)):
            total = total + lax.dot_general(a, b, nt, preferred_element_type=jnp.float32)
    out_ref[:32, :] = total


def unpack_kernel(in_ref, out_ref):
    low = lax.broadcasted_iota(jnp.int32, (16, LANES), 1) < HALF
    for t in range(out_ref.shape[1] // LANES):
        even = in_ref[32 * t : 32 * t + 16, :]
        odd = in_ref[32 * t + 16 : 32 * t + 32, :]
        out_ref[:16, LANES * t : LANES * (t + 1)] = jnp.where(low, even, pltpu.roll(odd, HALF, 1))
        out_ref[16:, LANES * t : LANES * (t + 1)] = jnp.where(low, pltpu.roll(even, HALF, 1), odd)


def send(x, move):
    wide, narrow = lax.axis_size("wide"), lax.axis_size("narrow")
    pairs = []
    for w in range(wide):
        for n in range(narrow):
            to = move(w, n)
            if to is not None:
                pairs.append((w * narrow + n, to[0] * narrow + to[1]))
    return lax.ppermute(x, AXES, pairs)


def half_sum(x):
    x = x + send(x, lambda w, n: (w, n ^ 1))
    x = x + send(x, lambda w, n: (w, n ^ 2)) + send(x, lambda w, n: (w, n ^ 4)) + send(x, lambda w, n: (w, n ^ 6))
    x = x + send(x, lambda w, n: (w ^ 1, n)) + send(x, lambda w, n: (w, n ^ 8)) + send(x, lambda w, n: (w ^ 1, n ^ 8))
    far = lax.axis_size("wide") // 2
    own = jnp.where(jnp.bitwise_and(lax.axis_index("narrow"), 1) == 0, x, 0.0)
    half = far // 2
    for step in range(half):
        own = own + send(
            x,
            lambda w, n, step=step: (w ^ (2 * (step + half * (n & 1))), n) if step + (n & 1) else None,
        )
    return own


SMEM = pl.BlockSpec(memory_space=pltpu.SMEM)
VMEM = pl.BlockSpec(memory_space=pltpu.VMEM)
HBM = pl.BlockSpec(memory_space=pltpu.HBM)


def shards(panel, signs, sample_rows, counts):
    width, length = panel.shape
    slab = LOW * HIGH
    slabs = length // slab
    blocks = lax.axis_size("wide") * lax.axis_size("narrow")
    samples = sample_rows.shape[0]
    scale = 1.0 / math.sqrt(slab * blocks)
    f32 = jnp.float32

    sent = pl.pallas_call(
        lambda *refs: local_kernel(scale, *refs),
        in_specs=[SMEM, HBM, HBM, HBM],
        out_specs=HBM,
        out_shape=jax.ShapeDtypeStruct((17 * blocks, LANES), f32),
        scratch_shapes=[
            pltpu.VMEM((slabs, width, slab), f32),
            pltpu.VMEM((1, length), jnp.int32),
            pltpu.VMEM((1, samples), jnp.int32),
            pltpu.VMEM((2 * HIGH, 2 * HIGH), jnp.bfloat16),
            pltpu.VMEM((HIGH, LANES), f32),
            pltpu.VMEM((HIGH, LANES), f32),
            pltpu.VMEM((2, width * LOW, LANES), f32),
            pltpu.VMEM((17 * blocks, LANES), f32),
            pltpu.SemaphoreType.DMA((slabs + 2,)),
            pltpu.SemaphoreType.DMA((slabs,)),
        ],
        compiler_params=pltpu.CompilerParams(vmem_limit_bytes=60 * 2**20),
    )(counts, panel, signs.reshape(1, length), sample_rows.reshape(1, samples))

    got = lax.all_to_all(sent.reshape(17 * blocks, 1, LANES), AXES, 0, 0, tiled=True).reshape(17 * blocks, LANES)

    mixed, mask = pl.pallas_call(
        lambda *refs: across_kernel(blocks, *refs),
        in_specs=[VMEM],
        out_specs=(HBM, HBM),
        out_shape=(pltpu.HBM((blocks, 16, LANES), f32), pltpu.HBM((blocks, LANES), f32)),
        scratch_shapes=[
            pltpu.VMEM((16 * blocks, LANES), f32),
            pltpu.VMEM((blocks, LANES), f32),
            pltpu.SemaphoreType.DMA((3,)),
        ],
        compiler_params=pltpu.CompilerParams(vmem_limit_bytes=32 * 2**20),
    )(got)

    back = lax.all_to_all(mixed, AXES, 0, 0, tiled=True).reshape(16 * blocks, LANES)

    steps = 8
    part = pl.pallas_call(
        gram_kernel,
        grid=(steps,),
        in_specs=[
            SMEM,
            pl.BlockSpec((blocks // steps, 16, LANES), lambda s: (s, 0, 0)),
            pl.BlockSpec((blocks // steps, LANES), lambda s: (s, 0)),
        ],
        out_specs=pl.BlockSpec((40, 32), lambda s: (0, 0)),
        out_shape=jax.ShapeDtypeStruct((40, 32), f32),
        compiler_params=pltpu.CompilerParams(vmem_limit_bytes=60 * 2**20),
    )(counts, mixed, mask)
    total, back = lax.optimization_barrier((half_sum(part), back))
    total = total + send(total, lambda w, n: (w, n ^ 1))
    gram = total[:32] / total[32:33]

    out = pl.pallas_call(
        unpack_kernel,
        grid=(slabs,),
        in_specs=[pl.BlockSpec((32 * LOW, LANES), lambda s: (s, 0))],
        out_specs=pl.BlockSpec((width, slab), lambda s: (0, s)),
        out_shape=jax.ShapeDtypeStruct((width, length), f32),
        compiler_params=pltpu.CompilerParams(vmem_limit_bytes=32 * 2**20),
    )(back)
    return out, gram


def solution(mesh):
    placed = (P(None, AXES), P(AXES), P(AXES), P(AXES))
    return jax.shard_map(
        shards,
        mesh=mesh,
        in_specs=placed,
        out_specs=(P(None, AXES), P()),
        check_vma=False,
    )
```

time: 151 us -> 145 us (0.960); the launches traced: 150 us -> 143 us
  local copies, waits for them, and re-layouts: 6.62 us -> 0.01 us
  Pallas kernels: 10.5 us -> 14.2 us
  starting transfers between devices: 23.4 us -> 20.5 us
  waiting for transfers between devices: 35.8 us -> 33.4 us
    ppermute x8 -> x12, waiting for transfers between devices: 35.8 us -> 26.8 us  [send(): return lax.ppermute(x, AXES, pairs)]
    all_to_all x1, waiting for transfers between devices: 0.01 us -> 6.66 us  [shards(): lax.all_to_all(mixed, AXES, 0, 0, tiled=True).reshape(16 * blocks, LANES)]
    unnamed x10 -> x0, local copies, waits for them, and re-layouts: 6.04 us -> none
    pallas_call x3, Pallas kernels: 8.27 us -> 12 us  [the longest x1 6.22 us: shards(): pl.pallas_call(gram_kernel, grid=(steps,), in_specs=[SMEM, pl.BlockSpec((...]
    ppermute x8 -> x12, starting transfers between devices: 16.9 us -> 14 us  [send(): return lax.ppermute(x, AXES, pairs)]
  transfers between devices with their start and end apart: 9 -> 13, of which waited for: 8 -> 9; matrix products, arithmetic and copies ran while one was open for 1% -> 1% of each run, Pallas kernels for 3% -> 6%
where the time goes in v2:
time: 145 us; the launch traced here: 143 us
  blocking collectives  71.8 us (50%)
  waiting for transfers between devices  33.4 us (23%)
  starting transfers between devices  20.5 us (14%)
  Pallas kernels  14.2 us (10%)
    all_to_all x1, blocking collectives, shards(): lax.all_to_all(sent.reshape(17 * blocks, 1, LANES), AXES, 0, 0, tiled=True)  71.8 us
    ppermute x12, waiting for transfers between devices, send(): return lax.ppermute(x, AXES, pairs)  26.8 us
    ppermute x12, starting transfers between devices, send(): return lax.ppermute(x, AXES, pairs)  14 us
    all_to_all x1, waiting for transfers between devices, shards(): lax.all_to_all(mixed, AXES, 0, 0, tiled=True).reshape(16 * blocks, LANES)  6.66 us
    all_to_all x1, starting transfers between devices, shards(): lax.all_to_all(mixed, AXES, 0, 0, tiled=True).reshape(16 * blocks, LANES)  6.48 us
    pallas_call x1, Pallas kernels, shards(): pl.pallas_call(gram_kernel, grid=(steps,), in_specs=[SMEM, pl.BlockSpec((...  6.22 us
    pallas_call x1, Pallas kernels, shards(): pl.pallas_call(lambda *refs: local_kernel(scale, *refs), in_specs=[SMEM,...  3.59 us
  transfers between devices with their start and end apart: 13, of which 9 were waited for; matrix products, arithmetic and copies ran while one was open for 1% of the time, Pallas kernels for 6%

profile of v2, /device:TPU:2, one launch (start us, length us, event | category | flops | bytes accessed | tf_op | source)
XLA Modules:
  0.0 142.6 jit_solution(1584091915339457404)
XLA Ops:
  1.3 3.6 %shard_map.59 = f32[4352,128]{1,0:T(8,128)} custom-call(s32[1]{0:T(128)S(6)} %copy.7.refs_0_.counts_ref, f32[32,16384]{1,0:T(8,128)} %refs_1_.1, s32[1,16384]{1,0:T(1,128)} %bitcast.12, s32[1,1024]{1,0:T(1,128)} %bitcast.13), custom_call_target="tpu_custom_call" | custom-call | tf_op jit(solution)/shard_map/pallas_call | solution.py:225
  4.9 71.8 %all_to_all.10 = f32[4352,1,128]{2,1,0:T(1,128)S(1)} all-to-all(f32[4352,1,128]{2,1,0:T(1,128)} %bitcast.11), channel_id=1, replica_groups=mesh['wide'=16,'narrow'=16] {'wide','narrow'}, dimensions={0} | all-to-all | bytes 4456448 | tf_op jit(solution)/shard_map/all_to_all | solution.py:245
  76.7 2.2 %shard_map.60 = (f32[256,16,128]{2,1,0:T(8,128)}, f32[256,128]{1,0:T(8,128)}) custom-call(f32[4352,128]{1,0:T(8,128)S(1)} %bitcast.9), custom_call_target="tpu_custom_call" | custom-call | tf_op jit(solution)/shard_map/pallas_call | solution.py:247
  78.8 6.5 %all-to-all-start.1 = ((f32[256,16,128]{2,1,0:T(8,128)}), f32[256,16,128]{2,1,0:T(8,128)S(1)}, u32[]{:S(2)}, u32[]{:S(2)}) async-start(f32[256,16,128]{2,1,0:T(8,128)} %get-tuple-element.6.y_ref), calls=%async_computation.1 | async-start | bytes 4194304 | tf_op jit(solution)/shard_map/all_to_all | solution.py:260
  85.3 6.2 %shard_map.61 = f32[40,32]{1,0:T(8,128)} custom-call(s32[1]{0:T(128)S(6)} %copy.7.refs_0_.counts_ref, f32[256,16,128]{2,1,0:T(8,128)} %get-tuple-element.6.y_ref, f32[256,128]{1,0:T(8,128)} %get-tuple-element.7.mask_ref), custom_call_target="tpu_custom_call" | custom-call | tf_op jit(solution)/shard_map/pallas_call | solution.py:263
  91.5 0.1 collective-permute-start
  91.7 1.3 collective-permute-done
  92.9 0.7 add.36
  93.7 1.5 %collective-permute-start.1 = (f32[40,32]{1,0:T(8,128)S(1)}, f32[40,32]{1,0:T(8,128)S(1)}, u32[]{:S(2)}, u32[]{:S(2)}) collective-permute-start(f32[40,32]{1,0:T(8,128)S(1)} %add.36), channel_id=1, source_target_pairs={{0,2},{1,3},{2,0},{3,1},{4,6},{5,7},{6,4},{7,5},{8,10},{9,11},{10,... | collective-permute-start | bytes 15368 | tf_op jit(solution)/shard_map/ppermute | solution.py:193
  95.2 2.8 %collective-permute-start.2 = (f32[40,32]{1,0:T(8,128)S(1)}, f32[40,32]{1,0:T(8,128)S(1)}, u32[]{:S(2)}, u32[]{:S(2)}) collective-permute-start(f32[40,32]{1,0:T(8,128)S(1)} %add.36), channel_id=1, source_target_pairs={{0,4},{1,5},{2,6},{3,7},{4,0},{5,1},{6,2},{7,3},{8,12},{9,13},{10,... | collective-permute-start | bytes 15368 | tf_op jit(solution)/shard_map/ppermute | solution.py:193
  98.0 0.4 collective-permute-start.3
  98.4 0.0 collective-permute-done.1
  98.4 2.4 %collective-permute-done.2 = f32[40,32]{1,0:T(8,128)S(1)} collective-permute-done((f32[40,32]{1,0:T(8,128)S(1)}, f32[40,32]{1,0:T(8,128)S(1)}, u32[]{:S(2)}, u32[]{:S(2)}) %collective-permute-start.2) | collective-permute-done | bytes 5152 | tf_op jit(solution)/shard_map/ppermute | solution.py:193
  100.8 2.3 %collective-permute-done.3 = f32[40,32]{1,0:T(8,128)S(1)} collective-permute-done((f32[40,32]{1,0:T(8,128)S(1)}, f32[40,32]{1,0:T(8,128)S(1)}, u32[]{:S(2)}, u32[]{:S(2)}) %collective-permute-start.3) | collective-permute-done | bytes 5152 | tf_op jit(solution)/shard_map/ppermute | solution.py:193
  103.1 0.6 collective-permute-start.4
  103.7 2.6 %collective-permute-start.5 = (f32[40,32]{1,0:T(8,128)S(1)}, f32[40,32]{1,0:T(8,128)S(1)}, u32[]{:S(2)}, u32[]{:S(2)}) collective-permute-start(f32[40,32]{1,0:T(8,128)S(1)} %add_add_fusion.2), channel_id=1, source_target_pairs={{0,8},{1,9},{2,10},{3,11},{4,12},{5,13},{6,14},{7,15},{8,0},{9,1},... | collective-permute-start | bytes 15368 | tf_op jit(solution)/shard_map/ppermute | solution.py:193
  106.3 0.4 collective-permute-start.6
  106.6 0.4 collective-permute-done.4
  107.1 2.3 %collective-permute-done.5 = f32[40,32]{1,0:T(8,128)S(1)} collective-permute-done((f32[40,32]{1,0:T(8,128)S(1)}, f32[40,32]{1,0:T(8,128)S(1)}, u32[]{:S(2)}, u32[]{:S(2)}) %collective-permute-start.5) | collective-permute-done | bytes 5152 | tf_op jit(solution)/shard_map/ppermute | solution.py:193
  109.4 0.9 collective-permute-done.6
  110.2 4.2 %collective-permute-start.10 = (f32[40,32]{1,0:T(8,128)S(1)}, f32[40,32]{1,0:T(8,128)S(1)}, u32[]{:S(2)}, u32[]{:S(2)}) collective-permute-start(f32[40,32]{1,0:T(8,128)S(1)} %add_add_fusion.1), channel_id=1, source_target_pairs={{0,96},{1,225},{2,98},{3,227},{4,100},{5,229},{6,102},{7,231},{8,1... | collective-permute-start | bytes 15368 | tf_op jit(solution)/shard_map/ppermute | solution.py:193
  114.5 0.7 collective-permute-start.7
  115.1 0.1 collective-permute-start.8
  115.2 0.6 collective-permute-start.9
  115.8 16.2 %collective-permute-done.10 = f32[40,32]{1,0:T(8,128)S(1)} collective-permute-done((f32[40,32]{1,0:T(8,128)S(1)}, f32[40,32]{1,0:T(8,128)S(1)}, u32[]{:S(2)}, u32[]{:S(2)}) %collective-permute-start.10) | collective-permute-done | bytes 5152 | tf_op jit(solution)/shard_map/ppermute | solution.py:193
  132.0 0.0 collective-permute-done.7
  132.0 1.1 collective-permute-done.8
  133.1 0.0 collective-permute-done.9
  133.1 6.7 %all-to-all-done.1 = f32[256,16,128]{2,1,0:T(8,128)S(1)} async-done(((f32[256,16,128]{2,1,0:T(8,128)}), f32[256,16,128]{2,1,0:T(8,128)S(1)}, u32[]{:S(2)}, u32[]{:S(2)}) %all-to-all-start.1) | async-done | bytes 2097184 | tf_op jit(solution)/shard_map/all_to_all | solution.py:260
  139.7 0.0 collective-permute-start.11
  139.7 2.2 %shard_map.62 = f32[32,16384]{1,0:T(8,128)} custom-call(f32[4096,128]{1,0:T(8,128)S(1)} %bitcast.10), custom_call_target="tpu_custom_call" | custom-call | tf_op jit(solution)/shard_map/pallas_call | solution.py:279
  141.9 0.0 collective-permute-done.11
  142.0 0.6 slice_divide_fusion
  (5 shorter events, 0.0 us)
Async XLA Ops:
  78.8 60.9 %all-to-all-start.1 = ((f32[256,16,128]{2,1,0:T(8,128)}), f32[256,16,128]{2,1,0:T(8,128)S(1)}, u32[]{:S(2)}, u32[]{:S(2)}) async-start(f32[256,16,128]{2,1,0:T(8,128)} %get-tuple-element.6.y_ref), calls=%async_computation.1 | async-start | bytes 4194304 | tf_op jit(solution)/shard_map/all_to_all | solution.py:260
  91.5 1.4 collective-permute-start
  93.7 4.7 %collective-permute-start.1 = (f32[40,32]{1,0:T(8,128)S(1)}, f32[40,32]{1,0:T(8,128)S(1)}, u32[]{:S(2)}, u32[]{:S(2)}) collective-permute-start(f32[40,32]{1,0:T(8,128)S(1)} %add.36), channel_id=1, source_target_pairs={{0,2},{1,3},{2,0},{3,1},{4,6},{5,7},{6,4},{7,5},{8,10},{9,11},{10,... | collective-permute-start | bytes 15368 | tf_op jit(solution)/shard_map/ppermute | solution.py:193
  95.2 5.6 %collective-permute-start.2 = (f32[40,32]{1,0:T(8,128)S(1)}, f32[40,32]{1,0:T(8,128)S(1)}, u32[]{:S(2)}, u32[]{:S(2)}) collective-permute-start(f32[40,32]{1,0:T(8,128)S(1)} %add.36), channel_id=1, source_target_pairs={{0,4},{1,5},{2,6},{3,7},{4,0},{5,1},{6,2},{7,3},{8,12},{9,13},{10,... | collective-permute-start | bytes 15368 | tf_op jit(solution)/shard_map/ppermute | solution.py:193
  98.0 5.1 %collective-permute-start.3 = (f32[40,32]{1,0:T(8,128)S(1)}, f32[40,32]{1,0:T(8,128)S(1)}, u32[]{:S(2)}, u32[]{:S(2)}) collective-permute-start(f32[40,32]{1,0:T(8,128)S(1)} %add.36), channel_id=1, source_target_pairs={{0,6},{1,7},{2,4},{3,5},{4,2},{5,3},{6,0},{7,1},{8,14},{9,15},{10,... | collective-permute-start | bytes 15368 | tf_op jit(solution)/shard_map/ppermute | solution.py:193
  103.1 4.0 %collective-permute-start.4 = (f32[40,32]{1,0:T(8,128)S(1)}, f32[40,32]{1,0:T(8,128)S(1)}, u32[]{:S(2)}, u32[]{:S(2)}) collective-permute-start(f32[40,32]{1,0:T(8,128)S(1)} %add_add_fusion.2), channel_id=1, source_target_pairs={{0,16},{1,17},{2,18},{3,19},{4,20},{5,21},{6,22},{7,23},{8,24},{9,... | collective-permute-start | bytes 15368 | tf_op jit(solution)/shard_map/ppermute | solution.py:193
  103.7 5.7 %collective-permute-start.5 = (f32[40,32]{1,0:T(8,128)S(1)}, f32[40,32]{1,0:T(8,128)S(1)}, u32[]{:S(2)}, u32[]{:S(2)}) collective-permute-start(f32[40,32]{1,0:T(8,128)S(1)} %add_add_fusion.2), channel_id=1, source_target_pairs={{0,8},{1,9},{2,10},{3,11},{4,12},{5,13},{6,14},{7,15},{8,0},{9,1},... | collective-permute-start | bytes 15368 | tf_op jit(solution)/shard_map/ppermute | solution.py:193
  106.3 3.9 %collective-permute-start.6 = (f32[40,32]{1,0:T(8,128)S(1)}, f32[40,32]{1,0:T(8,128)S(1)}, u32[]{:S(2)}, u32[]{:S(2)}) collective-permute-start(f32[40,32]{1,0:T(8,128)S(1)} %add_add_fusion.2), channel_id=1, source_target_pairs={{0,24},{1,25},{2,26},{3,27},{4,28},{5,29},{6,30},{7,31},{8,16},{9,... | collective-permute-start | bytes 15368 | tf_op jit(solution)/shard_map/ppermute | solution.py:193
  110.2 21.7 %collective-permute-start.10 = (f32[40,32]{1,0:T(8,128)S(1)}, f32[40,32]{1,0:T(8,128)S(1)}, u32[]{:S(2)}, u32[]{:S(2)}) collective-permute-start(f32[40,32]{1,0:T(8,128)S(1)} %add_add_fusion.1), channel_id=1, source_target_pairs={{0,96},{1,225},{2,98},{3,227},{4,100},{5,229},{6,102},{7,231},{8,1... | collective-permute-start | bytes 15368 | tf_op jit(solution)/shard_map/ppermute | solution.py:193
  114.5 17.5 %collective-permute-start.7 = (f32[40,32]{1,0:T(8,128)S(1)}, f32[40,32]{1,0:T(8,128)S(1)}, u32[]{:S(2)}, u32[]{:S(2)}) collective-permute-start(f32[40,32]{1,0:T(8,128)S(1)} %add_add_fusion.1), channel_id=1, source_target_pairs={{1,129},{3,131},{5,133},{7,135},{9,137},{11,139},{13,141},{15,143}... | collective-permute-start | bytes 15368 | tf_op jit(solution)/shard_map/ppermute | solution.py:193
  115.1 17.9 %collective-permute-start.8 = (f32[40,32]{1,0:T(8,128)S(1)}, f32[40,32]{1,0:T(8,128)S(1)}, u32[]{:S(2)}, u32[]{:S(2)}) collective-permute-start(f32[40,32]{1,0:T(8,128)S(1)} %add_add_fusion.1), channel_id=1, source_target_pairs={{0,32},{1,161},{2,34},{3,163},{4,36},{5,165},{6,38},{7,167},{8,40}... | collective-permute-start | bytes 15368 | tf_op jit(solution)/shard_map/ppermute | solution.py:193
  115.2 17.8 %collective-permute-start.9 = (f32[40,32]{1,0:T(8,128)S(1)}, f32[40,32]{1,0:T(8,128)S(1)}, u32[]{:S(2)}, u32[]{:S(2)}) collective-permute-start(f32[40,32]{1,0:T(8,128)S(1)} %add_add_fusion.1), channel_id=1, source_target_pairs={{0,64},{1,193},{2,66},{3,195},{4,68},{5,197},{6,70},{7,199},{8,72}... | collective-permute-start | bytes 15368 | tf_op jit(solution)/shard_map/ppermute | solution.py:193
  139.7 2.2 %collective-permute-start.11 = (f32[40,32]{1,0:T(8,128)S(1)}, f32[40,32]{1,0:T(8,128)S(1)}, u32[]{:S(2)}, u32[]{:S(2)}) collective-permute-start(f32[40,32]{1,0:T(8,128)S(1)} %add_add_fusion), channel_id=1, source_target_pairs={{0,1},{1,0},{2,3},{3,2},{4,5},{5,4},{6,7},{7,6},{8,9},{9,8},{10,11... | collective-permute-start | bytes 15368 | tf_op jit(solution)/shard_map/ppermute | solution.py:193

commit v3 on v0

v3 whole, which is shorter than its diff:
```python
import math

import jax
import jax.numpy as jnp
from jax import lax
from jax.experimental import pallas as pl
from jax.experimental.pallas import tpu as pltpu
from jax.sharding import Mesh
from jax.sharding import PartitionSpec as P

LOW = 32
HIGH = 128
LANES = 128
CHIP = ("wide", "high")
AXES = ("wide", "high", "core")
SMEM = pl.BlockSpec(memory_space=pltpu.SMEM)
VMEM = pl.BlockSpec(memory_space=pltpu.VMEM)
HBM = pl.BlockSpec(memory_space=pltpu.HBM)
PARAMS = pltpu.CompilerParams(vmem_limit_bytes=32 * 2**20)


def signs_of(i, j, n):
    v = jnp.bitwise_and(i, j)
    shift = 1
    while shift < n.bit_length():
        v = jnp.bitwise_xor(v, jnp.right_shift(v, shift))
        shift *= 2
    return (1 - 2 * jnp.bitwise_and(v, 1)).astype(jnp.float32)


def split(x):
    hi = x.astype(jnp.bfloat16)
    lo = (x - hi.astype(jnp.float32)).astype(jnp.bfloat16)
    return hi, lo


def dot(a, b):
    return jnp.dot(a, b, preferred_element_type=jnp.float32)


def butterfly(vs):
    step = 1
    while step < len(vs):
        out = list(vs)
        for i in range(len(vs)):
            if not i & step:
                out[i] = vs[i] + vs[i | step]
                out[i | step] = vs[i] - vs[i | step]
        vs = out
        step *= 2
    return vs


def prepare_kernel(counts_ref, rows_ref, panel_ref, signs_ref, mask_ref, own_ref):
    rows = rows_ref[...]
    samples = rows.shape[1]
    slot = lax.broadcasted_iota(jnp.int32, (1, samples), 1)
    rows = jnp.where(slot < counts_ref[0], rows, -1)
    at = lax.broadcasted_iota(jnp.int32, (HIGH, samples), 0)
    tile = (jnp.right_shift(rows, 7) == at).astype(jnp.float32).astype(jnp.bfloat16)
    inner = (jnp.bitwise_and(rows, HIGH - 1) == at).astype(jnp.float32).astype(jnp.bfloat16)
    mask_ref[...] = lax.dot_general(tile, inner, (((1,), (1,)), ((), ())), preferred_element_type=jnp.float32)
    own_sign = 1 - 2 * lax.axis_index("core")
    own_ref[...] = panel_ref[...] * (signs_ref[...] * own_sign).astype(jnp.float32)


def local_kernel(scale, own_ref, other_ref, other_signs_ref, mask_ref, out_ref, x_ref):
    width, length = own_ref.shape
    slab = LOW * HIGH
    i = lax.broadcasted_iota(jnp.int32, (2 * HIGH, HIGH), 0)
    j = lax.broadcasted_iota(jnp.int32, (2 * HIGH, HIGH), 1)
    table = (signs_of(jnp.bitwise_and(i, HIGH - 1), j, HIGH) * scale).astype(jnp.bfloat16)
    per = 8
    for s in range(length // slab):
        for g in range(width // 8):
            vs = []
            for a in range(LOW):
                cols = slice(slab * s + LANES * a, slab * s + LANES * (a + 1))
                rows = slice(8 * g, 8 * g + 8)
                vs.append(own_ref[rows, cols] + other_ref[rows, cols] * other_signs_ref[:, cols].astype(jnp.float32))
            for a, v in enumerate(butterfly(vs)):
                x_ref[s % 2, width * a + 8 * g : width * a + 8 * g + 8, :] = v
        for c in range(LOW // per):
            hi, lo = split(x_ref[s % 2, width * per * c : width * per * (c + 1), :])
            z = dot(jnp.concatenate([hi, lo], axis=1), table)
            for k in range(per):
                t = LOW * s + per * c + k
                row = (width + 1) * t
                out_ref[row : row + width, :] = z[width * k : width * (k + 1), :]
                out_ref[row + width : row + width + 1, :] = mask_ref[t : t + 1, :]


def across_kernel(chips, width, in_ref, out_hbm, mask_hbm, keep_ref, mask_ref, sems):
    i = lax.broadcasted_iota(jnp.int32, (chips, 2 * chips), 0)
    j = lax.broadcasted_iota(jnp.int32, (chips, 2 * chips), 1)
    table = signs_of(i, jnp.where(j < chips, j, j - chips), chips).astype(jnp.bfloat16)
    mask_ref[...] = in_ref[pl.ds(width, chips, stride=width + 1), :]
    copies = [pltpu.make_async_copy(mask_ref, mask_hbm, sems.at[width // 8])]
    copies[0].start()
    tiles = keep_ref.reshape(chips, width, LANES)
    for part in range(width // 8):
        for k in range(8 * part, 8 * part + 8, 2):
            x = jnp.concatenate(
                [in_ref[pl.ds(k + n, chips, stride=width + 1), :] for n in range(2)], axis=1
            )
            y = dot(table, jnp.concatenate(split(x), axis=0))
            for n in range(2):
                keep_ref[pl.ds(k + n, chips, stride=width), :] = y[:, LANES * n : LANES * (n + 1)]
        rows = pl.ds(8 * part, 8)
        copies.append(pltpu.make_async_copy(tiles.at[:, rows, :], out_hbm.at[:, rows, :], sems.at[part]))
        copies[-1].start()
    for copy in copies:
        copy.wait()


def gram_kernel(counts_ref, y_ref, mask_ref, out_ref):
    blocks, width, _ = y_ref.shape

    @pl.when(pl.program_id(0) == 0)
    def _():
        out_ref[:width, :] = jnp.zeros((width, width), jnp.float32)
        out_ref[width:, :] = jnp.full((8, width), counts_ref[0].astype(jnp.float32))

    total = out_ref[:width, :]
    per = 8
    for c in range(0, blocks, per):
        plain = jnp.concatenate([y_ref[d] for d in range(c, c + per)], axis=1)
        masked = jnp.concatenate([y_ref[d] * mask_ref[d : d + 1, :] for d in range(c, c + per)], axis=1)
        a_hi, a_lo = split(masked)
        b_hi, b_lo = split(plain)
        nt = (((1,), (1,)), ((), ()))
        for a, b in ((a_hi, b_hi), (a_hi, b_lo), (a_lo, b_hi)):
            total = total + lax.dot_general(a, b, nt, preferred_element_type=jnp.float32)
    out_ref[:width, :] = total


def unpack_kernel(in_ref, out_ref):
    for t in range(in_ref.shape[0]):
        out_ref[:, LANES * t : LANES * (t + 1)] = in_ref[t]


def send(x, move):
    wide, high, core = (lax.axis_size(axis) for axis in AXES)
    pairs = []
    for w in range(wide):
        for h in range(high):
            for c in range(core):
                to = move(w, h, c)
                if to is not None:
                    pairs.append(((w * high + h) * core + c, (to[0] * high + to[1]) * core + to[2]))
    return lax.ppermute(x, AXES, pairs)


def half_sum(x):
    x = x + send(x, lambda w, h, c: (w, h, c ^ 1))
    x = x + sum(send(x, lambda w, h, c, n=n: (w, h ^ n, c)) for n in (1, 2, 3))
    x = x + sum(send(x, lambda w, h, c, n=n: (w ^ (n & 1), h ^ (2 * (n & 2)), c)) for n in (1, 2, 3))
    half = lax.axis_size("wide") // 4
    own = jnp.where(lax.axis_index("core") == 0, x, 0.0)
    for step in range(half):
        own = own + send(
            x,
            lambda w, h, c, step=step: (w ^ (2 * (step + half * c)), h, c) if step + c else None,
        )
    return own


def shards(panel, signs, sample_rows, counts):
    width, length = panel.shape
    slab = LOW * HIGH
    chips = lax.axis_size("wide") * lax.axis_size("high")
    samples = sample_rows.shape[0]
    scale = 1.0 / math.sqrt(slab * chips * lax.axis_size("core"))
    f32 = jnp.float32
    message = width + 1

    swap = [(0, 1), (1, 0)]
    other = lax.ppermute(panel, "core", swap)
    other_signs = lax.ppermute(signs, "core", swap)

    live, own = pl.pallas_call(
        prepare_kernel,
        in_specs=[SMEM, VMEM, VMEM, VMEM],
        out_shape=(jax.ShapeDtypeStruct((chips, LANES), f32), jax.ShapeDtypeStruct((width, length), f32)),
        compiler_params=PARAMS,
    )(counts, sample_rows.reshape(1, samples), panel, signs.reshape(1, length))

    sent = pl.pallas_call(
        lambda *refs: local_kernel(scale, *refs),
        out_shape=jax.ShapeDtypeStruct((message * chips, LANES), f32),
        scratch_shapes=[pltpu.VMEM((2, width * LOW, LANES), f32)],
        compiler_params=PARAMS,
    )(own, other, other_signs.reshape(1, length), live)

    got = lax.all_to_all(sent.reshape(message * chips, 1, LANES), CHIP, 0, 0, tiled=True)

    mixed, mask = pl.pallas_call(
        lambda *refs: across_kernel(chips, width, *refs),
        in_specs=[VMEM],
        out_specs=(HBM, HBM),
        out_shape=(pltpu.HBM((chips, width, LANES), f32), pltpu.HBM((chips, LANES), f32)),
        scratch_shapes=[
            pltpu.VMEM((width * chips, LANES), f32),
            pltpu.VMEM((chips, LANES), f32),
            pltpu.SemaphoreType.DMA((width // 8 + 1,)),
        ],
        compiler_params=PARAMS,
    )(got.reshape(message * chips, LANES))

    back = lax.all_to_all(mixed, CHIP, 0, 0, tiled=True)

    steps = 8
    part = pl.pallas_call(
        gram_kernel,
        grid=(steps,),
        in_specs=[
            SMEM,
            pl.BlockSpec((chips // steps, width, LANES), lambda s: (s, 0, 0)),
            pl.BlockSpec((chips // steps, LANES), lambda s: (s, 0)),
        ],
        out_specs=pl.BlockSpec((width + 8, width), lambda s: (0, 0)),
        out_shape=jax.ShapeDtypeStruct((width + 8, width), f32),
        compiler_params=pltpu.CompilerParams(vmem_limit_bytes=60 * 2**20),
    )(counts, mixed, mask)
    total = half_sum(part)
    total = total + send(total, lambda w, h, c: (w, h, c ^ 1))
    gram = total[:width] / total[width : width + 1]

    pieces = 4
    out = pl.pallas_call(
        unpack_kernel,
        grid=(pieces,),
        in_specs=[pl.BlockSpec((chips // pieces, width, LANES), lambda s: (s, 0, 0))],
        out_specs=pl.BlockSpec((width, length // pieces), lambda s: (0, s)),
        out_shape=jax.ShapeDtypeStruct((width, length), f32),
        compiler_params=PARAMS,
    )(back)
    return out, gram


def solution(mesh):
    wide, narrow = mesh.devices.shape
    mesh = Mesh(mesh.devices.reshape(wide, narrow // 2, 2), AXES)
    placed = (P(None, AXES), P(AXES), P(AXES), P(AXES))
    return jax.shard_map(
        shards,
        mesh=mesh,
        in_specs=placed,
        out_specs=(P(None, AXES), P()),
        check_vma=False,
    )
```

time: 553 us -> 141 us (0.25)
  waiting for transfers between devices: 405 us -> 31 us
  other arithmetic: 26.4 us -> 1.38 us
  local copies, waits for them, and re-layouts: 15.4 us -> 3.11 us
  Pallas kernels: 0 us -> 11.8 us
  blocking collectives: 76.1 us -> 69.4 us
    ppermute x8 -> x14, waiting for transfers between devices: 405 us -> 27.5 us  [the longest x12 27.5 us: send(): return lax.ppermute(x, AXES, pairs)]
    psum x1 -> x0, blocking collectives: 76.1 us -> none  [shards(): lax.psum((outer, jnp.sum(counts.astype(jnp.float32))), ('wide', 'narrow'))]
    all_to_all x0 -> x1, blocking collectives: none -> 69.4 us  [shards(): lax.all_to_all(sent.reshape(message * chips, 1, LANES), CHIP, 0, 0, tiled...]
    add x7 -> x5, other arithmetic: 19.4 us -> 0.77 us  [the longest x1 0.73 us: half_sum(): x = x + send(x, lambda w, h, c: (w, h, c ^ 1))]
    pallas_call x0 -> x5, Pallas kernels: none -> 11.8 us  [the longest x1 5.77 us: shards(): pl.pallas_call(gram_kernel, grid=(steps,), in_specs=[SMEM, pl.BlockSpec((...]
    all_to_all x0 -> x1, starting transfers between devices: none -> 7.34 us  [shards(): back = lax.all_to_all(mixed, CHIP, 0, 0, tiled=True)]
    mul x1 -> x0, local copies, waits for them, and re-layouts: 6.26 us -> none  [shards(): mixed = work * (1.0 / math.sqrt(LOW * HIGH * blocks))]
    gather x1 -> x0, local copies, waits for them, and re-layouts: 6.19 us -> none  [shards(): picked = mixed[:, sample_rows] * live[None, :]]
  transfers between devices with their start and end apart: 8 -> 15, of which waited for: 8 -> 10; matrix products, arithmetic and copies ran while one was open for 0% -> 1% of each run, Pallas kernels for 0% -> 4%
where the time goes in v3:
time: 141 us; the launch traced here: 140 us
  blocking collectives  69.4 us (49%)
  waiting for transfers between devices  31 us (22%)
  starting transfers between devices  21.6 us (15%)
  Pallas kernels  11.8 us (8%)
  local copies, waits for them, and re-layouts  3.11 us (2%)
    all_to_all x1, blocking collectives, shards(): lax.all_to_all(sent.reshape(message * chips, 1, LANES), CHIP, 0, 0, tiled...  69.4 us
    ppermute x12, waiting for transfers between devices, send(): return lax.ppermute(x, AXES, pairs)  27.5 us
    ppermute x12, starting transfers between devices, send(): return lax.ppermute(x, AXES, pairs)  13.7 us
    all_to_all x1, starting transfers between devices, shards(): back = lax.all_to_all(mixed, CHIP, 0, 0, tiled=True)  7.34 us
    pallas_call x1, Pallas kernels, shards(): pl.pallas_call(gram_kernel, grid=(steps,), in_specs=[SMEM, pl.BlockSpec((...  5.77 us
    all_to_all x1, waiting for transfers between devices, shards(): back = lax.all_to_all(mixed, CHIP, 0, 0, tiled=True)  3.5 us
    unnamed x6, local copies, waits for them, and re-layouts  3.11 us
  transfers between devices with their start and end apart: 15, of which 10 were waited for; matrix products, arithmetic and copies ran while one was open for 1% of the time, Pallas kernels for 4%

profile of v3, /device:TPU:2, one launch (start us, length us, event | category | flops | bytes accessed | tf_op | source)
XLA Modules:
  0.0 139.7 jit_solution(17860852814729137951)
XLA Ops:
  0.6 0.1 collective-permute-start
  0.7 0.5 collective-permute-start.1
  1.9 0.0 copy-start
  1.9 1.6 %copy-done = f32[32,16384]{1,0:T(8,128)S(1)} copy-done((f32[32,16384]{1,0:T(8,128)S(1)}, f32[32,16384]{1,0:T(8,128)}, u32[]{:S(2)}) %copy-start) | copy-done | bytes 2097176
  3.5 0.0 copy-start.1
  3.5 0.8 copy-done.1
  4.3 0.0 copy-start.2
  4.3 0.7 copy-done.2
  5.0 0.5 shard_map.59
  5.5 0.0 collective-permute-done.1
  5.5 0.0 collective-permute-done.refs_1_
  5.5 1.3 shard_map.60
  6.9 69.4 %all_to_all.10 = f32[4224,1,128]{2,1,0:T(1,128)S(1)} all-to-all(f32[4224,1,128]{2,1,0:T(1,128)S(1)} %bitcast.9), channel_id=1, replica_groups=mesh['wide'=16,'high'=8,'core'=2] {'wide','high'}, dimensions={0} | all-to-all | bytes 4325376 | tf_op jit(solution)/shard_map/all_to_all | solution.py:195
  76.3 2.3 %shard_map.61 = (f32[128,32,128]{2,1,0:T(8,128)}, f32[128,128]{1,0:T(8,128)}) custom-call(f32[4224,128]{1,0:T(8,128)S(1)} %bitcast.10), custom_call_target="tpu_custom_call" | custom-call | tf_op jit(solution)/shard_map/pallas_call | solution.py:197
  78.7 7.3 %all-to-all-start.1 = ((f32[128,32,128]{2,1,0:T(8,128)}), f32[128,32,128]{2,1,0:T(8,128)S(1)}, u32[]{:S(2)}, u32[]{:S(2)}) async-start(f32[128,32,128]{2,1,0:T(8,128)} %get-tuple-element.8.y_ref), calls=%async_computation.1 | async-start | bytes 4194304 | tf_op jit(solution)/shard_map/all_to_all | solution.py:210
  86.0 5.8 %shard_map.63 = f32[40,32]{1,0:T(8,128)} custom-call(s32[1]{0:T(128)S(6)} %copy.7.counts_ref, f32[128,32,128]{2,1,0:T(8,128)} %get-tuple-element.8.y_ref, f32[128,128]{1,0:T(8,128)} %get-tuple-element.9.mask_ref), custom_call_target="tpu_custom_call" | custom-call | tf_op jit(solution)/shard_map/pallas_call | solution.py:213
  91.8 0.0 collective-permute-start.2
  91.8 1.4 %collective-permute-done.2 = f32[40,32]{1,0:T(8,128)S(1)} collective-permute-done((f32[40,32]{1,0:T(8,128)}, f32[40,32]{1,0:T(8,128)S(1)}, u32[]{:S(2)}, u32[]{:S(2)}) %collective-permute-start.2) | collective-permute-done | bytes 5152 | tf_op jit(solution)/shard_map/ppermute | solution.py:151
  93.2 0.7 add.36
  93.9 1.5 %collective-permute-start.3 = (f32[40,32]{1,0:T(8,128)S(1)}, f32[40,32]{1,0:T(8,128)S(1)}, u32[]{:S(2)}, u32[]{:S(2)}) collective-permute-start(f32[40,32]{1,0:T(8,128)S(1)} %add.36), channel_id=1, source_target_pairs={{0,2},{1,3},{2,0},{3,1},{4,6},{5,7},{6,4},{7,5},{8,10},{9,11},{10,... | collective-permute-start | bytes 15368 | tf_op jit(solution)/shard_map/ppermute | solution.py:151
  95.4 2.7 %collective-permute-start.4 = (f32[40,32]{1,0:T(8,128)S(1)}, f32[40,32]{1,0:T(8,128)S(1)}, u32[]{:S(2)}, u32[]{:S(2)}) collective-permute-start(f32[40,32]{1,0:T(8,128)S(1)} %add.36), channel_id=1, source_target_pairs={{0,4},{1,5},{2,6},{3,7},{4,0},{5,1},{6,2},{7,3},{8,12},{9,13},{10,... | collective-permute-start | bytes 15368 | tf_op jit(solution)/shard_map/ppermute | solution.py:151
  98.1 0.5 collective-permute-start.5
  98.6 0.0 collective-permute-done.3
  98.6 3.5 %collective-permute-done.4 = f32[40,32]{1,0:T(8,128)S(1)} collective-permute-done((f32[40,32]{1,0:T(8,128)S(1)}, f32[40,32]{1,0:T(8,128)S(1)}, u32[]{:S(2)}, u32[]{:S(2)}) %collective-permute-start.4) | collective-permute-done | bytes 5152 | tf_op jit(solution)/shard_map/ppermute | solution.py:151
  102.1 1.1 collective-permute-done.5
  103.2 0.6 collective-permute-start.6
  103.8 2.7 %collective-permute-start.7 = (f32[40,32]{1,0:T(8,128)S(1)}, f32[40,32]{1,0:T(8,128)S(1)}, u32[]{:S(2)}, u32[]{:S(2)}) collective-permute-start(f32[40,32]{1,0:T(8,128)S(1)} %add_add_fusion.2), channel_id=1, source_target_pairs={{0,8},{1,9},{2,10},{3,11},{4,12},{5,13},{6,14},{7,15},{8,0},{9,1},... | collective-permute-start | bytes 15368 | tf_op jit(solution)/shard_map/ppermute | solution.py:151
  106.5 0.5 collective-permute-start.8
  107.0 0.2 collective-permute-done.6
  107.2 2.0 %collective-permute-done.7 = f32[40,32]{1,0:T(8,128)S(1)} collective-permute-done((f32[40,32]{1,0:T(8,128)S(1)}, f32[40,32]{1,0:T(8,128)S(1)}, u32[]{:S(2)}, u32[]{:S(2)}) %collective-permute-start.7) | collective-permute-done | bytes 5152 | tf_op jit(solution)/shard_map/ppermute | solution.py:151
  109.2 1.1 collective-permute-done.8
  110.3 1.3 collective-permute-start.10
  111.7 2.8 %collective-permute-start.11 = (f32[40,32]{1,0:T(8,128)S(1)}, f32[40,32]{1,0:T(8,128)S(1)}, u32[]{:S(2)}, u32[]{:S(2)}) collective-permute-start(f32[40,32]{1,0:T(8,128)S(1)} %add_add_fusion.1), channel_id=1, source_target_pairs={{0,64},{1,193},{2,66},{3,195},{4,68},{5,197},{6,70},{7,199},{8,72}... | collective-permute-start | bytes 15368 | tf_op jit(solution)/shard_map/ppermute | solution.py:151
  114.4 0.4 collective-permute-start.12
  114.8 0.7 collective-permute-start.9
  115.5 16.9 %collective-permute-done.10 = f32[40,32]{1,0:T(8,128)S(1)} collective-permute-done((f32[40,32]{1,0:T(8,128)S(1)}, f32[40,32]{1,0:T(8,128)S(1)}, u32[]{:S(2)}, u32[]{:S(2)}) %collective-permute-start.10) | collective-permute-done | bytes 5152 | tf_op jit(solution)/shard_map/ppermute | solution.py:151
  132.4 0.0 collective-permute-done.11
  132.4 0.1 collective-permute-done.12
  132.5 0.0 collective-permute-done.9
  132.5 0.1 collective-permute-start.13
  132.6 1.2 collective-permute-done.13
  133.8 0.6 slice_divide_fusion
  134.4 3.5 %all-to-all-done.1.in_ref = f32[128,32,128]{2,1,0:T(8,128)S(1)} async-done(((f32[128,32,128]{2,1,0:T(8,128)}), f32[128,32,128]{2,1,0:T(8,128)S(1)}, u32[]{:S(2)}, u32[]{:S(2)}) %all-to-all-start.1) | async-done | bytes 2097184 | tf_op jit(solution)/shard_map/all_to_all | solution.py:210
  137.9 1.8 %shard_map.62 = f32[32,16384]{1,0:T(8,128)} custom-call(f32[128,32,128]{2,1,0:T(8,128)S(1)} %all-to-all-done.1.in_ref), custom_call_target="tpu_custom_call" | custom-call | tf_op jit(solution)/shard_map/pallas_call | solution.py:230
  (5 shorter events, 0.0 us)
Async XLA Ops:
  0.6 4.9 %collective-permute-start = (f32[32,16384]{1,0:T(8,128)}, f32[32,16384]{1,0:T(8,128)S(1)}, u32[]{:S(2)}, u32[]{:S(2)}) collective-permute-start(f32[32,16384]{1,0:T(8,128)} %panel_ref.1), channel_id=1, source_target_pairs={{0,1},{1,0},{2,3},{3,2},{4,5},{5,4},{6,7},{7,6},{8,9},{9,8},{10,11... | collective-permute-start | bytes 6291464 | tf_op jit(solution)/shard_map/ppermute | solution.py:178
  0.7 4.8 %collective-permute-start.1 = (s32[16384]{0:T(1024)}, s32[16384]{0:T(1024)S(1)}, u32[]{:S(2)}, u32[]{:S(2)}) collective-permute-start(s32[16384]{0:T(1024)} %param.5), channel_id=1, source_target_pairs={{0,1},{1,0},{2,3},{3,2},{4,5},{5,4},{6,7},{7,6},{8,9},{9,8},{10,11... | collective-permute-start | bytes 196616 | tf_op jit(solution)/shard_map/ppermute | solution.py:179
  1.9 1.6 %copy-start = (f32[32,16384]{1,0:T(8,128)S(1)}, f32[32,16384]{1,0:T(8,128)}, u32[]{:S(2)}) copy-start(f32[32,16384]{1,0:T(8,128)} %panel_ref.1) | copy-start | bytes 6291460
  3.5 0.8 copy-start.1
  4.3 0.7 copy-start.2
  78.7 59.2 %all-to-all-start.1 = ((f32[128,32,128]{2,1,0:T(8,128)}), f32[128,32,128]{2,1,0:T(8,128)S(1)}, u32[]{:S(2)}, u32[]{:S(2)}) async-start(f32[128,32,128]{2,1,0:T(8,128)} %get-tuple-element.8.y_ref), calls=%async_computation.1 | async-start | bytes 4194304 | tf_op jit(solution)/shard_map/all_to_all | solution.py:210
  91.8 1.4 %collective-permute-start.2 = (f32[40,32]{1,0:T(8,128)}, f32[40,32]{1,0:T(8,128)S(1)}, u32[]{:S(2)}, u32[]{:S(2)}) collective-permute-start(f32[40,32]{1,0:T(8,128)} %shard_map.63), channel_id=1, source_target_pairs={{0,1},{1,0},{2,3},{3,2},{4,5},{5,4},{6,7},{7,6},{8,9},{9,8},{10,11... | collective-permute-start | bytes 15368 | tf_op jit(solution)/shard_map/ppermute | solution.py:151
  93.9 4.7 %collective-permute-start.3 = (f32[40,32]{1,0:T(8,128)S(1)}, f32[40,32]{1,0:T(8,128)S(1)}, u32[]{:S(2)}, u32[]{:S(2)}) collective-permute-start(f32[40,32]{1,0:T(8,128)S(1)} %add.36), channel_id=1, source_target_pairs={{0,2},{1,3},{2,0},{3,1},{4,6},{5,7},{6,4},{7,5},{8,10},{9,11},{10,... | collective-permute-start | bytes 15368 | tf_op jit(solution)/shard_map/ppermute | solution.py:151
  95.4 6.7 %collective-permute-start.4 = (f32[40,32]{1,0:T(8,128)S(1)}, f32[40,32]{1,0:T(8,128)S(1)}, u32[]{:S(2)}, u32[]{:S(2)}) collective-permute-start(f32[40,32]{1,0:T(8,128)S(1)} %add.36), channel_id=1, source_target_pairs={{0,4},{1,5},{2,6},{3,7},{4,0},{5,1},{6,2},{7,3},{8,12},{9,13},{10,... | collective-permute-start | bytes 15368 | tf_op jit(solution)/shard_map/ppermute | solution.py:151
  98.1 5.1 %collective-permute-start.5 = (f32[40,32]{1,0:T(8,128)S(1)}, f32[40,32]{1,0:T(8,128)S(1)}, u32[]{:S(2)}, u32[]{:S(2)}) collective-permute-start(f32[40,32]{1,0:T(8,128)S(1)} %add.36), channel_id=1, source_target_pairs={{0,6},{1,7},{2,4},{3,5},{4,2},{5,3},{6,0},{7,1},{8,14},{9,15},{10,... | collective-permute-start | bytes 15368 | tf_op jit(solution)/shard_map/ppermute | solution.py:151
  103.2 4.0 %collective-permute-start.6 = (f32[40,32]{1,0:T(8,128)S(1)}, f32[40,32]{1,0:T(8,128)S(1)}, u32[]{:S(2)}, u32[]{:S(2)}) collective-permute-start(f32[40,32]{1,0:T(8,128)S(1)} %add_add_fusion.2), channel_id=1, source_target_pairs={{0,16},{1,17},{2,18},{3,19},{4,20},{5,21},{6,22},{7,23},{8,24},{9,... | collective-permute-start | bytes 15368 | tf_op jit(solution)/shard_map/ppermute | solution.py:151
  103.8 5.4 %collective-permute-start.7 = (f32[40,32]{1,0:T(8,128)S(1)}, f32[40,32]{1,0:T(8,128)S(1)}, u32[]{:S(2)}, u32[]{:S(2)}) collective-permute-start(f32[40,32]{1,0:T(8,128)S(1)} %add_add_fusion.2), channel_id=1, source_target_pairs={{0,8},{1,9},{2,10},{3,11},{4,12},{5,13},{6,14},{7,15},{8,0},{9,1},... | collective-permute-start | bytes 15368 | tf_op jit(solution)/shard_map/ppermute | solution.py:151
  106.5 3.8 %collective-permute-start.8 = (f32[40,32]{1,0:T(8,128)S(1)}, f32[40,32]{1,0:T(8,128)S(1)}, u32[]{:S(2)}, u32[]{:S(2)}) collective-permute-start(f32[40,32]{1,0:T(8,128)S(1)} %add_add_fusion.2), channel_id=1, source_target_pairs={{0,24},{1,25},{2,26},{3,27},{4,28},{5,29},{6,30},{7,31},{8,16},{9,... | collective-permute-start | bytes 15368 | tf_op jit(solution)/shard_map/ppermute | solution.py:151
  110.3 22.1 %collective-permute-start.10 = (f32[40,32]{1,0:T(8,128)S(1)}, f32[40,32]{1,0:T(8,128)S(1)}, u32[]{:S(2)}, u32[]{:S(2)}) collective-permute-start(f32[40,32]{1,0:T(8,128)S(1)} %add_add_fusion.1), channel_id=1, source_target_pairs={{0,32},{1,161},{2,34},{3,163},{4,36},{5,165},{6,38},{7,167},{8,40}... | collective-permute-start | bytes 15368 | tf_op jit(solution)/shard_map/ppermute | solution.py:151
  111.7 20.7 %collective-permute-start.11 = (f32[40,32]{1,0:T(8,128)S(1)}, f32[40,32]{1,0:T(8,128)S(1)}, u32[]{:S(2)}, u32[]{:S(2)}) collective-permute-start(f32[40,32]{1,0:T(8,128)S(1)} %add_add_fusion.1), channel_id=1, source_target_pairs={{0,64},{1,193},{2,66},{3,195},{4,68},{5,197},{6,70},{7,199},{8,72}... | collective-permute-start | bytes 15368 | tf_op jit(solution)/shard_map/ppermute | solution.py:151
  114.4 18.0 %collective-permute-start.12 = (f32[40,32]{1,0:T(8,128)S(1)}, f32[40,32]{1,0:T(8,128)S(1)}, u32[]{:S(2)}, u32[]{:S(2)}) collective-permute-start(f32[40,32]{1,0:T(8,128)S(1)} %add_add_fusion.1), channel_id=1, source_target_pairs={{0,96},{1,225},{2,98},{3,227},{4,100},{5,229},{6,102},{7,231},{8,1... | collective-permute-start | bytes 15368 | tf_op jit(solution)/shard_map/ppermute | solution.py:151
  114.8 17.7 %collective-permute-start.9 = (f32[40,32]{1,0:T(8,128)S(1)}, f32[40,32]{1,0:T(8,128)S(1)}, u32[]{:S(2)}, u32[]{:S(2)}) collective-permute-start(f32[40,32]{1,0:T(8,128)S(1)} %add_add_fusion.1), channel_id=1, source_target_pairs={{1,129},{3,131},{5,133},{7,135},{9,137},{11,139},{13,141},{15,143}... | collective-permute-start | bytes 15368 | tf_op jit(solution)/shard_map/ppermute | solution.py:151
  132.5 1.3 collective-permute-start.13

commit v4 on v3

--- a/solution.py
+++ b/solution.py
@@ -11,6 +11,7 @@
 LOW = 32
 HIGH = 128
 LANES = 128
+FAR = ((8, 6), (4, 5))
 CHIP = ("wide", "high")
 AXES = ("wide", "high", "core")
 SMEM = pl.BlockSpec(memory_space=pltpu.SMEM)
@@ -151,6 +152,15 @@
     return lax.ppermute(x, AXES, pairs)
 
 
+def paired_counts(counts):
+    got, side = counts, 0
+    for far_w, far_h in FAR:
+        got = send(got, lambda w, h, c: (w ^ far_w, h ^ far_h, c) if c else None)
+        side ^= far_w
+    first = jnp.bitwise_and(lax.axis_index("wide"), side & -side) == 0
+    return jnp.where(lax.axis_index("core") == 0, counts, jnp.where(first, counts + got, 0)), got
+
+
 def half_sum(x):
     x = x + send(x, lambda w, h, c: (w, h, c ^ 1))
     x = x + sum(send(x, lambda w, h, c, n=n: (w, h ^ n, c)) for n in (1, 2, 3))
@@ -192,6 +202,9 @@
         compiler_params=PARAMS,
     )(own, other, other_signs.reshape(1, length), live)
 
+    after, _ = lax.optimization_barrier((counts, other))
+    brought, step = paired_counts(after)
+    sent, step = lax.optimization_barrier((sent, step))
     got = lax.all_to_all(sent.reshape(message * chips, 1, LANES), CHIP, 0, 0, tiled=True)
 
     mixed, mask = pl.pallas_call(
@@ -220,8 +233,8 @@
         ],
         out_specs=pl.BlockSpec((width + 8, width), lambda s: (0, 0)),
         out_shape=jax.ShapeDtypeStruct((width + 8, width), f32),
-        compiler_params=pltpu.CompilerParams(vmem_limit_bytes=60 * 2**20),
-    )(counts, mixed, mask)
+        compiler_params=PARAMS,
+    )(brought, mixed, mask)
     total = half_sum(part)
     total = total + send(total, lambda w, h, c: (w, h, c ^ 1))
     gram = total[:width] / total[width : width + 1]

time: 141 us -> 132 us (0.936)
  starting transfers between devices: 21.6 us -> 45.7 us
  blocking collectives: 69.4 us -> 51.3 us
  waiting for transfers between devices: 31 us -> 17.3 us
  Pallas kernels: 11.8 us -> 8.05 us
  local copies, waits for them, and re-layouts: 3.11 us -> 4.71 us
    ppermute x12 -> x14, starting transfers between devices: 13.7 us -> 34.5 us  [send(): return lax.ppermute(x, AXES, pairs)]
    all_to_all x1, blocking collectives: 69.4 us -> 51.3 us  [shards(): lax.all_to_all(sent.reshape(message * chips, 1, LANES), CHIP, 0, 0, tiled...]
    ppermute x12 -> x14, waiting for transfers between devices: 27.5 us -> 17.3 us  [send(): return lax.ppermute(x, AXES, pairs)]
    pallas_call x1, Pallas kernels: 5.77 us -> 2.02 us  [shards(): pl.pallas_call(gram_kernel, grid=(steps,), in_specs=[SMEM, pl.BlockSpec((...]
    all_to_all x1, waiting for transfers between devices: 3.5 us -> 0.01 us  [shards(): back = lax.all_to_all(mixed, CHIP, 0, 0, tiled=True)]
    all_to_all x1, starting transfers between devices: 7.34 us -> 10.6 us  [shards(): back = lax.all_to_all(mixed, CHIP, 0, 0, tiled=True)]
    unnamed x6 -> x10, local copies, waits for them, and re-layouts: 3.11 us -> 4.7 us
  transfers between devices with their start and end apart: 15 -> 17, of which waited for: 10 -> 10; matrix products, arithmetic and copies ran while one was open for 1% -> 1% of each run, Pallas kernels for 4% -> 3%
where the time goes in v4:
time: 132 us; the launch traced here: 130 us
  blocking collectives  51.3 us (39%)
  starting transfers between devices  45.7 us (35%)
  waiting for transfers between devices  17.3 us (13%)
  Pallas kernels  8.05 us (6%)
  local copies, waits for them, and re-layouts  4.71 us (4%)
  between operations  2.1 us (2%)
    all_to_all x1, blocking collectives, shards(): lax.all_to_all(sent.reshape(message * chips, 1, LANES), CHIP, 0, 0, tiled...  51.3 us
    ppermute x14, starting transfers between devices, send(): return lax.ppermute(x, AXES, pairs)  34.5 us
    ppermute x14, waiting for transfers between devices, send(): return lax.ppermute(x, AXES, pairs)  17.3 us
    all_to_all x1, starting transfers between devices, shards(): back = lax.all_to_all(mixed, CHIP, 0, 0, tiled=True)  10.6 us
    unnamed x10, local copies, waits for them, and re-layouts  4.7 us
  transfers between devices with their start and end apart: 17, of which 10 were waited for; matrix products, arithmetic and copies ran while one was open for 1% of the time, Pallas kernels for 3%

profile of v4, /device:TPU:2, one launch (start us, length us, event | category | flops | bytes accessed | tf_op | source)
XLA Modules:
  0.0 129.8 jit_solution(10204005650517757870)
XLA Ops:
  0.6 0.1 collective-permute-start
  0.7 0.5 collective-permute-start.1
  1.9 0.0 copy-start.1
  1.9 1.6 %copy-done.1 = f32[32,16384]{1,0:T(8,128)S(1)} copy-done((f32[32,16384]{1,0:T(8,128)S(1)}, f32[32,16384]{1,0:T(8,128)}, u32[]{:S(2)}) %copy-start.1) | copy-done | bytes 2097176
  3.5 0.0 copy-start.2
  3.5 0.8 copy-done.2
  4.3 0.0 copy-start.4
  4.3 0.7 copy-done.4
  5.0 0.5 shard_map.59
  5.5 0.0 collective-permute-done.refs_1_
  5.5 1.2 collective-permute-start.2
  6.7 0.0 collective-permute-done.1
  6.7 1.4 %shard_map.60 = f32[4224,128]{1,0:T(8,128)S(1)} custom-call(f32[32,16384]{1,0:T(8,128)S(1)} %get-tuple-element.8.refs_0_, f32[32,16384]{1,0:T(8,128)S(1)} %collective-permute-done.refs_1_, s32[1,16384]{1,0:T(1,128)S(1)} %bitcast.13, f32[128,128]{1,0:T(8,128)S(1)} %get-tuple-element.9.refs_3_), custom_call_target="tpu_custom_call" | custom-call | tf_op jit(solution)/shard_map/pallas_call | solution.py:198
  8.1 0.0 collective-permute-done.2
  8.1 1.3 collective-permute-start.3
  9.3 0.0 collective-permute-done.3
  9.3 51.3 %all_to_all.10 = f32[4224,1,128]{2,1,0:T(1,128)S(1)} all-to-all(f32[4224,1,128]{2,1,0:T(1,128)S(1)} %bitcast.11), channel_id=1, replica_groups=mesh['wide'=16,'high'=8,'core'=2] {'wide','high'}, dimensions={0} | all-to-all | bytes 4325376 | tf_op jit(solution)/shard_map/all_to_all | solution.py:208
  60.6 2.3 %shard_map.61 = (f32[128,32,128]{2,1,0:T(8,128)}, f32[128,128]{1,0:T(8,128)}) custom-call(f32[4224,128]{1,0:T(8,128)S(1)} %bitcast.12), custom_call_target="tpu_custom_call" | custom-call | tf_op jit(solution)/shard_map/pallas_call | solution.py:210
  63.0 0.0 copy-start.3
  63.0 10.6 %all-to-all-start.1 = ((f32[128,32,128]{2,1,0:T(8,128)}), f32[128,32,128]{2,1,0:T(8,128)S(1)}, u32[]{:S(2)}, u32[]{:S(2)}) async-start(f32[128,32,128]{2,1,0:T(8,128)} %get-tuple-element.12.y_ref), calls=%async_computation.1 | async-start | bytes 4194304 | tf_op jit(solution)/shard_map/all_to_all | solution.py:223
  74.3 0.0 copy-done.3
  74.3 0.0 copy-start
  74.3 1.6 %copy-done = f32[128,32,128]{2,1,0:T(8,128)S(1)} copy-done((f32[128,32,128]{2,1,0:T(8,128)S(1)}, f32[128,32,128]{2,1,0:T(8,128)}, u32[]{:S(2)}) %copy-start) | copy-done | bytes 2097176
  75.9 2.0 %shard_map.63 = f32[40,32]{1,0:T(8,128)S(1)} custom-call(s32[1]{0:T(128)S(6)} %select_n.28.counts_ref, f32[128,32,128]{2,1,0:T(8,128)S(1)} %copy-done, f32[128,128]{1,0:T(8,128)S(1)} %copy-done.3), custom_call_target="tpu_custom_call" | custom-call | tf_op jit(solution)/shard_map/pallas_call | solution.py:226
  77.9 15.7 %collective-permute-start.4 = (f32[40,32]{1,0:T(8,128)S(1)}, f32[40,32]{1,0:T(8,128)S(1)}, u32[]{:S(2)}, u32[]{:S(2)}) collective-permute-start(f32[40,32]{1,0:T(8,128)S(1)} %shard_map.63), channel_id=1, source_target_pairs={{0,1},{1,0},{2,3},{3,2},{4,5},{5,4},{6,7},{7,6},{8,9},{9,8},{10,11... | collective-permute-start | bytes 15368 | tf_op jit(solution)/shard_map/ppermute | solution.py:152
  93.6 0.8 collective-permute-done.4
  94.4 1.5 %collective-permute-start.5 = (f32[40,32]{1,0:T(8,128)S(1)}, f32[40,32]{1,0:T(8,128)S(1)}, u32[]{:S(2)}, u32[]{:S(2)}) collective-permute-start(f32[40,32]{1,0:T(8,128)S(1)} %add.40), channel_id=1, source_target_pairs={{0,2},{1,3},{2,0},{3,1},{4,6},{5,7},{6,4},{7,5},{8,10},{9,11},{10,... | collective-permute-start | bytes 15368 | tf_op jit(solution)/shard_map/ppermute | solution.py:152
  95.9 2.7 %collective-permute-start.6 = (f32[40,32]{1,0:T(8,128)S(1)}, f32[40,32]{1,0:T(8,128)S(1)}, u32[]{:S(2)}, u32[]{:S(2)}) collective-permute-start(f32[40,32]{1,0:T(8,128)S(1)} %add.40), channel_id=1, source_target_pairs={{0,4},{1,5},{2,6},{3,7},{4,0},{5,1},{6,2},{7,3},{8,12},{9,13},{10,... | collective-permute-start | bytes 15368 | tf_op jit(solution)/shard_map/ppermute | solution.py:152
  98.6 0.6 collective-permute-start.7
  99.1 0.0 collective-permute-done.5
  99.1 2.1 %collective-permute-done.6 = f32[40,32]{1,0:T(8,128)S(1)} collective-permute-done((f32[40,32]{1,0:T(8,128)S(1)}, f32[40,32]{1,0:T(8,128)S(1)}, u32[]{:S(2)}, u32[]{:S(2)}) %collective-permute-start.6) | collective-permute-done | bytes 5152 | tf_op jit(solution)/shard_map/ppermute | solution.py:152
  101.2 2.5 %collective-permute-done.7 = f32[40,32]{1,0:T(8,128)S(1)} collective-permute-done((f32[40,32]{1,0:T(8,128)S(1)}, f32[40,32]{1,0:T(8,128)S(1)}, u32[]{:S(2)}, u32[]{:S(2)}) %collective-permute-start.7) | collective-permute-done | bytes 5152 | tf_op jit(solution)/shard_map/ppermute | solution.py:152
  103.7 1.7 %collective-permute-start.10 = (f32[40,32]{1,0:T(8,128)S(1)}, f32[40,32]{1,0:T(8,128)S(1)}, u32[]{:S(2)}, u32[]{:S(2)}) collective-permute-start(f32[40,32]{1,0:T(8,128)S(1)} %add_add_fusion.2), channel_id=1, source_target_pairs={{0,24},{1,25},{2,26},{3,27},{4,28},{5,29},{6,30},{7,31},{8,16},{9,... | collective-permute-start | bytes 15368 | tf_op jit(solution)/shard_map/ppermute | solution.py:152
  105.3 1.7 %collective-permute-start.8 = (f32[40,32]{1,0:T(8,128)S(1)}, f32[40,32]{1,0:T(8,128)S(1)}, u32[]{:S(2)}, u32[]{:S(2)}) collective-permute-start(f32[40,32]{1,0:T(8,128)S(1)} %add_add_fusion.2), channel_id=1, source_target_pairs={{0,16},{1,17},{2,18},{3,19},{4,20},{5,21},{6,22},{7,23},{8,24},{9,... | collective-permute-start | bytes 15368 | tf_op jit(solution)/shard_map/ppermute | solution.py:152
  107.0 0.2 collective-permute-start.9
  107.2 0.3 collective-permute-done.10
  107.5 1.6 %collective-permute-done.8 = f32[40,32]{1,0:T(8,128)S(1)} collective-permute-done((f32[40,32]{1,0:T(8,128)S(1)}, f32[40,32]{1,0:T(8,128)S(1)}, u32[]{:S(2)}, u32[]{:S(2)}) %collective-permute-start.8) | collective-permute-done | bytes 5152 | tf_op jit(solution)/shard_map/ppermute | solution.py:152
  109.1 3.4 %collective-permute-done.9 = f32[40,32]{1,0:T(8,128)S(1)} collective-permute-done((f32[40,32]{1,0:T(8,128)S(1)}, f32[40,32]{1,0:T(8,128)S(1)}, u32[]{:S(2)}, u32[]{:S(2)}) %collective-permute-start.9) | collective-permute-done | bytes 5152 | tf_op jit(solution)/shard_map/ppermute | solution.py:152
  112.6 0.7 collective-permute-start.11
  113.2 1.8 %collective-permute-start.12 = (f32[40,32]{1,0:T(8,128)S(1)}, f32[40,32]{1,0:T(8,128)S(1)}, u32[]{:S(2)}, u32[]{:S(2)}) collective-permute-start(f32[40,32]{1,0:T(8,128)S(1)} %add_add_fusion.1), channel_id=1, source_target_pairs={{0,32},{1,161},{2,34},{3,163},{4,36},{5,165},{6,38},{7,167},{8,40}... | collective-permute-start | bytes 15368 | tf_op jit(solution)/shard_map/ppermute | solution.py:152
  115.0 2.4 %collective-permute-start.13 = (f32[40,32]{1,0:T(8,128)S(1)}, f32[40,32]{1,0:T(8,128)S(1)}, u32[]{:S(2)}, u32[]{:S(2)}) collective-permute-start(f32[40,32]{1,0:T(8,128)S(1)} %add_add_fusion.1), channel_id=1, source_target_pairs={{0,64},{1,193},{2,66},{3,195},{4,68},{5,197},{6,70},{7,199},{8,72}... | collective-permute-start | bytes 15368 | tf_op jit(solution)/shard_map/ppermute | solution.py:152
  117.4 0.3 collective-permute-start.14
  117.7 0.0 collective-permute-done.11
  117.7 0.3 collective-permute-done.12
  118.0 2.3 %collective-permute-done.13 = f32[40,32]{1,0:T(8,128)S(1)} collective-permute-done((f32[40,32]{1,0:T(8,128)S(1)}, f32[40,32]{1,0:T(8,128)S(1)}, u32[]{:S(2)}, u32[]{:S(2)}) %collective-permute-start.13) | collective-permute-done | bytes 5152 | tf_op jit(solution)/shard_map/ppermute | solution.py:152
  120.3 3.2 %collective-permute-done.14 = f32[40,32]{1,0:T(8,128)S(1)} collective-permute-done((f32[40,32]{1,0:T(8,128)S(1)}, f32[40,32]{1,0:T(8,128)S(1)}, u32[]{:S(2)}, u32[]{:S(2)}) %collective-permute-start.14) | collective-permute-done | bytes 5152 | tf_op jit(solution)/shard_map/ppermute | solution.py:152
  123.5 3.0 %collective-permute-start.15 = (f32[40,32]{1,0:T(8,128)S(1)}, f32[40,32]{1,0:T(8,128)S(1)}, u32[]{:S(2)}, u32[]{:S(2)}) collective-permute-start(f32[40,32]{1,0:T(8,128)S(1)} %add_add_fusion), channel_id=1, source_target_pairs={{0,1},{1,0},{2,3},{3,2},{4,5},{5,4},{6,7},{7,6},{8,9},{9,8},{10,11... | collective-permute-start | bytes 15368 | tf_op jit(solution)/shard_map/ppermute | solution.py:152
  126.5 0.8 collective-permute-done.15
  127.3 0.6 slice_divide_fusion
  128.0 0.0 all-to-all-done.1.in_ref
  128.0 1.8 %shard_map.62 = f32[32,16384]{1,0:T(8,128)} custom-call(f32[128,32,128]{2,1,0:T(8,128)S(1)} %all-to-all-done.1.in_ref), custom_call_target="tpu_custom_call" | custom-call | tf_op jit(solution)/shard_map/pallas_call | solution.py:243
  (6 shorter events, 0.0 us)
Async XLA Ops:
  0.6 4.9 %collective-permute-start = (f32[32,16384]{1,0:T(8,128)}, f32[32,16384]{1,0:T(8,128)S(1)}, u32[]{:S(2)}, u32[]{:S(2)}) collective-permute-start(f32[32,16384]{1,0:T(8,128)} %panel_ref.1), channel_id=1, source_target_pairs={{0,1},{1,0},{2,3},{3,2},{4,5},{5,4},{6,7},{7,6},{8,9},{9,8},{10,11... | collective-permute-start | bytes 6291464 | tf_op jit(solution)/shard_map/ppermute | solution.py:188
  0.7 6.0 %collective-permute-start.1 = (s32[16384]{0:T(1024)}, s32[16384]{0:T(1024)S(1)}, u32[]{:S(2)}, u32[]{:S(2)}) collective-permute-start(s32[16384]{0:T(1024)} %param.5), channel_id=1, source_target_pairs={{0,1},{1,0},{2,3},{3,2},{4,5},{5,4},{6,7},{7,6},{8,9},{9,8},{10,11... | collective-permute-start | bytes 196616 | tf_op jit(solution)/shard_map/ppermute | solution.py:189
  1.9 1.6 %copy-start.1 = (f32[32,16384]{1,0:T(8,128)S(1)}, f32[32,16384]{1,0:T(8,128)}, u32[]{:S(2)}) copy-start(f32[32,16384]{1,0:T(8,128)} %panel_ref.1) | copy-start | bytes 6291460
  3.5 0.8 copy-start.2
  4.3 0.7 copy-start.4
  5.5 2.5 %collective-permute-start.2 = (s32[1]{0:T(128)}, s32[1]{0:T(128)}, u32[]{:S(2)}, u32[]{:S(2)}) collective-permute-start(s32[1]{0:T(128)} %param.7), channel_id=1, source_target_pairs={{1,141},{3,143},{5,137},{7,139},{9,133},{11,135},{13,129},{15,131}... | collective-permute-start | bytes 20 | tf_op jit(solution)/shard_map/ppermute | solution.py:152
  8.1 1.3 collective-permute-start.3
  63.0 11.3 %copy-start.3 = (f32[128,128]{1,0:T(8,128)S(1)}, f32[128,128]{1,0:T(8,128)}, u32[]{:S(2)}) copy-start(f32[128,128]{1,0:T(8,128)} %get-tuple-element.13.mask_ref) | copy-start | bytes 196612
  63.0 65.0 %all-to-all-start.1 = ((f32[128,32,128]{2,1,0:T(8,128)}), f32[128,32,128]{2,1,0:T(8,128)S(1)}, u32[]{:S(2)}, u32[]{:S(2)}) async-start(f32[128,32,128]{2,1,0:T(8,128)} %get-tuple-element.12.y_ref), calls=%async_computation.1 | async-start | bytes 4194304 | tf_op jit(solution)/shard_map/all_to_all | solution.py:223
  74.3 1.6 %copy-start = (f32[128,32,128]{2,1,0:T(8,128)S(1)}, f32[128,32,128]{2,1,0:T(8,128)}, u32[]{:S(2)}) copy-start(f32[128,32,128]{2,1,0:T(8,128)} %get-tuple-element.12.y_ref) | copy-start | bytes 6291460
  77.9 16.5 %collective-permute-start.4 = (f32[40,32]{1,0:T(8,128)S(1)}, f32[40,32]{1,0:T(8,128)S(1)}, u32[]{:S(2)}, u32[]{:S(2)}) collective-permute-start(f32[40,32]{1,0:T(8,128)S(1)} %shard_map.63), channel_id=1, source_target_pairs={{0,1},{1,0},{2,3},{3,2},{4,5},{5,4},{6,7},{7,6},{8,9},{9,8},{10,11... | collective-permute-start | bytes 15368 | tf_op jit(solution)/shard_map/ppermute | solution.py:152
  94.4 4.7 %collective-permute-start.5 = (f32[40,32]{1,0:T(8,128)S(1)}, f32[40,32]{1,0:T(8,128)S(1)}, u32[]{:S(2)}, u32[]{:S(2)}) collective-permute-start(f32[40,32]{1,0:T(8,128)S(1)} %add.40), channel_id=1, source_target_pairs={{0,2},{1,3},{2,0},{3,1},{4,6},{5,7},{6,4},{7,5},{8,10},{9,11},{10,... | collective-permute-start | bytes 15368 | tf_op jit(solution)/shard_map/ppermute | solution.py:152
  95.9 5.3 %collective-permute-start.6 = (f32[40,32]{1,0:T(8,128)S(1)}, f32[40,32]{1,0:T(8,128)S(1)}, u32[]{:S(2)}, u32[]{:S(2)}) collective-permute-start(f32[40,32]{1,0:T(8,128)S(1)} %add.40), channel_id=1, source_target_pairs={{0,4},{1,5},{2,6},{3,7},{4,0},{5,1},{6,2},{7,3},{8,12},{9,13},{10,... | collective-permute-start | bytes 15368 | tf_op jit(solution)/shard_map/ppermute | solution.py:152
  98.6 5.1 %collective-permute-start.7 = (f32[40,32]{1,0:T(8,128)S(1)}, f32[40,32]{1,0:T(8,128)S(1)}, u32[]{:S(2)}, u32[]{:S(2)}) collective-permute-start(f32[40,32]{1,0:T(8,128)S(1)} %add.40), channel_id=1, source_target_pairs={{0,6},{1,7},{2,4},{3,5},{4,2},{5,3},{6,0},{7,1},{8,14},{9,15},{10,... | collective-permute-start | bytes 15368 | tf_op jit(solution)/shard_map/ppermute | solution.py:152
  103.7 3.9 %collective-permute-start.10 = (f32[40,32]{1,0:T(8,128)S(1)}, f32[40,32]{1,0:T(8,128)S(1)}, u32[]{:S(2)}, u32[]{:S(2)}) collective-permute-start(f32[40,32]{1,0:T(8,128)S(1)} %add_add_fusion.2), channel_id=1, source_target_pairs={{0,24},{1,25},{2,26},{3,27},{4,28},{5,29},{6,30},{7,31},{8,16},{9,... | collective-permute-start | bytes 15368 | tf_op jit(solution)/shard_map/ppermute | solution.py:152
  105.3 3.8 %collective-permute-start.8 = (f32[40,32]{1,0:T(8,128)S(1)}, f32[40,32]{1,0:T(8,128)S(1)}, u32[]{:S(2)}, u32[]{:S(2)}) collective-permute-start(f32[40,32]{1,0:T(8,128)S(1)} %add_add_fusion.2), channel_id=1, source_target_pairs={{0,16},{1,17},{2,18},{3,19},{4,20},{5,21},{6,22},{7,23},{8,24},{9,... | collective-permute-start | bytes 15368 | tf_op jit(solution)/shard_map/ppermute | solution.py:152
  107.0 5.5 %collective-permute-start.9 = (f32[40,32]{1,0:T(8,128)S(1)}, f32[40,32]{1,0:T(8,128)S(1)}, u32[]{:S(2)}, u32[]{:S(2)}) collective-permute-start(f32[40,32]{1,0:T(8,128)S(1)} %add_add_fusion.2), channel_id=1, source_target_pairs={{0,8},{1,9},{2,10},{3,11},{4,12},{5,13},{6,14},{7,15},{8,0},{9,1},... | collective-permute-start | bytes 15368 | tf_op jit(solution)/shard_map/ppermute | solution.py:152
  112.6 5.1 %collective-permute-start.11 = (f32[40,32]{1,0:T(8,128)S(1)}, f32[40,32]{1,0:T(8,128)S(1)}, u32[]{:S(2)}, u32[]{:S(2)}) collective-permute-start(f32[40,32]{1,0:T(8,128)S(1)} %add_add_fusion.1), channel_id=1, source_target_pairs={{1,129},{3,131},{5,133},{7,135},{9,137},{11,139},{13,141},{15,143}... | collective-permute-start | bytes 15368 | tf_op jit(solution)/shard_map/ppermute | solution.py:152
  113.2 4.8 %collective-permute-start.12 = (f32[40,32]{1,0:T(8,128)S(1)}, f32[40,32]{1,0:T(8,128)S(1)}, u32[]{:S(2)}, u32[]{:S(2)}) collective-permute-start(f32[40,32]{1,0:T(8,128)S(1)} %add_add_fusion.1), channel_id=1, source_target_pairs={{0,32},{1,161},{2,34},{3,163},{4,36},{5,165},{6,38},{7,167},{8,40}... | collective-permute-start | bytes 15368 | tf_op jit(solution)/shard_map/ppermute | solution.py:152
  115.0 5.4 %collective-permute-start.13 = (f32[40,32]{1,0:T(8,128)S(1)}, f32[40,32]{1,0:T(8,128)S(1)}, u32[]{:S(2)}, u32[]{:S(2)}) collective-permute-start(f32[40,32]{1,0:T(8,128)S(1)} %add_add_fusion.1), channel_id=1, source_target_pairs={{0,64},{1,193},{2,66},{3,195},{4,68},{5,197},{6,70},{7,199},{8,72}... | collective-permute-start | bytes 15368 | tf_op jit(solution)/shard_map/ppermute | solution.py:152
  117.4 6.1 %collective-permute-start.14 = (f32[40,32]{1,0:T(8,128)S(1)}, f32[40,32]{1,0:T(8,128)S(1)}, u32[]{:S(2)}, u32[]{:S(2)}) collective-permute-start(f32[40,32]{1,0:T(8,128)S(1)} %add_add_fusion.1), channel_id=1, source_target_pairs={{0,96},{1,225},{2,98},{3,227},{4,100},{5,229},{6,102},{7,231},{8,1... | collective-permute-start | bytes 15368 | tf_op jit(solution)/shard_map/ppermute | solution.py:152
  123.5 3.8 %collective-permute-start.15 = (f32[40,32]{1,0:T(8,128)S(1)}, f32[40,32]{1,0:T(8,128)S(1)}, u32[]{:S(2)}, u32[]{:S(2)}) collective-permute-start(f32[40,32]{1,0:T(8,128)S(1)} %add_add_fusion), channel_id=1, source_target_pairs={{0,1},{1,0},{2,3},{3,2},{4,5},{5,4},{6,7},{7,6},{8,9},{9,8},{10,11... | collective-permute-start | bytes 15368 | tf_op jit(solution)/shard_map/ppermute | solution.py:152

commit v5 on v4

--- a/solution.py
+++ b/solution.py
@@ -52,7 +52,24 @@
     return vs
 
 
-def prepare_kernel(counts_ref, rows_ref, panel_ref, signs_ref, mask_ref, own_ref):
+def prepare_kernel(
+    counts_ref, rows_hbm, panel_hbm, signs_hbm, mask_ref, own_ref, rows_ref, panel_ref, signs_ref, sems
+):
+    width = panel_hbm.shape[0]
+    groups = [slice(8 * g, 8 * g + 8) for g in range(width // 8)]
+    small = [
+        pltpu.make_async_copy(source, target, sems.at[n])
+        for n, (source, target) in enumerate(
+            ((rows_hbm, rows_ref), (signs_hbm, signs_ref))
+        )
+    ]
+    big = [
+        pltpu.make_async_copy(panel_hbm.at[rows, :], panel_ref.at[rows, :], sems.at[2 + g])
+        for g, rows in enumerate(groups)
+    ]
+    for copy in small + big:
+        copy.start()
+    small[0].wait()
     rows = rows_ref[...]
     samples = rows.shape[1]
     slot = lax.broadcasted_iota(jnp.int32, (1, samples), 1)
@@ -62,7 +79,11 @@
     inner = (jnp.bitwise_and(rows, HIGH - 1) == at).astype(jnp.float32).astype(jnp.bfloat16)
     mask_ref[...] = lax.dot_general(tile, inner, (((1,), (1,)), ((), ())), preferred_element_type=jnp.float32)
     own_sign = 1 - 2 * lax.axis_index("core")
-    own_ref[...] = panel_ref[...] * (signs_ref[...] * own_sign).astype(jnp.float32)
+    small[1].wait()
+    sign = (signs_ref[...] * own_sign).astype(jnp.float32)
+    for g, rows in enumerate(groups):
+        big[g].wait()
+        own_ref[rows, :] = panel_ref[rows, :] * sign
 
 
 def local_kernel(scale, own_ref, other_ref, other_signs_ref, mask_ref, out_ref, x_ref):
@@ -188,12 +209,23 @@
     other = lax.ppermute(panel, "core", swap)
     other_signs = lax.ppermute(signs, "core", swap)
 
+    inputs = (sample_rows.reshape(1, samples), panel, signs.reshape(1, length))
     live, own = pl.pallas_call(
         prepare_kernel,
-        in_specs=[SMEM, VMEM, VMEM, VMEM],
+        in_specs=[SMEM] + [HBM] * 3,
+        out_specs=(VMEM, VMEM),
         out_shape=(jax.ShapeDtypeStruct((chips, LANES), f32), jax.ShapeDtypeStruct((width, length), f32)),
-        compiler_params=PARAMS,
-    )(counts, sample_rows.reshape(1, samples), panel, signs.reshape(1, length))
+        scratch_shapes=[
+            pltpu.VMEM((1, samples), jnp.int32),
+            pltpu.VMEM((width, length), f32),
+            pltpu.VMEM((1, length), jnp.int32),
+            pltpu.SemaphoreType.DMA((width // 8 + 2,)),
+        ],
+        compiler_params=PARAMS,
+    )(counts, *(pltpu.with_memory_space_constraint(x, pltpu.HBM) for x in inputs))
+
+    after, own = lax.optimization_barrier((counts, own))
+    brought, step = paired_counts(after)
 
     sent = pl.pallas_call(
         lambda *refs: local_kernel(scale, *refs),
@@ -202,8 +234,6 @@
         compiler_params=PARAMS,
     )(own, other, other_signs.reshape(1, length), live)
 
-    after, _ = lax.optimization_barrier((counts, other))
-    brought, step = paired_counts(after)
     sent, step = lax.optimization_barrier((sent, step))
     got = lax.all_to_all(sent.reshape(message * chips, 1, LANES), CHIP, 0, 0, tiled=True)
 

time: 132 us -> 130 us (0.985)
  local copies, waits for them, and re-layouts: 4.71 us -> 1.6 us
    unnamed x10 -> x4, local copies, waits for them, and re-layouts: 4.7 us -> 1.59 us
  transfers between devices with their start and end apart: 17 -> 17, of which waited for: 10 -> 10; matrix products, arithmetic and copies ran while one was open for 1% -> 1% of each run, Pallas kernels for 3% -> 4%
where the time goes in v5:
time: 130 us; the launch traced here: 128 us
  blocking collectives  51.3 us (39%)
  starting transfers between devices  45.6 us (35%)
  waiting for transfers between devices  17.3 us (13%)
  Pallas kernels  9.18 us (7%)
  between operations  2.09 us (2%)
  local copies, waits for them, and re-layouts  1.6 us (1%)
    all_to_all x1, blocking collectives, shards(): lax.all_to_all(sent.reshape(message * chips, 1, LANES), CHIP, 0, 0, tiled...  51.3 us
    ppermute x14, starting transfers between devices, send(): return lax.ppermute(x, AXES, pairs)  34.5 us
    ppermute x14, waiting for transfers between devices, send(): return lax.ppermute(x, AXES, pairs)  17.3 us
    all_to_all x1, starting transfers between devices, shards(): back = lax.all_to_all(mixed, CHIP, 0, 0, tiled=True)  10.5 us
  transfers between devices with their start and end apart: 17, of which 10 were waited for; matrix products, arithmetic and copies ran while one was open for 1% of the time, Pallas kernels for 4%

profile of v5, /device:TPU:2, one launch (start us, length us, event | category | flops | bytes accessed | tf_op | source)
XLA Modules:
  0.0 127.6 jit_solution(12267327361977523609)
XLA Ops:
  0.6 0.1 collective-permute-start
  0.7 0.5 collective-permute-start.1
  1.9 1.7 %shard_map.59 = (f32[128,128]{1,0:T(8,128)S(1)}, f32[32,16384]{1,0:T(8,128)S(1)}) custom-call(s32[1]{0:T(128)S(6)} %copy.7.counts_ref, s32[1,1024]{1,0:T(1,128)} %bitcast.15, f32[32,16384]{1,0:T(8,128)} %panel_hbm.1, s32[1,16384]{1,0:T(1,128)} %bitcast.14), custom_call_target="tpu_custom_call" | custom-call | tf_op jit(solution)/shard_map/pallas_call | solution.py:213
  3.6 1.2 collective-permute-start.2
  4.7 0.0 collective-permute-done.2
  4.7 1.2 collective-permute-start.3
  6.0 0.0 collective-permute-done.1
  6.0 0.0 collective-permute-done.refs_1_
  6.0 1.3 %shard_map.60 = f32[4224,128]{1,0:T(8,128)S(1)} custom-call(f32[32,16384]{1,0:T(8,128)S(1)} %get-tuple-element.10.refs_0_, f32[32,16384]{1,0:T(8,128)S(1)} %collective-permute-done.refs_1_, s32[1,16384]{1,0:T(1,128)S(1)} %bitcast.13, f32[128,128]{1,0:T(8,128)S(1)} %get-tuple-element.11.refs_3_), custom_call_target="tpu_custom_call" | custom-call | tf_op jit(solution)/shard_map/pallas_call | solution.py:230
  7.3 0.0 collective-permute-done.3
  7.3 51.3 %all_to_all.10 = f32[4224,1,128]{2,1,0:T(1,128)S(1)} all-to-all(f32[4224,1,128]{2,1,0:T(1,128)S(1)} %bitcast.11), channel_id=1, replica_groups=mesh['wide'=16,'high'=8,'core'=2] {'wide','high'}, dimensions={0} | all-to-all | bytes 4325376 | tf_op jit(solution)/shard_map/all_to_all | solution.py:238
  58.6 2.3 %shard_map.61 = (f32[128,32,128]{2,1,0:T(8,128)}, f32[128,128]{1,0:T(8,128)}) custom-call(f32[4224,128]{1,0:T(8,128)S(1)} %bitcast.12), custom_call_target="tpu_custom_call" | custom-call | tf_op jit(solution)/shard_map/pallas_call | solution.py:240
  60.9 0.0 copy-start.1
  60.9 10.5 %all-to-all-start.1 = ((f32[128,32,128]{2,1,0:T(8,128)}), f32[128,32,128]{2,1,0:T(8,128)S(1)}, u32[]{:S(2)}, u32[]{:S(2)}) async-start(f32[128,32,128]{2,1,0:T(8,128)} %get-tuple-element.14.y_ref), calls=%async_computation.1 | async-start | bytes 4194304 | tf_op jit(solution)/shard_map/all_to_all | solution.py:253
  72.2 0.0 copy-done.1
  72.2 0.0 copy-start
  72.2 1.6 %copy-done = f32[128,32,128]{2,1,0:T(8,128)S(1)} copy-done((f32[128,32,128]{2,1,0:T(8,128)S(1)}, f32[128,32,128]{2,1,0:T(8,128)}, u32[]{:S(2)}) %copy-start) | copy-done | bytes 2097176
  73.8 2.0 %shard_map.63 = f32[40,32]{1,0:T(8,128)S(1)} custom-call(s32[1]{0:T(128)S(6)} %select_n.28.counts_ref, f32[128,32,128]{2,1,0:T(8,128)S(1)} %copy-done, f32[128,128]{1,0:T(8,128)S(1)} %copy-done.1), custom_call_target="tpu_custom_call" | custom-call | tf_op jit(solution)/shard_map/pallas_call | solution.py:256
  75.8 15.8 %collective-permute-start.4 = (f32[40,32]{1,0:T(8,128)S(1)}, f32[40,32]{1,0:T(8,128)S(1)}, u32[]{:S(2)}, u32[]{:S(2)}) collective-permute-start(f32[40,32]{1,0:T(8,128)S(1)} %shard_map.63), channel_id=1, source_target_pairs={{0,1},{1,0},{2,3},{3,2},{4,5},{5,4},{6,7},{7,6},{8,9},{9,8},{10,11... | collective-permute-start | bytes 15368 | tf_op jit(solution)/shard_map/ppermute | solution.py:173
  91.6 0.8 collective-permute-done.4
  92.4 1.5 %collective-permute-start.5 = (f32[40,32]{1,0:T(8,128)S(1)}, f32[40,32]{1,0:T(8,128)S(1)}, u32[]{:S(2)}, u32[]{:S(2)}) collective-permute-start(f32[40,32]{1,0:T(8,128)S(1)} %add.40), channel_id=1, source_target_pairs={{0,2},{1,3},{2,0},{3,1},{4,6},{5,7},{6,4},{7,5},{8,10},{9,11},{10,... | collective-permute-start | bytes 15368 | tf_op jit(solution)/shard_map/ppermute | solution.py:173
  93.9 2.7 %collective-permute-start.6 = (f32[40,32]{1,0:T(8,128)S(1)}, f32[40,32]{1,0:T(8,128)S(1)}, u32[]{:S(2)}, u32[]{:S(2)}) collective-permute-start(f32[40,32]{1,0:T(8,128)S(1)} %add.40), channel_id=1, source_target_pairs={{0,4},{1,5},{2,6},{3,7},{4,0},{5,1},{6,2},{7,3},{8,12},{9,13},{10,... | collective-permute-start | bytes 15368 | tf_op jit(solution)/shard_map/ppermute | solution.py:173
  96.6 0.6 collective-permute-start.7
  97.1 0.0 collective-permute-done.5
  97.1 2.1 %collective-permute-done.6 = f32[40,32]{1,0:T(8,128)S(1)} collective-permute-done((f32[40,32]{1,0:T(8,128)S(1)}, f32[40,32]{1,0:T(8,128)S(1)}, u32[]{:S(2)}, u32[]{:S(2)}) %collective-permute-start.6) | collective-permute-done | bytes 5152 | tf_op jit(solution)/shard_map/ppermute | solution.py:173
  99.2 2.5 %collective-permute-done.7 = f32[40,32]{1,0:T(8,128)S(1)} collective-permute-done((f32[40,32]{1,0:T(8,128)S(1)}, f32[40,32]{1,0:T(8,128)S(1)}, u32[]{:S(2)}, u32[]{:S(2)}) %collective-permute-start.7) | collective-permute-done | bytes 5152 | tf_op jit(solution)/shard_map/ppermute | solution.py:173
  101.7 1.6 %collective-permute-start.10 = (f32[40,32]{1,0:T(8,128)S(1)}, f32[40,32]{1,0:T(8,128)S(1)}, u32[]{:S(2)}, u32[]{:S(2)}) collective-permute-start(f32[40,32]{1,0:T(8,128)S(1)} %add_add_fusion.2), channel_id=1, source_target_pairs={{0,24},{1,25},{2,26},{3,27},{4,28},{5,29},{6,30},{7,31},{8,16},{9,... | collective-permute-start | bytes 15368 | tf_op jit(solution)/shard_map/ppermute | solution.py:173
  103.3 1.7 %collective-permute-start.8 = (f32[40,32]{1,0:T(8,128)S(1)}, f32[40,32]{1,0:T(8,128)S(1)}, u32[]{:S(2)}, u32[]{:S(2)}) collective-permute-start(f32[40,32]{1,0:T(8,128)S(1)} %add_add_fusion.2), channel_id=1, source_target_pairs={{0,16},{1,17},{2,18},{3,19},{4,20},{5,21},{6,22},{7,23},{8,24},{9,... | collective-permute-start | bytes 15368 | tf_op jit(solution)/shard_map/ppermute | solution.py:173
  105.0 0.3 collective-permute-start.9
  105.3 0.3 collective-permute-done.10
  105.6 1.5 %collective-permute-done.8 = f32[40,32]{1,0:T(8,128)S(1)} collective-permute-done((f32[40,32]{1,0:T(8,128)S(1)}, f32[40,32]{1,0:T(8,128)S(1)}, u32[]{:S(2)}, u32[]{:S(2)}) %collective-permute-start.8) | collective-permute-done | bytes 5152 | tf_op jit(solution)/shard_map/ppermute | solution.py:173
  107.1 3.4 %collective-permute-done.9 = f32[40,32]{1,0:T(8,128)S(1)} collective-permute-done((f32[40,32]{1,0:T(8,128)S(1)}, f32[40,32]{1,0:T(8,128)S(1)}, u32[]{:S(2)}, u32[]{:S(2)}) %collective-permute-start.9) | collective-permute-done | bytes 5152 | tf_op jit(solution)/shard_map/ppermute | solution.py:173
  110.5 0.7 collective-permute-start.11
  111.2 1.7 %collective-permute-start.12 = (f32[40,32]{1,0:T(8,128)S(1)}, f32[40,32]{1,0:T(8,128)S(1)}, u32[]{:S(2)}, u32[]{:S(2)}) collective-permute-start(f32[40,32]{1,0:T(8,128)S(1)} %add_add_fusion.1), channel_id=1, source_target_pairs={{0,32},{1,161},{2,34},{3,163},{4,36},{5,165},{6,38},{7,167},{8,40}... | collective-permute-start | bytes 15368 | tf_op jit(solution)/shard_map/ppermute | solution.py:173
  112.8 2.5 %collective-permute-start.13 = (f32[40,32]{1,0:T(8,128)S(1)}, f32[40,32]{1,0:T(8,128)S(1)}, u32[]{:S(2)}, u32[]{:S(2)}) collective-permute-start(f32[40,32]{1,0:T(8,128)S(1)} %add_add_fusion.1), channel_id=1, source_target_pairs={{0,64},{1,193},{2,66},{3,195},{4,68},{5,197},{6,70},{7,199},{8,72}... | collective-permute-start | bytes 15368 | tf_op jit(solution)/shard_map/ppermute | solution.py:173
  115.3 0.3 collective-permute-start.14
  115.6 0.0 collective-permute-done.11
  115.6 0.3 collective-permute-done.12
  115.9 2.4 %collective-permute-done.13 = f32[40,32]{1,0:T(8,128)S(1)} collective-permute-done((f32[40,32]{1,0:T(8,128)S(1)}, f32[40,32]{1,0:T(8,128)S(1)}, u32[]{:S(2)}, u32[]{:S(2)}) %collective-permute-start.13) | collective-permute-done | bytes 5152 | tf_op jit(solution)/shard_map/ppermute | solution.py:173
  118.3 3.1 %collective-permute-done.14 = f32[40,32]{1,0:T(8,128)S(1)} collective-permute-done((f32[40,32]{1,0:T(8,128)S(1)}, f32[40,32]{1,0:T(8,128)S(1)}, u32[]{:S(2)}, u32[]{:S(2)}) %collective-permute-start.14) | collective-permute-done | bytes 5152 | tf_op jit(solution)/shard_map/ppermute | solution.py:173
  121.5 2.9 %collective-permute-start.15 = (f32[40,32]{1,0:T(8,128)S(1)}, f32[40,32]{1,0:T(8,128)S(1)}, u32[]{:S(2)}, u32[]{:S(2)}) collective-permute-start(f32[40,32]{1,0:T(8,128)S(1)} %add_add_fusion), channel_id=1, source_target_pairs={{0,1},{1,0},{2,3},{3,2},{4,5},{5,4},{6,7},{7,6},{8,9},{9,8},{10,11... | collective-permute-start | bytes 15368 | tf_op jit(solution)/shard_map/ppermute | solution.py:173
  124.3 0.8 collective-permute-done.15
  125.2 0.6 slice_divide_fusion
  125.8 0.0 all-to-all-done.1.in_ref
  125.8 1.8 %shard_map.62 = f32[32,16384]{1,0:T(8,128)} custom-call(f32[128,32,128]{2,1,0:T(8,128)S(1)} %all-to-all-done.1.in_ref), custom_call_target="tpu_custom_call" | custom-call | tf_op jit(solution)/shard_map/pallas_call | solution.py:273
  (6 shorter events, 0.0 us)
Async XLA Ops:
  0.6 5.4 %collective-permute-start = (f32[32,16384]{1,0:T(8,128)}, f32[32,16384]{1,0:T(8,128)S(1)}, u32[]{:S(2)}, u32[]{:S(2)}) collective-permute-start(f32[32,16384]{1,0:T(8,128)} %panel_hbm.1), channel_id=1, source_target_pairs={{0,1},{1,0},{2,3},{3,2},{4,5},{5,4},{6,7},{7,6},{8,9},{9,8},{10,11... | collective-permute-start | bytes 6291464 | tf_op jit(solution)/shard_map/ppermute | solution.py:209
  0.7 5.3 %collective-permute-start.1 = (s32[16384]{0:T(1024)}, s32[16384]{0:T(1024)S(1)}, u32[]{:S(2)}, u32[]{:S(2)}) collective-permute-start(s32[16384]{0:T(1024)} %param.5), channel_id=1, source_target_pairs={{0,1},{1,0},{2,3},{3,2},{4,5},{5,4},{6,7},{7,6},{8,9},{9,8},{10,11... | collective-permute-start | bytes 196616 | tf_op jit(solution)/shard_map/ppermute | solution.py:210
  3.6 1.2 collective-permute-start.2
  4.7 2.6 %collective-permute-start.3 = (s32[1]{0:T(128)}, s32[1]{0:T(128)}, u32[]{:S(2)}, u32[]{:S(2)}) collective-permute-start(s32[1]{0:T(128)} %collective-permute-done.2), channel_id=1, source_target_pairs={{1,75},{3,73},{5,79},{7,77},{9,67},{11,65},{13,71},{15,69},{17,91}... | collective-permute-start | bytes 20 | tf_op jit(solution)/shard_map/ppermute | solution.py:173
  60.9 11.2 %copy-start.1 = (f32[128,128]{1,0:T(8,128)S(1)}, f32[128,128]{1,0:T(8,128)}, u32[]{:S(2)}) copy-start(f32[128,128]{1,0:T(8,128)} %get-tuple-element.15.mask_ref) | copy-start | bytes 196612
  60.9 64.9 %all-to-all-start.1 = ((f32[128,32,128]{2,1,0:T(8,128)}), f32[128,32,128]{2,1,0:T(8,128)S(1)}, u32[]{:S(2)}, u32[]{:S(2)}) async-start(f32[128,32,128]{2,1,0:T(8,128)} %get-tuple-element.14.y_ref), calls=%async_computation.1 | async-start | bytes 4194304 | tf_op jit(solution)/shard_map/all_to_all | solution.py:253
  72.2 1.6 %copy-start = (f32[128,32,128]{2,1,0:T(8,128)S(1)}, f32[128,32,128]{2,1,0:T(8,128)}, u32[]{:S(2)}) copy-start(f32[128,32,128]{2,1,0:T(8,128)} %get-tuple-element.14.y_ref) | copy-start | bytes 6291460
  75.8 16.6 %collective-permute-start.4 = (f32[40,32]{1,0:T(8,128)S(1)}, f32[40,32]{1,0:T(8,128)S(1)}, u32[]{:S(2)}, u32[]{:S(2)}) collective-permute-start(f32[40,32]{1,0:T(8,128)S(1)} %shard_map.63), channel_id=1, source_target_pairs={{0,1},{1,0},{2,3},{3,2},{4,5},{5,4},{6,7},{7,6},{8,9},{9,8},{10,11... | collective-permute-start | bytes 15368 | tf_op jit(solution)/shard_map/ppermute | solution.py:173
  92.4 4.7 %collective-permute-start.5 = (f32[40,32]{1,0:T(8,128)S(1)}, f32[40,32]{1,0:T(8,128)S(1)}, u32[]{:S(2)}, u32[]{:S(2)}) collective-permute-start(f32[40,32]{1,0:T(8,128)S(1)} %add.40), channel_id=1, source_target_pairs={{0,2},{1,3},{2,0},{3,1},{4,6},{5,7},{6,4},{7,5},{8,10},{9,11},{10,... | collective-permute-start | bytes 15368 | tf_op jit(solution)/shard_map/ppermute | solution.py:173
  93.9 5.3 %collective-permute-start.6 = (f32[40,32]{1,0:T(8,128)S(1)}, f32[40,32]{1,0:T(8,128)S(1)}, u32[]{:S(2)}, u32[]{:S(2)}) collective-permute-start(f32[40,32]{1,0:T(8,128)S(1)} %add.40), channel_id=1, source_target_pairs={{0,4},{1,5},{2,6},{3,7},{4,0},{5,1},{6,2},{7,3},{8,12},{9,13},{10,... | collective-permute-start | bytes 15368 | tf_op jit(solution)/shard_map/ppermute | solution.py:173
  96.6 5.1 %collective-permute-start.7 = (f32[40,32]{1,0:T(8,128)S(1)}, f32[40,32]{1,0:T(8,128)S(1)}, u32[]{:S(2)}, u32[]{:S(2)}) collective-permute-start(f32[40,32]{1,0:T(8,128)S(1)} %add.40), channel_id=1, source_target_pairs={{0,6},{1,7},{2,4},{3,5},{4,2},{5,3},{6,0},{7,1},{8,14},{9,15},{10,... | collective-permute-start | bytes 15368 | tf_op jit(solution)/shard_map/ppermute | solution.py:173
  101.7 3.9 %collective-permute-start.10 = (f32[40,32]{1,0:T(8,128)S(1)}, f32[40,32]{1,0:T(8,128)S(1)}, u32[]{:S(2)}, u32[]{:S(2)}) collective-permute-start(f32[40,32]{1,0:T(8,128)S(1)} %add_add_fusion.2), channel_id=1, source_target_pairs={{0,24},{1,25},{2,26},{3,27},{4,28},{5,29},{6,30},{7,31},{8,16},{9,... | collective-permute-start | bytes 15368 | tf_op jit(solution)/shard_map/ppermute | solution.py:173
  103.3 3.8 %collective-permute-start.8 = (f32[40,32]{1,0:T(8,128)S(1)}, f32[40,32]{1,0:T(8,128)S(1)}, u32[]{:S(2)}, u32[]{:S(2)}) collective-permute-start(f32[40,32]{1,0:T(8,128)S(1)} %add_add_fusion.2), channel_id=1, source_target_pairs={{0,16},{1,17},{2,18},{3,19},{4,20},{5,21},{6,22},{7,23},{8,24},{9,... | collective-permute-start | bytes 15368 | tf_op jit(solution)/shard_map/ppermute | solution.py:173
  105.0 5.5 %collective-permute-start.9 = (f32[40,32]{1,0:T(8,128)S(1)}, f32[40,32]{1,0:T(8,128)S(1)}, u32[]{:S(2)}, u32[]{:S(2)}) collective-permute-start(f32[40,32]{1,0:T(8,128)S(1)} %add_add_fusion.2), channel_id=1, source_target_pairs={{0,8},{1,9},{2,10},{3,11},{4,12},{5,13},{6,14},{7,15},{8,0},{9,1},... | collective-permute-start | bytes 15368 | tf_op jit(solution)/shard_map/ppermute | solution.py:173
  110.5 5.1 %collective-permute-start.11 = (f32[40,32]{1,0:T(8,128)S(1)}, f32[40,32]{1,0:T(8,128)S(1)}, u32[]{:S(2)}, u32[]{:S(2)}) collective-permute-start(f32[40,32]{1,0:T(8,128)S(1)} %add_add_fusion.1), channel_id=1, source_target_pairs={{1,129},{3,131},{5,133},{7,135},{9,137},{11,139},{13,141},{15,143}... | collective-permute-start | bytes 15368 | tf_op jit(solution)/shard_map/ppermute | solution.py:173
  111.2 4.8 %collective-permute-start.12 = (f32[40,32]{1,0:T(8,128)S(1)}, f32[40,32]{1,0:T(8,128)S(1)}, u32[]{:S(2)}, u32[]{:S(2)}) collective-permute-start(f32[40,32]{1,0:T(8,128)S(1)} %add_add_fusion.1), channel_id=1, source_target_pairs={{0,32},{1,161},{2,34},{3,163},{4,36},{5,165},{6,38},{7,167},{8,40}... | collective-permute-start | bytes 15368 | tf_op jit(solution)/shard_map/ppermute | solution.py:173
  112.8 5.5 %collective-permute-start.13 = (f32[40,32]{1,0:T(8,128)S(1)}, f32[40,32]{1,0:T(8,128)S(1)}, u32[]{:S(2)}, u32[]{:S(2)}) collective-permute-start(f32[40,32]{1,0:T(8,128)S(1)} %add_add_fusion.1), channel_id=1, source_target_pairs={{0,64},{1,193},{2,66},{3,195},{4,68},{5,197},{6,70},{7,199},{8,72}... | collective-permute-start | bytes 15368 | tf_op jit(solution)/shard_map/ppermute | solution.py:173
  115.3 6.2 %collective-permute-start.14 = (f32[40,32]{1,0:T(8,128)S(1)}, f32[40,32]{1,0:T(8,128)S(1)}, u32[]{:S(2)}, u32[]{:S(2)}) collective-permute-start(f32[40,32]{1,0:T(8,128)S(1)} %add_add_fusion.1), channel_id=1, source_target_pairs={{0,96},{1,225},{2,98},{3,227},{4,100},{5,229},{6,102},{7,231},{8,1... | collective-permute-start | bytes 15368 | tf_op jit(solution)/shard_map/ppermute | solution.py:173
  121.5 3.7 %collective-permute-start.15 = (f32[40,32]{1,0:T(8,128)S(1)}, f32[40,32]{1,0:T(8,128)S(1)}, u32[]{:S(2)}, u32[]{:S(2)}) collective-permute-start(f32[40,32]{1,0:T(8,128)S(1)} %add_add_fusion), channel_id=1, source_target_pairs={{0,1},{1,0},{2,3},{3,2},{4,5},{5,4},{6,7},{7,6},{8,9},{9,8},{10,11... | collective-permute-start | bytes 15368 | tf_op jit(solution)/shard_map/ppermute | solution.py:173

commit v6 on v5

--- a/solution.py
+++ b/solution.py
@@ -11,7 +11,7 @@
 LOW = 32
 HIGH = 128
 LANES = 128
-FAR = ((8, 6), (4, 5))
+FAR = ((8, 6), (4, 6))
 CHIP = ("wide", "high")
 AXES = ("wide", "high", "core")
 SMEM = pl.BlockSpec(memory_space=pltpu.SMEM)
@@ -135,25 +135,31 @@
         copy.wait()
 
 
-def gram_kernel(counts_ref, y_ref, mask_ref, out_ref):
-    blocks, width, _ = y_ref.shape
-
-    @pl.when(pl.program_id(0) == 0)
-    def _():
-        out_ref[:width, :] = jnp.zeros((width, width), jnp.float32)
-        out_ref[width:, :] = jnp.full((8, width), counts_ref[0].astype(jnp.float32))
-
-    total = out_ref[:width, :]
+def gram_kernel(counts_ref, y_hbm, mask_hbm, out_ref, y_ref, mask_ref, sems):
+    blocks, width, _ = y_hbm.shape
+    parts = sems.shape[0] - 1
+    step = blocks // parts
+    copies = [pltpu.make_async_copy(mask_hbm, mask_ref, sems.at[parts])]
+    for n in range(parts):
+        rows = pl.ds(step * n, step)
+        copies.append(pltpu.make_async_copy(y_hbm.at[rows], y_ref.at[rows], sems.at[n]))
+    for copy in copies:
+        copy.start()
+    copies[0].wait()
+    total = jnp.zeros((width, width), jnp.float32)
     per = 8
+    nt = (((1,), (1,)), ((), ()))
     for c in range(0, blocks, per):
+        if c % step == 0:
+            copies[1 + c // step].wait()
         plain = jnp.concatenate([y_ref[d] for d in range(c, c + per)], axis=1)
         masked = jnp.concatenate([y_ref[d] * mask_ref[d : d + 1, :] for d in range(c, c + per)], axis=1)
         a_hi, a_lo = split(masked)
         b_hi, b_lo = split(plain)
-        nt = (((1,), (1,)), ((), ()))
         for a, b in ((a_hi, b_hi), (a_hi, b_lo), (a_lo, b_hi)):
             total = total + lax.dot_general(a, b, nt, preferred_element_type=jnp.float32)
     out_ref[:width, :] = total
+    out_ref[width:, :] = jnp.full((8, width), counts_ref[0].astype(jnp.float32))
 
 
 def unpack_kernel(in_ref, out_ref):
@@ -252,19 +258,18 @@
 
     back = lax.all_to_all(mixed, CHIP, 0, 0, tiled=True)
 
-    steps = 8
     part = pl.pallas_call(
         gram_kernel,
-        grid=(steps,),
-        in_specs=[
-            SMEM,
-            pl.BlockSpec((chips // steps, width, LANES), lambda s: (s, 0, 0)),
-            pl.BlockSpec((chips // steps, LANES), lambda s: (s, 0)),
+        in_specs=[SMEM, HBM, HBM],
+        out_specs=VMEM,
+        out_shape=jax.ShapeDtypeStruct((width + 8, width), f32),
+        scratch_shapes=[
+            pltpu.VMEM((chips, width, LANES), f32),
+            pltpu.VMEM((chips, LANES), f32),
+            pltpu.SemaphoreType.DMA((9,)),
         ],
-        out_specs=pl.BlockSpec((width + 8, width), lambda s: (0, 0)),
-        out_shape=jax.ShapeDtypeStruct((width + 8, width), f32),
-        compiler_params=PARAMS,
-    )(brought, mixed, mask)
+        compiler_params=PARAMS,
+    )(brought, *(pltpu.with_memory_space_constraint(x, pltpu.HBM) for x in (mixed, mask)))
     total = half_sum(part)
     total = total + send(total, lambda w, h, c: (w, h, c ^ 1))
     gram = total[:width] / total[width : width + 1]

time: 130 us -> 128 us (0.985)
  local copies, waits for them, and re-layouts: 1.6 us -> 0.01 us
    unnamed x4 -> x0, local copies, waits for them, and re-layouts: 1.59 us -> none
    ppermute x14, starting transfers between devices: 34.5 us -> 35.9 us  [send(): return lax.ppermute(x, AXES, pairs)]
  transfers between devices with their start and end apart: 17 -> 17, of which waited for: 10 -> 9; matrix products, arithmetic and copies ran while one was open for 1% -> 1% of each run, Pallas kernels for 4% -> 5%
where the time goes in v6:
time: 128 us; the launch traced here: 126 us
  blocking collectives  50.1 us (39%)
  starting transfers between devices  46.5 us (36%)
  waiting for transfers between devices  16.5 us (13%)
  Pallas kernels  10.3 us (8%)
  between operations  2 us (2%)
    all_to_all x1, blocking collectives, shards(): lax.all_to_all(sent.reshape(message * chips, 1, LANES), CHIP, 0, 0, tiled...  50.1 us
    ppermute x14, starting transfers between devices, send(): return lax.ppermute(x, AXES, pairs)  35.9 us
    ppermute x14, waiting for transfers between devices, send(): return lax.ppermute(x, AXES, pairs)  16.5 us
    all_to_all x1, starting transfers between devices, shards(): back = lax.all_to_all(mixed, CHIP, 0, 0, tiled=True)  9.94 us
    pallas_call x1, Pallas kernels, shards(): pl.pallas_call(gram_kernel, in_specs=[SMEM, HBM, HBM], out_specs=VMEM, ou...  3.15 us
  transfers between devices with their start and end apart: 17, of which 9 were waited for; matrix products, arithmetic and copies ran while one was open for 1% of the time, Pallas kernels for 5%

profile of v6, /device:TPU:2, one launch (start us, length us, event | category | flops | bytes accessed | tf_op | source)
XLA Modules:
  0.0 126.0 jit_solution(8283128520136904585)
XLA Ops:
  0.6 0.1 collective-permute-start
  0.7 0.5 collective-permute-start.1
  1.9 1.7 %shard_map.59 = (f32[128,128]{1,0:T(8,128)S(1)}, f32[32,16384]{1,0:T(8,128)S(1)}) custom-call(s32[1]{0:T(128)S(6)} %copy.7.counts_ref, s32[1,1024]{1,0:T(1,128)} %bitcast.15, f32[32,16384]{1,0:T(8,128)} %panel_hbm.1, s32[1,16384]{1,0:T(1,128)} %bitcast.14), custom_call_target="tpu_custom_call" | custom-call | tf_op jit(solution)/shard_map/pallas_call | solution.py:219
  3.6 1.2 collective-permute-start.2
  4.8 0.0 collective-permute-done.2
  4.8 1.2 collective-permute-start.3
  6.0 0.0 collective-permute-done.1
  6.0 0.0 collective-permute-done.refs_1_
  6.0 1.3 %shard_map.60 = f32[4224,128]{1,0:T(8,128)S(1)} custom-call(f32[32,16384]{1,0:T(8,128)S(1)} %get-tuple-element.10.refs_0_, f32[32,16384]{1,0:T(8,128)S(1)} %collective-permute-done.refs_1_, s32[1,16384]{1,0:T(1,128)S(1)} %bitcast.13, f32[128,128]{1,0:T(8,128)S(1)} %get-tuple-element.11.refs_3_), custom_call_target="tpu_custom_call" | custom-call | tf_op jit(solution)/shard_map/pallas_call | solution.py:236
  7.4 0.0 collective-permute-done.3
  7.4 50.1 %all_to_all.10 = f32[4224,1,128]{2,1,0:T(1,128)S(1)} all-to-all(f32[4224,1,128]{2,1,0:T(1,128)S(1)} %bitcast.11), channel_id=1, replica_groups=mesh['wide'=16,'high'=8,'core'=2] {'wide','high'}, dimensions={0} | all-to-all | bytes 4325376 | tf_op jit(solution)/shard_map/all_to_all | solution.py:244
  57.5 2.3 %shard_map.61 = (f32[128,32,128]{2,1,0:T(8,128)}, f32[128,128]{1,0:T(8,128)}) custom-call(f32[4224,128]{1,0:T(8,128)S(1)} %bitcast.12), custom_call_target="tpu_custom_call" | custom-call | tf_op jit(solution)/shard_map/pallas_call | solution.py:246
  59.8 9.9 %all-to-all-start.1 = ((f32[128,32,128]{2,1,0:T(8,128)}), f32[128,32,128]{2,1,0:T(8,128)S(1)}, u32[]{:S(2)}, u32[]{:S(2)}) async-start(f32[128,32,128]{2,1,0:T(8,128)} %get-tuple-element.14.y_hbm), calls=%async_computation.1 | async-start | bytes 4194304 | tf_op jit(solution)/shard_map/all_to_all | solution.py:259
  70.4 3.1 %shard_map.63 = f32[40,32]{1,0:T(8,128)S(1)} custom-call(s32[1]{0:T(128)S(6)} %select_n.28.counts_ref, f32[128,32,128]{2,1,0:T(8,128)} %get-tuple-element.14.y_hbm, f32[128,128]{1,0:T(8,128)} %get-tuple-element.15.mask_hbm), custom_call_target="tpu_custom_call" | custom-call | tf_op jit(solution)/shard_map/pallas_call | solution.py:261
  73.6 17.5 %collective-permute-start.4 = (f32[40,32]{1,0:T(8,128)S(1)}, f32[40,32]{1,0:T(8,128)S(1)}, u32[]{:S(2)}, u32[]{:S(2)}) collective-permute-start(f32[40,32]{1,0:T(8,128)S(1)} %shard_map.63), channel_id=1, source_target_pairs={{0,1},{1,0},{2,3},{3,2},{4,5},{5,4},{6,7},{7,6},{8,9},{9,8},{10,11... | collective-permute-start | bytes 15368 | tf_op jit(solution)/shard_map/ppermute | solution.py:179
  91.1 0.8 collective-permute-done.4
  91.9 1.5 %collective-permute-start.5 = (f32[40,32]{1,0:T(8,128)S(1)}, f32[40,32]{1,0:T(8,128)S(1)}, u32[]{:S(2)}, u32[]{:S(2)}) collective-permute-start(f32[40,32]{1,0:T(8,128)S(1)} %add.40), channel_id=1, source_target_pairs={{0,2},{1,3},{2,0},{3,1},{4,6},{5,7},{6,4},{7,5},{8,10},{9,11},{10,... | collective-permute-start | bytes 15368 | tf_op jit(solution)/shard_map/ppermute | solution.py:179
  93.4 2.7 %collective-permute-start.6 = (f32[40,32]{1,0:T(8,128)S(1)}, f32[40,32]{1,0:T(8,128)S(1)}, u32[]{:S(2)}, u32[]{:S(2)}) collective-permute-start(f32[40,32]{1,0:T(8,128)S(1)} %add.40), channel_id=1, source_target_pairs={{0,4},{1,5},{2,6},{3,7},{4,0},{5,1},{6,2},{7,3},{8,12},{9,13},{10,... | collective-permute-start | bytes 15368 | tf_op jit(solution)/shard_map/ppermute | solution.py:179
  96.1 0.6 collective-permute-start.7
  96.6 0.0 collective-permute-done.5
  96.6 2.1 %collective-permute-done.6 = f32[40,32]{1,0:T(8,128)S(1)} collective-permute-done((f32[40,32]{1,0:T(8,128)S(1)}, f32[40,32]{1,0:T(8,128)S(1)}, u32[]{:S(2)}, u32[]{:S(2)}) %collective-permute-start.6) | collective-permute-done | bytes 5152 | tf_op jit(solution)/shard_map/ppermute | solution.py:179
  98.7 2.5 %collective-permute-done.7 = f32[40,32]{1,0:T(8,128)S(1)} collective-permute-done((f32[40,32]{1,0:T(8,128)S(1)}, f32[40,32]{1,0:T(8,128)S(1)}, u32[]{:S(2)}, u32[]{:S(2)}) %collective-permute-start.7) | collective-permute-done | bytes 5152 | tf_op jit(solution)/shard_map/ppermute | solution.py:179
  101.2 1.7 %collective-permute-start.10 = (f32[40,32]{1,0:T(8,128)S(1)}, f32[40,32]{1,0:T(8,128)S(1)}, u32[]{:S(2)}, u32[]{:S(2)}) collective-permute-start(f32[40,32]{1,0:T(8,128)S(1)} %add_add_fusion.2), channel_id=1, source_target_pairs={{0,24},{1,25},{2,26},{3,27},{4,28},{5,29},{6,30},{7,31},{8,16},{9,... | collective-permute-start | bytes 15368 | tf_op jit(solution)/shard_map/ppermute | solution.py:179
  102.9 2.7 %collective-permute-start.8 = (f32[40,32]{1,0:T(8,128)S(1)}, f32[40,32]{1,0:T(8,128)S(1)}, u32[]{:S(2)}, u32[]{:S(2)}) collective-permute-start(f32[40,32]{1,0:T(8,128)S(1)} %add_add_fusion.2), channel_id=1, source_target_pairs={{0,16},{1,17},{2,18},{3,19},{4,20},{5,21},{6,22},{7,23},{8,24},{9,... | collective-permute-start | bytes 15368 | tf_op jit(solution)/shard_map/ppermute | solution.py:179
  105.6 0.0 collective-permute-start.9
  105.6 0.0 collective-permute-done.10
  105.6 1.8 %collective-permute-done.8 = f32[40,32]{1,0:T(8,128)S(1)} collective-permute-done((f32[40,32]{1,0:T(8,128)S(1)}, f32[40,32]{1,0:T(8,128)S(1)}, u32[]{:S(2)}, u32[]{:S(2)}) %collective-permute-start.8) | collective-permute-done | bytes 5152 | tf_op jit(solution)/shard_map/ppermute | solution.py:179
  107.4 4.0 %collective-permute-done.9 = f32[40,32]{1,0:T(8,128)S(1)} collective-permute-done((f32[40,32]{1,0:T(8,128)S(1)}, f32[40,32]{1,0:T(8,128)S(1)}, u32[]{:S(2)}, u32[]{:S(2)}) %collective-permute-start.9) | collective-permute-done | bytes 5152 | tf_op jit(solution)/shard_map/ppermute | solution.py:179
  111.5 0.7 collective-permute-start.11
  112.2 0.4 collective-permute-start.12
  112.6 2.8 %collective-permute-start.13 = (f32[40,32]{1,0:T(8,128)S(1)}, f32[40,32]{1,0:T(8,128)S(1)}, u32[]{:S(2)}, u32[]{:S(2)}) collective-permute-start(f32[40,32]{1,0:T(8,128)S(1)} %add_add_fusion.1), channel_id=1, source_target_pairs={{0,64},{1,193},{2,66},{3,195},{4,68},{5,197},{6,70},{7,199},{8,72}... | collective-permute-start | bytes 15368 | tf_op jit(solution)/shard_map/ppermute | solution.py:179
  115.4 1.3 %collective-permute-start.14 = (f32[40,32]{1,0:T(8,128)S(1)}, f32[40,32]{1,0:T(8,128)S(1)}, u32[]{:S(2)}, u32[]{:S(2)}) collective-permute-start(f32[40,32]{1,0:T(8,128)S(1)} %add_add_fusion.1), channel_id=1, source_target_pairs={{0,96},{1,225},{2,98},{3,227},{4,100},{5,229},{6,102},{7,231},{8,1... | collective-permute-start | bytes 15368 | tf_op jit(solution)/shard_map/ppermute | solution.py:179
  116.6 0.0 collective-permute-done.11
  116.6 0.2 collective-permute-done.12
  116.8 1.0 collective-permute-done.13
  117.8 3.3 %collective-permute-done.14 = f32[40,32]{1,0:T(8,128)S(1)} collective-permute-done((f32[40,32]{1,0:T(8,128)S(1)}, f32[40,32]{1,0:T(8,128)S(1)}, u32[]{:S(2)}, u32[]{:S(2)}) %collective-permute-start.14) | collective-permute-done | bytes 5152 | tf_op jit(solution)/shard_map/ppermute | solution.py:179
  121.0 1.7 %collective-permute-start.15 = (f32[40,32]{1,0:T(8,128)S(1)}, f32[40,32]{1,0:T(8,128)S(1)}, u32[]{:S(2)}, u32[]{:S(2)}) collective-permute-start(f32[40,32]{1,0:T(8,128)S(1)} %add_add_fusion), channel_id=1, source_target_pairs={{0,1},{1,0},{2,3},{3,2},{4,5},{5,4},{6,7},{7,6},{8,9},{9,8},{10,11... | collective-permute-start | bytes 15368 | tf_op jit(solution)/shard_map/ppermute | solution.py:179
  122.7 0.8 collective-permute-done.15
  123.6 0.6 slice_divide_fusion
  124.2 0.0 all-to-all-done.1.in_ref
  124.2 1.8 %shard_map.62 = f32[32,16384]{1,0:T(8,128)} custom-call(f32[128,32,128]{2,1,0:T(8,128)S(1)} %all-to-all-done.1.in_ref), custom_call_target="tpu_custom_call" | custom-call | tf_op jit(solution)/shard_map/pallas_call | solution.py:278
  (6 shorter events, 0.0 us)
Async XLA Ops:
  0.6 5.4 %collective-permute-start = (f32[32,16384]{1,0:T(8,128)}, f32[32,16384]{1,0:T(8,128)S(1)}, u32[]{:S(2)}, u32[]{:S(2)}) collective-permute-start(f32[32,16384]{1,0:T(8,128)} %panel_hbm.1), channel_id=1, source_target_pairs={{0,1},{1,0},{2,3},{3,2},{4,5},{5,4},{6,7},{7,6},{8,9},{9,8},{10,11... | collective-permute-start | bytes 6291464 | tf_op jit(solution)/shard_map/ppermute | solution.py:215
  0.7 5.3 %collective-permute-start.1 = (s32[16384]{0:T(1024)}, s32[16384]{0:T(1024)S(1)}, u32[]{:S(2)}, u32[]{:S(2)}) collective-permute-start(s32[16384]{0:T(1024)} %param.5), channel_id=1, source_target_pairs={{0,1},{1,0},{2,3},{3,2},{4,5},{5,4},{6,7},{7,6},{8,9},{9,8},{10,11... | collective-permute-start | bytes 196616 | tf_op jit(solution)/shard_map/ppermute | solution.py:216
  3.6 1.3 collective-permute-start.2
  4.8 2.6 %collective-permute-start.3 = (s32[1]{0:T(128)}, s32[1]{0:T(128)}, u32[]{:S(2)}, u32[]{:S(2)}) collective-permute-start(s32[1]{0:T(128)} %collective-permute-done.2), channel_id=1, source_target_pairs={{1,77},{3,79},{5,73},{7,75},{9,69},{11,71},{13,65},{15,67},{17,93}... | collective-permute-start | bytes 20 | tf_op jit(solution)/shard_map/ppermute | solution.py:179
  59.8 64.4 %all-to-all-start.1 = ((f32[128,32,128]{2,1,0:T(8,128)}), f32[128,32,128]{2,1,0:T(8,128)S(1)}, u32[]{:S(2)}, u32[]{:S(2)}) async-start(f32[128,32,128]{2,1,0:T(8,128)} %get-tuple-element.14.y_hbm), calls=%async_computation.1 | async-start | bytes 4194304 | tf_op jit(solution)/shard_map/all_to_all | solution.py:259
  73.6 18.3 %collective-permute-start.4 = (f32[40,32]{1,0:T(8,128)S(1)}, f32[40,32]{1,0:T(8,128)S(1)}, u32[]{:S(2)}, u32[]{:S(2)}) collective-permute-start(f32[40,32]{1,0:T(8,128)S(1)} %shard_map.63), channel_id=1, source_target_pairs={{0,1},{1,0},{2,3},{3,2},{4,5},{5,4},{6,7},{7,6},{8,9},{9,8},{10,11... | collective-permute-start | bytes 15368 | tf_op jit(solution)/shard_map/ppermute | solution.py:179
  91.9 4.7 %collective-permute-start.5 = (f32[40,32]{1,0:T(8,128)S(1)}, f32[40,32]{1,0:T(8,128)S(1)}, u32[]{:S(2)}, u32[]{:S(2)}) collective-permute-start(f32[40,32]{1,0:T(8,128)S(1)} %add.40), channel_id=1, source_target_pairs={{0,2},{1,3},{2,0},{3,1},{4,6},{5,7},{6,4},{7,5},{8,10},{9,11},{10,... | collective-permute-start | bytes 15368 | tf_op jit(solution)/shard_map/ppermute | solution.py:179
  93.4 5.3 %collective-permute-start.6 = (f32[40,32]{1,0:T(8,128)S(1)}, f32[40,32]{1,0:T(8,128)S(1)}, u32[]{:S(2)}, u32[]{:S(2)}) collective-permute-start(f32[40,32]{1,0:T(8,128)S(1)} %add.40), channel_id=1, source_target_pairs={{0,4},{1,5},{2,6},{3,7},{4,0},{5,1},{6,2},{7,3},{8,12},{9,13},{10,... | collective-permute-start | bytes 15368 | tf_op jit(solution)/shard_map/ppermute | solution.py:179
  96.1 5.1 %collective-permute-start.7 = (f32[40,32]{1,0:T(8,128)S(1)}, f32[40,32]{1,0:T(8,128)S(1)}, u32[]{:S(2)}, u32[]{:S(2)}) collective-permute-start(f32[40,32]{1,0:T(8,128)S(1)} %add.40), channel_id=1, source_target_pairs={{0,6},{1,7},{2,4},{3,5},{4,2},{5,3},{6,0},{7,1},{8,14},{9,15},{10,... | collective-permute-start | bytes 15368 | tf_op jit(solution)/shard_map/ppermute | solution.py:179
  101.2 4.4 %collective-permute-start.10 = (f32[40,32]{1,0:T(8,128)S(1)}, f32[40,32]{1,0:T(8,128)S(1)}, u32[]{:S(2)}, u32[]{:S(2)}) collective-permute-start(f32[40,32]{1,0:T(8,128)S(1)} %add_add_fusion.2), channel_id=1, source_target_pairs={{0,24},{1,25},{2,26},{3,27},{4,28},{5,29},{6,30},{7,31},{8,16},{9,... | collective-permute-start | bytes 15368 | tf_op jit(solution)/shard_map/ppermute | solution.py:179
  102.9 4.6 %collective-permute-start.8 = (f32[40,32]{1,0:T(8,128)S(1)}, f32[40,32]{1,0:T(8,128)S(1)}, u32[]{:S(2)}, u32[]{:S(2)}) collective-permute-start(f32[40,32]{1,0:T(8,128)S(1)} %add_add_fusion.2), channel_id=1, source_target_pairs={{0,16},{1,17},{2,18},{3,19},{4,20},{5,21},{6,22},{7,23},{8,24},{9,... | collective-permute-start | bytes 15368 | tf_op jit(solution)/shard_map/ppermute | solution.py:179
  105.6 5.9 %collective-permute-start.9 = (f32[40,32]{1,0:T(8,128)S(1)}, f32[40,32]{1,0:T(8,128)S(1)}, u32[]{:S(2)}, u32[]{:S(2)}) collective-permute-start(f32[40,32]{1,0:T(8,128)S(1)} %add_add_fusion.2), channel_id=1, source_target_pairs={{0,8},{1,9},{2,10},{3,11},{4,12},{5,13},{6,14},{7,15},{8,0},{9,1},... | collective-permute-start | bytes 15368 | tf_op jit(solution)/shard_map/ppermute | solution.py:179
  111.5 5.1 %collective-permute-start.11 = (f32[40,32]{1,0:T(8,128)S(1)}, f32[40,32]{1,0:T(8,128)S(1)}, u32[]{:S(2)}, u32[]{:S(2)}) collective-permute-start(f32[40,32]{1,0:T(8,128)S(1)} %add_add_fusion.1), channel_id=1, source_target_pairs={{1,129},{3,131},{5,133},{7,135},{9,137},{11,139},{13,141},{15,143}... | collective-permute-start | bytes 15368 | tf_op jit(solution)/shard_map/ppermute | solution.py:179
  112.2 4.6 %collective-permute-start.12 = (f32[40,32]{1,0:T(8,128)S(1)}, f32[40,32]{1,0:T(8,128)S(1)}, u32[]{:S(2)}, u32[]{:S(2)}) collective-permute-start(f32[40,32]{1,0:T(8,128)S(1)} %add_add_fusion.1), channel_id=1, source_target_pairs={{0,32},{1,161},{2,34},{3,163},{4,36},{5,165},{6,38},{7,167},{8,40}... | collective-permute-start | bytes 15368 | tf_op jit(solution)/shard_map/ppermute | solution.py:179
  112.6 5.2 %collective-permute-start.13 = (f32[40,32]{1,0:T(8,128)S(1)}, f32[40,32]{1,0:T(8,128)S(1)}, u32[]{:S(2)}, u32[]{:S(2)}) collective-permute-start(f32[40,32]{1,0:T(8,128)S(1)} %add_add_fusion.1), channel_id=1, source_target_pairs={{0,64},{1,193},{2,66},{3,195},{4,68},{5,197},{6,70},{7,199},{8,72}... | collective-permute-start | bytes 15368 | tf_op jit(solution)/shard_map/ppermute | solution.py:179
  115.4 5.7 %collective-permute-start.14 = (f32[40,32]{1,0:T(8,128)S(1)}, f32[40,32]{1,0:T(8,128)S(1)}, u32[]{:S(2)}, u32[]{:S(2)}) collective-permute-start(f32[40,32]{1,0:T(8,128)S(1)} %add_add_fusion.1), channel_id=1, source_target_pairs={{0,96},{1,225},{2,98},{3,227},{4,100},{5,229},{6,102},{7,231},{8,1... | collective-permute-start | bytes 15368 | tf_op jit(solution)/shard_map/ppermute | solution.py:179
  121.0 2.5 %collective-permute-start.15 = (f32[40,32]{1,0:T(8,128)S(1)}, f32[40,32]{1,0:T(8,128)S(1)}, u32[]{:S(2)}, u32[]{:S(2)}) collective-permute-start(f32[40,32]{1,0:T(8,128)S(1)} %add_add_fusion), channel_id=1, source_target_pairs={{0,1},{1,0},{2,3},{3,2},{4,5},{5,4},{6,7},{7,6},{8,9},{9,8},{10,11... | collective-permute-start | bytes 15368 | tf_op jit(solution)/shard_map/ppermute | solution.py:179

commit v7 on v6

--- a/solution.py
+++ b/solution.py
@@ -162,9 +162,18 @@
     out_ref[width:, :] = jnp.full((8, width), counts_ref[0].astype(jnp.float32))
 
 
-def unpack_kernel(in_ref, out_ref):
-    for t in range(in_ref.shape[0]):
-        out_ref[:, LANES * t : LANES * (t + 1)] = in_ref[t]
+def unpack_kernel(in_ref, out_hbm, keep_ref, sems):
+    chips = in_ref.shape[0]
+    pieces = sems.shape[0]
+    copies = []
+    for n in range(pieces):
+        for t in range(chips // pieces * n, chips // pieces * (n + 1)):
+            keep_ref[:, LANES * t : LANES * (t + 1)] = in_ref[t]
+        cols = pl.ds(LANES * (chips // pieces) * n, LANES * (chips // pieces))
+        copies.append(pltpu.make_async_copy(keep_ref.at[:, cols], out_hbm.at[:, cols], sems.at[n]))
+        copies[-1].start()
+    for copy in copies:
+        copy.wait()
 
 
 def send(x, move):
@@ -274,13 +283,12 @@
     total = total + send(total, lambda w, h, c: (w, h, c ^ 1))
     gram = total[:width] / total[width : width + 1]
 
-    pieces = 4
     out = pl.pallas_call(
         unpack_kernel,
-        grid=(pieces,),
-        in_specs=[pl.BlockSpec((chips // pieces, width, LANES), lambda s: (s, 0, 0))],
-        out_specs=pl.BlockSpec((width, length // pieces), lambda s: (0, s)),
-        out_shape=jax.ShapeDtypeStruct((width, length), f32),
+        in_specs=[VMEM],
+        out_specs=HBM,
+        out_shape=pltpu.HBM((width, length), f32),
+        scratch_shapes=[pltpu.VMEM((width, length), f32), pltpu.SemaphoreType.DMA((8,))],
         compiler_params=PARAMS,
     )(back)
     return out, gram

time: 128 us -> 127 us (level)
  no operation moved by 1% of the time
where the time goes in v7:
time: 127 us; the launch traced here: 126 us
  blocking collectives  50.1 us (39%)
  starting transfers between devices  46.5 us (37%)
  waiting for transfers between devices  16.5 us (13%)
  Pallas kernels  9.88 us (8%)
  between operations  2.16 us (2%)
    all_to_all x1, blocking collectives, shards(): lax.all_to_all(sent.reshape(message * chips, 1, LANES), CHIP, 0, 0, tiled...  50.1 us
    ppermute x14, starting transfers between devices, send(): return lax.ppermute(x, AXES, pairs)  35.9 us
    ppermute x14, waiting for transfers between devices, send(): return lax.ppermute(x, AXES, pairs)  16.5 us
    all_to_all x1, starting transfers between devices, shards(): back = lax.all_to_all(mixed, CHIP, 0, 0, tiled=True)  9.94 us
    pallas_call x1, Pallas kernels, shards(): pl.pallas_call(gram_kernel, in_specs=[SMEM, HBM, HBM], out_specs=VMEM, ou...  3.15 us
  transfers between devices with their start and end apart: 17, of which 9 were waited for; matrix products, arithmetic and copies ran while one was open for 1% of the time, Pallas kernels for 5%

profile of v7, /device:TPU:2, one launch (start us, length us, event | category | flops | bytes accessed | tf_op | source)
XLA Modules:
  0.0 125.8 jit_solution(10797973344744979511)
XLA Ops:
  0.6 0.1 collective-permute-start
  0.7 0.5 collective-permute-start.1
  1.9 1.7 %shard_map.59 = (f32[128,128]{1,0:T(8,128)S(1)}, f32[32,16384]{1,0:T(8,128)S(1)}) custom-call(s32[1]{0:T(128)S(6)} %copy.7.counts_ref, s32[1,1024]{1,0:T(1,128)} %bitcast.15, f32[32,16384]{1,0:T(8,128)} %panel_hbm.1, s32[1,16384]{1,0:T(1,128)} %bitcast.14), custom_call_target="tpu_custom_call" | custom-call | tf_op jit(solution)/shard_map/pallas_call | solution.py:228
  3.6 1.2 collective-permute-start.2
  4.8 0.0 collective-permute-done.2
  4.8 1.2 collective-permute-start.3
  6.0 0.0 collective-permute-done.1
  6.0 0.0 collective-permute-done.refs_1_
  6.0 1.3 %shard_map.60 = f32[4224,128]{1,0:T(8,128)S(1)} custom-call(f32[32,16384]{1,0:T(8,128)S(1)} %get-tuple-element.10.refs_0_, f32[32,16384]{1,0:T(8,128)S(1)} %collective-permute-done.refs_1_, s32[1,16384]{1,0:T(1,128)S(1)} %bitcast.13, f32[128,128]{1,0:T(8,128)S(1)} %get-tuple-element.11.refs_3_), custom_call_target="tpu_custom_call" | custom-call | tf_op jit(solution)/shard_map/pallas_call | solution.py:245
  7.4 0.0 collective-permute-done.3
  7.4 50.1 %all_to_all.10 = f32[4224,1,128]{2,1,0:T(1,128)S(1)} all-to-all(f32[4224,1,128]{2,1,0:T(1,128)S(1)} %bitcast.11), channel_id=1, replica_groups=mesh['wide'=16,'high'=8,'core'=2] {'wide','high'}, dimensions={0} | all-to-all | bytes 4325376 | tf_op jit(solution)/shard_map/all_to_all | solution.py:253
  57.5 2.3 %shard_map.61 = (f32[128,32,128]{2,1,0:T(8,128)}, f32[128,128]{1,0:T(8,128)}) custom-call(f32[4224,128]{1,0:T(8,128)S(1)} %bitcast.12), custom_call_target="tpu_custom_call" | custom-call | tf_op jit(solution)/shard_map/pallas_call | solution.py:255
  59.8 9.9 %all-to-all-start.1 = ((f32[128,32,128]{2,1,0:T(8,128)}), f32[128,32,128]{2,1,0:T(8,128)S(1)}, u32[]{:S(2)}, u32[]{:S(2)}) async-start(f32[128,32,128]{2,1,0:T(8,128)} %get-tuple-element.14.y_hbm), calls=%async_computation.1 | async-start | bytes 4194304 | tf_op jit(solution)/shard_map/all_to_all | solution.py:268
  70.4 3.1 %shard_map.63 = f32[40,32]{1,0:T(8,128)S(1)} custom-call(s32[1]{0:T(128)S(6)} %select_n.28.counts_ref, f32[128,32,128]{2,1,0:T(8,128)} %get-tuple-element.14.y_hbm, f32[128,128]{1,0:T(8,128)} %get-tuple-element.15.mask_hbm), custom_call_target="tpu_custom_call" | custom-call | tf_op jit(solution)/shard_map/pallas_call | solution.py:270
  73.6 17.5 %collective-permute-start.4 = (f32[40,32]{1,0:T(8,128)S(1)}, f32[40,32]{1,0:T(8,128)S(1)}, u32[]{:S(2)}, u32[]{:S(2)}) collective-permute-start(f32[40,32]{1,0:T(8,128)S(1)} %shard_map.63), channel_id=1, source_target_pairs={{0,1},{1,0},{2,3},{3,2},{4,5},{5,4},{6,7},{7,6},{8,9},{9,8},{10,11... | collective-permute-start | bytes 15368 | tf_op jit(solution)/shard_map/ppermute | solution.py:188
  91.1 0.8 collective-permute-done.4
  91.9 1.5 %collective-permute-start.5 = (f32[40,32]{1,0:T(8,128)S(1)}, f32[40,32]{1,0:T(8,128)S(1)}, u32[]{:S(2)}, u32[]{:S(2)}) collective-permute-start(f32[40,32]{1,0:T(8,128)S(1)} %add.40), channel_id=1, source_target_pairs={{0,2},{1,3},{2,0},{3,1},{4,6},{5,7},{6,4},{7,5},{8,10},{9,11},{10,... | collective-permute-start | bytes 15368 | tf_op jit(solution)/shard_map/ppermute | solution.py:188
  93.4 2.7 %collective-permute-start.6 = (f32[40,32]{1,0:T(8,128)S(1)}, f32[40,32]{1,0:T(8,128)S(1)}, u32[]{:S(2)}, u32[]{:S(2)}) collective-permute-start(f32[40,32]{1,0:T(8,128)S(1)} %add.40), channel_id=1, source_target_pairs={{0,4},{1,5},{2,6},{3,7},{4,0},{5,1},{6,2},{7,3},{8,12},{9,13},{10,... | collective-permute-start | bytes 15368 | tf_op jit(solution)/shard_map/ppermute | solution.py:188
  96.1 0.6 collective-permute-start.7
  96.6 0.0 collective-permute-done.5
  96.6 2.1 %collective-permute-done.6 = f32[40,32]{1,0:T(8,128)S(1)} collective-permute-done((f32[40,32]{1,0:T(8,128)S(1)}, f32[40,32]{1,0:T(8,128)S(1)}, u32[]{:S(2)}, u32[]{:S(2)}) %collective-permute-start.6) | collective-permute-done | bytes 5152 | tf_op jit(solution)/shard_map/ppermute | solution.py:188
  98.7 2.5 %collective-permute-done.7 = f32[40,32]{1,0:T(8,128)S(1)} collective-permute-done((f32[40,32]{1,0:T(8,128)S(1)}, f32[40,32]{1,0:T(8,128)S(1)}, u32[]{:S(2)}, u32[]{:S(2)}) %collective-permute-start.7) | collective-permute-done | bytes 5152 | tf_op jit(solution)/shard_map/ppermute | solution.py:188
  101.2 1.7 %collective-permute-start.10 = (f32[40,32]{1,0:T(8,128)S(1)}, f32[40,32]{1,0:T(8,128)S(1)}, u32[]{:S(2)}, u32[]{:S(2)}) collective-permute-start(f32[40,32]{1,0:T(8,128)S(1)} %add_add_fusion.2), channel_id=1, source_target_pairs={{0,24},{1,25},{2,26},{3,27},{4,28},{5,29},{6,30},{7,31},{8,16},{9,... | collective-permute-start | bytes 15368 | tf_op jit(solution)/shard_map/ppermute | solution.py:188
  102.9 2.7 %collective-permute-start.8 = (f32[40,32]{1,0:T(8,128)S(1)}, f32[40,32]{1,0:T(8,128)S(1)}, u32[]{:S(2)}, u32[]{:S(2)}) collective-permute-start(f32[40,32]{1,0:T(8,128)S(1)} %add_add_fusion.2), channel_id=1, source_target_pairs={{0,16},{1,17},{2,18},{3,19},{4,20},{5,21},{6,22},{7,23},{8,24},{9,... | collective-permute-start | bytes 15368 | tf_op jit(solution)/shard_map/ppermute | solution.py:188
  105.6 0.0 collective-permute-start.9
  105.6 0.0 collective-permute-done.10
  105.6 1.8 %collective-permute-done.8 = f32[40,32]{1,0:T(8,128)S(1)} collective-permute-done((f32[40,32]{1,0:T(8,128)S(1)}, f32[40,32]{1,0:T(8,128)S(1)}, u32[]{:S(2)}, u32[]{:S(2)}) %collective-permute-start.8) | collective-permute-done | bytes 5152 | tf_op jit(solution)/shard_map/ppermute | solution.py:188
  107.4 4.0 %collective-permute-done.9 = f32[40,32]{1,0:T(8,128)S(1)} collective-permute-done((f32[40,32]{1,0:T(8,128)S(1)}, f32[40,32]{1,0:T(8,128)S(1)}, u32[]{:S(2)}, u32[]{:S(2)}) %collective-permute-start.9) | collective-permute-done | bytes 5152 | tf_op jit(solution)/shard_map/ppermute | solution.py:188
  111.5 0.7 collective-permute-start.11
  112.2 0.4 collective-permute-start.12
  112.6 2.8 %collective-permute-start.13 = (f32[40,32]{1,0:T(8,128)S(1)}, f32[40,32]{1,0:T(8,128)S(1)}, u32[]{:S(2)}, u32[]{:S(2)}) collective-permute-start(f32[40,32]{1,0:T(8,128)S(1)} %add_add_fusion.1), channel_id=1, source_target_pairs={{0,64},{1,193},{2,66},{3,195},{4,68},{5,197},{6,70},{7,199},{8,72}... | collective-permute-start | bytes 15368 | tf_op jit(solution)/shard_map/ppermute | solution.py:188
  115.4 1.3 %collective-permute-start.14 = (f32[40,32]{1,0:T(8,128)S(1)}, f32[40,32]{1,0:T(8,128)S(1)}, u32[]{:S(2)}, u32[]{:S(2)}) collective-permute-start(f32[40,32]{1,0:T(8,128)S(1)} %add_add_fusion.1), channel_id=1, source_target_pairs={{0,96},{1,225},{2,98},{3,227},{4,100},{5,229},{6,102},{7,231},{8,1... | collective-permute-start | bytes 15368 | tf_op jit(solution)/shard_map/ppermute | solution.py:188
  116.6 0.0 collective-permute-done.11
  116.6 0.2 collective-permute-done.12
  116.8 1.0 collective-permute-done.13
  117.8 3.3 %collective-permute-done.14 = f32[40,32]{1,0:T(8,128)S(1)} collective-permute-done((f32[40,32]{1,0:T(8,128)S(1)}, f32[40,32]{1,0:T(8,128)S(1)}, u32[]{:S(2)}, u32[]{:S(2)}) %collective-permute-start.14) | collective-permute-done | bytes 5152 | tf_op jit(solution)/shard_map/ppermute | solution.py:188
  121.0 1.7 %collective-permute-start.15 = (f32[40,32]{1,0:T(8,128)S(1)}, f32[40,32]{1,0:T(8,128)S(1)}, u32[]{:S(2)}, u32[]{:S(2)}) collective-permute-start(f32[40,32]{1,0:T(8,128)S(1)} %add_add_fusion), channel_id=1, source_target_pairs={{0,1},{1,0},{2,3},{3,2},{4,5},{5,4},{6,7},{7,6},{8,9},{9,8},{10,11... | collective-permute-start | bytes 15368 | tf_op jit(solution)/shard_map/ppermute | solution.py:188
  122.7 0.8 collective-permute-done.15
  123.6 0.6 slice_divide_fusion
  124.2 0.0 all-to-all-done.1.in_ref
  124.2 1.4 %shard_map.62 = f32[32,16384]{1,0:T(8,128)} custom-call(f32[128,32,128]{2,1,0:T(8,128)S(1)} %all-to-all-done.1.in_ref), custom_call_target="tpu_custom_call" | custom-call | tf_op jit(solution)/shard_map/pallas_call | solution.py:286
  (6 shorter events, 0.0 us)
Async XLA Ops:
  0.6 5.4 %collective-permute-start = (f32[32,16384]{1,0:T(8,128)}, f32[32,16384]{1,0:T(8,128)S(1)}, u32[]{:S(2)}, u32[]{:S(2)}) collective-permute-start(f32[32,16384]{1,0:T(8,128)} %panel_hbm.1), channel_id=1, source_target_pairs={{0,1},{1,0},{2,3},{3,2},{4,5},{5,4},{6,7},{7,6},{8,9},{9,8},{10,11... | collective-permute-start | bytes 6291464 | tf_op jit(solution)/shard_map/ppermute | solution.py:224
  0.7 5.3 %collective-permute-start.1 = (s32[16384]{0:T(1024)}, s32[16384]{0:T(1024)S(1)}, u32[]{:S(2)}, u32[]{:S(2)}) collective-permute-start(s32[16384]{0:T(1024)} %param.5), channel_id=1, source_target_pairs={{0,1},{1,0},{2,3},{3,2},{4,5},{5,4},{6,7},{7,6},{8,9},{9,8},{10,11... | collective-permute-start | bytes 196616 | tf_op jit(solution)/shard_map/ppermute | solution.py:225
  3.6 1.3 collective-permute-start.2
  4.8 2.6 %collective-permute-start.3 = (s32[1]{0:T(128)}, s32[1]{0:T(128)}, u32[]{:S(2)}, u32[]{:S(2)}) collective-permute-start(s32[1]{0:T(128)} %collective-permute-done.2), channel_id=1, source_target_pairs={{1,77},{3,79},{5,73},{7,75},{9,69},{11,71},{13,65},{15,67},{17,93}... | collective-permute-start | bytes 20 | tf_op jit(solution)/shard_map/ppermute | solution.py:188
  59.8 64.4 %all-to-all-start.1 = ((f32[128,32,128]{2,1,0:T(8,128)}), f32[128,32,128]{2,1,0:T(8,128)S(1)}, u32[]{:S(2)}, u32[]{:S(2)}) async-start(f32[128,32,128]{2,1,0:T(8,128)} %get-tuple-element.14.y_hbm), calls=%async_computation.1 | async-start | bytes 4194304 | tf_op jit(solution)/shard_map/all_to_all | solution.py:268
  73.6 18.3 %collective-permute-start.4 = (f32[40,32]{1,0:T(8,128)S(1)}, f32[40,32]{1,0:T(8,128)S(1)}, u32[]{:S(2)}, u32[]{:S(2)}) collective-permute-start(f32[40,32]{1,0:T(8,128)S(1)} %shard_map.63), channel_id=1, source_target_pairs={{0,1},{1,0},{2,3},{3,2},{4,5},{5,4},{6,7},{7,6},{8,9},{9,8},{10,11... | collective-permute-start | bytes 15368 | tf_op jit(solution)/shard_map/ppermute | solution.py:188
  91.9 4.7 %collective-permute-start.5 = (f32[40,32]{1,0:T(8,128)S(1)}, f32[40,32]{1,0:T(8,128)S(1)}, u32[]{:S(2)}, u32[]{:S(2)}) collective-permute-start(f32[40,32]{1,0:T(8,128)S(1)} %add.40), channel_id=1, source_target_pairs={{0,2},{1,3},{2,0},{3,1},{4,6},{5,7},{6,4},{7,5},{8,10},{9,11},{10,... | collective-permute-start | bytes 15368 | tf_op jit(solution)/shard_map/ppermute | solution.py:188
  93.4 5.3 %collective-permute-start.6 = (f32[40,32]{1,0:T(8,128)S(1)}, f32[40,32]{1,0:T(8,128)S(1)}, u32[]{:S(2)}, u32[]{:S(2)}) collective-permute-start(f32[40,32]{1,0:T(8,128)S(1)} %add.40), channel_id=1, source_target_pairs={{0,4},{1,5},{2,6},{3,7},{4,0},{5,1},{6,2},{7,3},{8,12},{9,13},{10,... | collective-permute-start | bytes 15368 | tf_op jit(solution)/shard_map/ppermute | solution.py:188
  96.1 5.1 %collective-permute-start.7 = (f32[40,32]{1,0:T(8,128)S(1)}, f32[40,32]{1,0:T(8,128)S(1)}, u32[]{:S(2)}, u32[]{:S(2)}) collective-permute-start(f32[40,32]{1,0:T(8,128)S(1)} %add.40), channel_id=1, source_target_pairs={{0,6},{1,7},{2,4},{3,5},{4,2},{5,3},{6,0},{7,1},{8,14},{9,15},{10,... | collective-permute-start | bytes 15368 | tf_op jit(solution)/shard_map/ppermute | solution.py:188
  101.2 4.4 %collective-permute-start.10 = (f32[40,32]{1,0:T(8,128)S(1)}, f32[40,32]{1,0:T(8,128)S(1)}, u32[]{:S(2)}, u32[]{:S(2)}) collective-permute-start(f32[40,32]{1,0:T(8,128)S(1)} %add_add_fusion.2), channel_id=1, source_target_pairs={{0,24},{1,25},{2,26},{3,27},{4,28},{5,29},{6,30},{7,31},{8,16},{9,... | collective-permute-start | bytes 15368 | tf_op jit(solution)/shard_map/ppermute | solution.py:188
  102.9 4.6 %collective-permute-start.8 = (f32[40,32]{1,0:T(8,128)S(1)}, f32[40,32]{1,0:T(8,128)S(1)}, u32[]{:S(2)}, u32[]{:S(2)}) collective-permute-start(f32[40,32]{1,0:T(8,128)S(1)} %add_add_fusion.2), channel_id=1, source_target_pairs={{0,16},{1,17},{2,18},{3,19},{4,20},{5,21},{6,22},{7,23},{8,24},{9,... | collective-permute-start | bytes 15368 | tf_op jit(solution)/shard_map/ppermute | solution.py:188
  105.6 5.9 %collective-permute-start.9 = (f32[40,32]{1,0:T(8,128)S(1)}, f32[40,32]{1,0:T(8,128)S(1)}, u32[]{:S(2)}, u32[]{:S(2)}) collective-permute-start(f32[40,32]{1,0:T(8,128)S(1)} %add_add_fusion.2), channel_id=1, source_target_pairs={{0,8},{1,9},{2,10},{3,11},{4,12},{5,13},{6,14},{7,15},{8,0},{9,1},... | collective-permute-start | bytes 15368 | tf_op jit(solution)/shard_map/ppermute | solution.py:188
  111.5 5.1 %collective-permute-start.11 = (f32[40,32]{1,0:T(8,128)S(1)}, f32[40,32]{1,0:T(8,128)S(1)}, u32[]{:S(2)}, u32[]{:S(2)}) collective-permute-start(f32[40,32]{1,0:T(8,128)S(1)} %add_add_fusion.1), channel_id=1, source_target_pairs={{1,129},{3,131},{5,133},{7,135},{9,137},{11,139},{13,141},{15,143}... | collective-permute-start | bytes 15368 | tf_op jit(solution)/shard_map/ppermute | solution.py:188
  112.2 4.6 %collective-permute-start.12 = (f32[40,32]{1,0:T(8,128)S(1)}, f32[40,32]{1,0:T(8,128)S(1)}, u32[]{:S(2)}, u32[]{:S(2)}) collective-permute-start(f32[40,32]{1,0:T(8,128)S(1)} %add_add_fusion.1), channel_id=1, source_target_pairs={{0,32},{1,161},{2,34},{3,163},{4,36},{5,165},{6,38},{7,167},{8,40}... | collective-permute-start | bytes 15368 | tf_op jit(solution)/shard_map/ppermute | solution.py:188
  112.6 5.2 %collective-permute-start.13 = (f32[40,32]{1,0:T(8,128)S(1)}, f32[40,32]{1,0:T(8,128)S(1)}, u32[]{:S(2)}, u32[]{:S(2)}) collective-permute-start(f32[40,32]{1,0:T(8,128)S(1)} %add_add_fusion.1), channel_id=1, source_target_pairs={{0,64},{1,193},{2,66},{3,195},{4,68},{5,197},{6,70},{7,199},{8,72}... | collective-permute-start | bytes 15368 | tf_op jit(solution)/shard_map/ppermute | solution.py:188
  115.4 5.7 %collective-permute-start.14 = (f32[40,32]{1,0:T(8,128)S(1)}, f32[40,32]{1,0:T(8,128)S(1)}, u32[]{:S(2)}, u32[]{:S(2)}) collective-permute-start(f32[40,32]{1,0:T(8,128)S(1)} %add_add_fusion.1), channel_id=1, source_target_pairs={{0,96},{1,225},{2,98},{3,227},{4,100},{5,229},{6,102},{7,231},{8,1... | collective-permute-start | bytes 15368 | tf_op jit(solution)/shard_map/ppermute | solution.py:188
  121.0 2.5 %collective-permute-start.15 = (f32[40,32]{1,0:T(8,128)S(1)}, f32[40,32]{1,0:T(8,128)S(1)}, u32[]{:S(2)}, u32[]{:S(2)}) collective-permute-start(f32[40,32]{1,0:T(8,128)S(1)} %add_add_fusion), channel_id=1, source_target_pairs={{0,1},{1,0},{2,3},{3,2},{4,5},{5,4},{6,7},{7,6},{8,9},{9,8},{10,11... | collective-permute-start | bytes 15368 | tf_op jit(solution)/shard_map/ppermute | solution.py:188

commit v8 on v7

--- a/solution.py
+++ b/solution.py
@@ -116,9 +116,7 @@
     i = lax.broadcasted_iota(jnp.int32, (chips, 2 * chips), 0)
     j = lax.broadcasted_iota(jnp.int32, (chips, 2 * chips), 1)
     table = signs_of(i, jnp.where(j < chips, j, j - chips), chips).astype(jnp.bfloat16)
-    mask_ref[...] = in_ref[pl.ds(width, chips, stride=width + 1), :]
-    copies = [pltpu.make_async_copy(mask_ref, mask_hbm, sems.at[width // 8])]
-    copies[0].start()
+    copies = []
     tiles = keep_ref.reshape(chips, width, LANES)
     for part in range(width // 8):
         for k in range(8 * part, 8 * part + 8, 2):
@@ -131,6 +129,9 @@
         rows = pl.ds(8 * part, 8)
         copies.append(pltpu.make_async_copy(tiles.at[:, rows, :], out_hbm.at[:, rows, :], sems.at[part]))
         copies[-1].start()
+    mask_ref[...] = in_ref[pl.ds(width, chips, stride=width + 1), :]
+    copies.append(pltpu.make_async_copy(mask_ref, mask_hbm, sems.at[width // 8]))
+    copies[-1].start()
     for copy in copies:
         copy.wait()
 

time: 127 us -> 127 us (level)
  no operation moved by 1% of the time
where the time goes in v8:
time: 127 us; the launch traced here: 126 us
  blocking collectives  50.1 us (39%)
  starting transfers between devices  46.4 us (37%)
  waiting for transfers between devices  16.6 us (13%)
  Pallas kernels  9.96 us (8%)
  between operations  2.16 us (2%)
    all_to_all x1, blocking collectives, shards(): lax.all_to_all(sent.reshape(message * chips, 1, LANES), CHIP, 0, 0, tiled...  50.1 us
    ppermute x14, starting transfers between devices, send(): return lax.ppermute(x, AXES, pairs)  35.9 us
    ppermute x14, waiting for transfers between devices, send(): return lax.ppermute(x, AXES, pairs)  16.6 us
    all_to_all x1, starting transfers between devices, shards(): back = lax.all_to_all(mixed, CHIP, 0, 0, tiled=True)  9.95 us
    pallas_call x1, Pallas kernels, shards(): pl.pallas_call(gram_kernel, in_specs=[SMEM, HBM, HBM], out_specs=VMEM, ou...  3.15 us
  transfers between devices with their start and end apart: 17, of which 9 were waited for; matrix products, arithmetic and copies ran while one was open for 1% of the time, Pallas kernels for 5%

profile of v8, /device:TPU:2, one launch (start us, length us, event | category | flops | bytes accessed | tf_op | source)
XLA Modules:
  0.0 125.9 jit_solution(10003118928715614360)
XLA Ops:
  0.6 0.1 collective-permute-start
  0.7 0.5 collective-permute-start.1
  1.9 1.7 %shard_map.59 = (f32[128,128]{1,0:T(8,128)S(1)}, f32[32,16384]{1,0:T(8,128)S(1)}) custom-call(s32[1]{0:T(128)S(6)} %copy.7.counts_ref, s32[1,1024]{1,0:T(1,128)} %bitcast.15, f32[32,16384]{1,0:T(8,128)} %panel_hbm.1, s32[1,16384]{1,0:T(1,128)} %bitcast.14), custom_call_target="tpu_custom_call" | custom-call | tf_op jit(solution)/shard_map/pallas_call | solution.py:229
  3.6 1.2 collective-permute-start.2
  4.8 0.0 collective-permute-done.2
  4.8 1.2 collective-permute-start.3
  6.0 0.0 collective-permute-done.1
  6.0 0.0 collective-permute-done.refs_1_
  6.0 1.3 %shard_map.60 = f32[4224,128]{1,0:T(8,128)S(1)} custom-call(f32[32,16384]{1,0:T(8,128)S(1)} %get-tuple-element.10.refs_0_, f32[32,16384]{1,0:T(8,128)S(1)} %collective-permute-done.refs_1_, s32[1,16384]{1,0:T(1,128)S(1)} %bitcast.13, f32[128,128]{1,0:T(8,128)S(1)} %get-tuple-element.11.refs_3_), custom_call_target="tpu_custom_call" | custom-call | tf_op jit(solution)/shard_map/pallas_call | solution.py:246
  7.4 0.0 collective-permute-done.3
  7.4 50.1 %all_to_all.10 = f32[4224,1,128]{2,1,0:T(1,128)S(1)} all-to-all(f32[4224,1,128]{2,1,0:T(1,128)S(1)} %bitcast.11), channel_id=1, replica_groups=mesh['wide'=16,'high'=8,'core'=2] {'wide','high'}, dimensions={0} | all-to-all | bytes 4325376 | tf_op jit(solution)/shard_map/all_to_all | solution.py:254
  57.5 2.4 %shard_map.61 = (f32[128,32,128]{2,1,0:T(8,128)}, f32[128,128]{1,0:T(8,128)}) custom-call(f32[4224,128]{1,0:T(8,128)S(1)} %bitcast.12), custom_call_target="tpu_custom_call" | custom-call | tf_op jit(solution)/shard_map/pallas_call | solution.py:256
  59.9 9.9 %all-to-all-start.1 = ((f32[128,32,128]{2,1,0:T(8,128)}), f32[128,32,128]{2,1,0:T(8,128)S(1)}, u32[]{:S(2)}, u32[]{:S(2)}) async-start(f32[128,32,128]{2,1,0:T(8,128)} %get-tuple-element.14.y_hbm), calls=%async_computation.1 | async-start | bytes 4194304 | tf_op jit(solution)/shard_map/all_to_all | solution.py:269
  70.5 3.1 %shard_map.63 = f32[40,32]{1,0:T(8,128)S(1)} custom-call(s32[1]{0:T(128)S(6)} %select_n.28.counts_ref, f32[128,32,128]{2,1,0:T(8,128)} %get-tuple-element.14.y_hbm, f32[128,128]{1,0:T(8,128)} %get-tuple-element.15.mask_hbm), custom_call_target="tpu_custom_call" | custom-call | tf_op jit(solution)/shard_map/pallas_call | solution.py:271
  73.7 17.5 %collective-permute-start.4 = (f32[40,32]{1,0:T(8,128)S(1)}, f32[40,32]{1,0:T(8,128)S(1)}, u32[]{:S(2)}, u32[]{:S(2)}) collective-permute-start(f32[40,32]{1,0:T(8,128)S(1)} %shard_map.63), channel_id=1, source_target_pairs={{0,1},{1,0},{2,3},{3,2},{4,5},{5,4},{6,7},{7,6},{8,9},{9,8},{10,11... | collective-permute-start | bytes 15368 | tf_op jit(solution)/shard_map/ppermute | solution.py:189
  91.2 0.8 collective-permute-done.4
  92.0 1.5 %collective-permute-start.5 = (f32[40,32]{1,0:T(8,128)S(1)}, f32[40,32]{1,0:T(8,128)S(1)}, u32[]{:S(2)}, u32[]{:S(2)}) collective-permute-start(f32[40,32]{1,0:T(8,128)S(1)} %add.40), channel_id=1, source_target_pairs={{0,2},{1,3},{2,0},{3,1},{4,6},{5,7},{6,4},{7,5},{8,10},{9,11},{10,... | collective-permute-start | bytes 15368 | tf_op jit(solution)/shard_map/ppermute | solution.py:189
  93.5 2.7 %collective-permute-start.6 = (f32[40,32]{1,0:T(8,128)S(1)}, f32[40,32]{1,0:T(8,128)S(1)}, u32[]{:S(2)}, u32[]{:S(2)}) collective-permute-start(f32[40,32]{1,0:T(8,128)S(1)} %add.40), channel_id=1, source_target_pairs={{0,4},{1,5},{2,6},{3,7},{4,0},{5,1},{6,2},{7,3},{8,12},{9,13},{10,... | collective-permute-start | bytes 15368 | tf_op jit(solution)/shard_map/ppermute | solution.py:189
  96.2 0.6 collective-permute-start.7
  96.7 0.0 collective-permute-done.5
  96.7 2.1 %collective-permute-done.6 = f32[40,32]{1,0:T(8,128)S(1)} collective-permute-done((f32[40,32]{1,0:T(8,128)S(1)}, f32[40,32]{1,0:T(8,128)S(1)}, u32[]{:S(2)}, u32[]{:S(2)}) %collective-permute-start.6) | collective-permute-done | bytes 5152 | tf_op jit(solution)/shard_map/ppermute | solution.py:189
  98.8 2.5 %collective-permute-done.7 = f32[40,32]{1,0:T(8,128)S(1)} collective-permute-done((f32[40,32]{1,0:T(8,128)S(1)}, f32[40,32]{1,0:T(8,128)S(1)}, u32[]{:S(2)}, u32[]{:S(2)}) %collective-permute-start.7) | collective-permute-done | bytes 5152 | tf_op jit(solution)/shard_map/ppermute | solution.py:189
  101.3 1.7 %collective-permute-start.10 = (f32[40,32]{1,0:T(8,128)S(1)}, f32[40,32]{1,0:T(8,128)S(1)}, u32[]{:S(2)}, u32[]{:S(2)}) collective-permute-start(f32[40,32]{1,0:T(8,128)S(1)} %add_add_fusion.2), channel_id=1, source_target_pairs={{0,24},{1,25},{2,26},{3,27},{4,28},{5,29},{6,30},{7,31},{8,16},{9,... | collective-permute-start | bytes 15368 | tf_op jit(solution)/shard_map/ppermute | solution.py:189
  103.1 2.6 %collective-permute-start.8 = (f32[40,32]{1,0:T(8,128)S(1)}, f32[40,32]{1,0:T(8,128)S(1)}, u32[]{:S(2)}, u32[]{:S(2)}) collective-permute-start(f32[40,32]{1,0:T(8,128)S(1)} %add_add_fusion.2), channel_id=1, source_target_pairs={{0,16},{1,17},{2,18},{3,19},{4,20},{5,21},{6,22},{7,23},{8,24},{9,... | collective-permute-start | bytes 15368 | tf_op jit(solution)/shard_map/ppermute | solution.py:189
  105.6 0.0 collective-permute-start.9
  105.7 0.0 collective-permute-done.10
  105.7 1.8 %collective-permute-done.8 = f32[40,32]{1,0:T(8,128)S(1)} collective-permute-done((f32[40,32]{1,0:T(8,128)S(1)}, f32[40,32]{1,0:T(8,128)S(1)}, u32[]{:S(2)}, u32[]{:S(2)}) %collective-permute-start.8) | collective-permute-done | bytes 5152 | tf_op jit(solution)/shard_map/ppermute | solution.py:189
  107.5 4.0 %collective-permute-done.9 = f32[40,32]{1,0:T(8,128)S(1)} collective-permute-done((f32[40,32]{1,0:T(8,128)S(1)}, f32[40,32]{1,0:T(8,128)S(1)}, u32[]{:S(2)}, u32[]{:S(2)}) %collective-permute-start.9) | collective-permute-done | bytes 5152 | tf_op jit(solution)/shard_map/ppermute | solution.py:189
  111.5 0.7 collective-permute-start.11
  112.1 0.5 collective-permute-start.12
  112.6 2.6 %collective-permute-start.13 = (f32[40,32]{1,0:T(8,128)S(1)}, f32[40,32]{1,0:T(8,128)S(1)}, u32[]{:S(2)}, u32[]{:S(2)}) collective-permute-start(f32[40,32]{1,0:T(8,128)S(1)} %add_add_fusion.1), channel_id=1, source_target_pairs={{0,64},{1,193},{2,66},{3,195},{4,68},{5,197},{6,70},{7,199},{8,72}... | collective-permute-start | bytes 15368 | tf_op jit(solution)/shard_map/ppermute | solution.py:189
  115.2 1.4 %collective-permute-start.14 = (f32[40,32]{1,0:T(8,128)S(1)}, f32[40,32]{1,0:T(8,128)S(1)}, u32[]{:S(2)}, u32[]{:S(2)}) collective-permute-start(f32[40,32]{1,0:T(8,128)S(1)} %add_add_fusion.1), channel_id=1, source_target_pairs={{0,96},{1,225},{2,98},{3,227},{4,100},{5,229},{6,102},{7,231},{8,1... | collective-permute-start | bytes 15368 | tf_op jit(solution)/shard_map/ppermute | solution.py:189
  116.6 0.0 collective-permute-done.11
  116.6 0.3 collective-permute-done.12
  116.9 0.9 collective-permute-done.13
  117.8 3.3 %collective-permute-done.14 = f32[40,32]{1,0:T(8,128)S(1)} collective-permute-done((f32[40,32]{1,0:T(8,128)S(1)}, f32[40,32]{1,0:T(8,128)S(1)}, u32[]{:S(2)}, u32[]{:S(2)}) %collective-permute-start.14) | collective-permute-done | bytes 5152 | tf_op jit(solution)/shard_map/ppermute | solution.py:189
  121.1 1.7 %collective-permute-start.15 = (f32[40,32]{1,0:T(8,128)S(1)}, f32[40,32]{1,0:T(8,128)S(1)}, u32[]{:S(2)}, u32[]{:S(2)}) collective-permute-start(f32[40,32]{1,0:T(8,128)S(1)} %add_add_fusion), channel_id=1, source_target_pairs={{0,1},{1,0},{2,3},{3,2},{4,5},{5,4},{6,7},{7,6},{8,9},{9,8},{10,11... | collective-permute-start | bytes 15368 | tf_op jit(solution)/shard_map/ppermute | solution.py:189
  122.8 0.8 collective-permute-done.15
  123.7 0.6 slice_divide_fusion
  124.3 0.0 all-to-all-done.1.in_ref
  124.3 1.4 %shard_map.62 = f32[32,16384]{1,0:T(8,128)} custom-call(f32[128,32,128]{2,1,0:T(8,128)S(1)} %all-to-all-done.1.in_ref), custom_call_target="tpu_custom_call" | custom-call | tf_op jit(solution)/shard_map/pallas_call | solution.py:287
  (6 shorter events, 0.0 us)
Async XLA Ops:
  0.6 5.4 %collective-permute-start = (f32[32,16384]{1,0:T(8,128)}, f32[32,16384]{1,0:T(8,128)S(1)}, u32[]{:S(2)}, u32[]{:S(2)}) collective-permute-start(f32[32,16384]{1,0:T(8,128)} %panel_hbm.1), channel_id=1, source_target_pairs={{0,1},{1,0},{2,3},{3,2},{4,5},{5,4},{6,7},{7,6},{8,9},{9,8},{10,11... | collective-permute-start | bytes 6291464 | tf_op jit(solution)/shard_map/ppermute | solution.py:225
  0.7 5.3 %collective-permute-start.1 = (s32[16384]{0:T(1024)}, s32[16384]{0:T(1024)S(1)}, u32[]{:S(2)}, u32[]{:S(2)}) collective-permute-start(s32[16384]{0:T(1024)} %param.5), channel_id=1, source_target_pairs={{0,1},{1,0},{2,3},{3,2},{4,5},{5,4},{6,7},{7,6},{8,9},{9,8},{10,11... | collective-permute-start | bytes 196616 | tf_op jit(solution)/shard_map/ppermute | solution.py:226
  3.6 1.3 collective-permute-start.2
  4.8 2.6 %collective-permute-start.3 = (s32[1]{0:T(128)}, s32[1]{0:T(128)}, u32[]{:S(2)}, u32[]{:S(2)}) collective-permute-start(s32[1]{0:T(128)} %collective-permute-done.2), channel_id=1, source_target_pairs={{1,77},{3,79},{5,73},{7,75},{9,69},{11,71},{13,65},{15,67},{17,93}... | collective-permute-start | bytes 20 | tf_op jit(solution)/shard_map/ppermute | solution.py:189
  59.9 64.4 %all-to-all-start.1 = ((f32[128,32,128]{2,1,0:T(8,128)}), f32[128,32,128]{2,1,0:T(8,128)S(1)}, u32[]{:S(2)}, u32[]{:S(2)}) async-start(f32[128,32,128]{2,1,0:T(8,128)} %get-tuple-element.14.y_hbm), calls=%async_computation.1 | async-start | bytes 4194304 | tf_op jit(solution)/shard_map/all_to_all | solution.py:269
  73.7 18.4 %collective-permute-start.4 = (f32[40,32]{1,0:T(8,128)S(1)}, f32[40,32]{1,0:T(8,128)S(1)}, u32[]{:S(2)}, u32[]{:S(2)}) collective-permute-start(f32[40,32]{1,0:T(8,128)S(1)} %shard_map.63), channel_id=1, source_target_pairs={{0,1},{1,0},{2,3},{3,2},{4,5},{5,4},{6,7},{7,6},{8,9},{9,8},{10,11... | collective-permute-start | bytes 15368 | tf_op jit(solution)/shard_map/ppermute | solution.py:189
  92.0 4.7 %collective-permute-start.5 = (f32[40,32]{1,0:T(8,128)S(1)}, f32[40,32]{1,0:T(8,128)S(1)}, u32[]{:S(2)}, u32[]{:S(2)}) collective-permute-start(f32[40,32]{1,0:T(8,128)S(1)} %add.40), channel_id=1, source_target_pairs={{0,2},{1,3},{2,0},{3,1},{4,6},{5,7},{6,4},{7,5},{8,10},{9,11},{10,... | collective-permute-start | bytes 15368 | tf_op jit(solution)/shard_map/ppermute | solution.py:189
  93.5 5.3 %collective-permute-start.6 = (f32[40,32]{1,0:T(8,128)S(1)}, f32[40,32]{1,0:T(8,128)S(1)}, u32[]{:S(2)}, u32[]{:S(2)}) collective-permute-start(f32[40,32]{1,0:T(8,128)S(1)} %add.40), channel_id=1, source_target_pairs={{0,4},{1,5},{2,6},{3,7},{4,0},{5,1},{6,2},{7,3},{8,12},{9,13},{10,... | collective-permute-start | bytes 15368 | tf_op jit(solution)/shard_map/ppermute | solution.py:189
  96.2 5.1 %collective-permute-start.7 = (f32[40,32]{1,0:T(8,128)S(1)}, f32[40,32]{1,0:T(8,128)S(1)}, u32[]{:S(2)}, u32[]{:S(2)}) collective-permute-start(f32[40,32]{1,0:T(8,128)S(1)} %add.40), channel_id=1, source_target_pairs={{0,6},{1,7},{2,4},{3,5},{4,2},{5,3},{6,0},{7,1},{8,14},{9,15},{10,... | collective-permute-start | bytes 15368 | tf_op jit(solution)/shard_map/ppermute | solution.py:189
  101.3 4.3 %collective-permute-start.10 = (f32[40,32]{1,0:T(8,128)S(1)}, f32[40,32]{1,0:T(8,128)S(1)}, u32[]{:S(2)}, u32[]{:S(2)}) collective-permute-start(f32[40,32]{1,0:T(8,128)S(1)} %add_add_fusion.2), channel_id=1, source_target_pairs={{0,24},{1,25},{2,26},{3,27},{4,28},{5,29},{6,30},{7,31},{8,16},{9,... | collective-permute-start | bytes 15368 | tf_op jit(solution)/shard_map/ppermute | solution.py:189
  103.1 4.4 %collective-permute-start.8 = (f32[40,32]{1,0:T(8,128)S(1)}, f32[40,32]{1,0:T(8,128)S(1)}, u32[]{:S(2)}, u32[]{:S(2)}) collective-permute-start(f32[40,32]{1,0:T(8,128)S(1)} %add_add_fusion.2), channel_id=1, source_target_pairs={{0,16},{1,17},{2,18},{3,19},{4,20},{5,21},{6,22},{7,23},{8,24},{9,... | collective-permute-start | bytes 15368 | tf_op jit(solution)/shard_map/ppermute | solution.py:189
  105.6 5.8 %collective-permute-start.9 = (f32[40,32]{1,0:T(8,128)S(1)}, f32[40,32]{1,0:T(8,128)S(1)}, u32[]{:S(2)}, u32[]{:S(2)}) collective-permute-start(f32[40,32]{1,0:T(8,128)S(1)} %add_add_fusion.2), channel_id=1, source_target_pairs={{0,8},{1,9},{2,10},{3,11},{4,12},{5,13},{6,14},{7,15},{8,0},{9,1},... | collective-permute-start | bytes 15368 | tf_op jit(solution)/shard_map/ppermute | solution.py:189
  111.5 5.1 %collective-permute-start.11 = (f32[40,32]{1,0:T(8,128)S(1)}, f32[40,32]{1,0:T(8,128)S(1)}, u32[]{:S(2)}, u32[]{:S(2)}) collective-permute-start(f32[40,32]{1,0:T(8,128)S(1)} %add_add_fusion.1), channel_id=1, source_target_pairs={{1,129},{3,131},{5,133},{7,135},{9,137},{11,139},{13,141},{15,143}... | collective-permute-start | bytes 15368 | tf_op jit(solution)/shard_map/ppermute | solution.py:189
  112.1 4.7 %collective-permute-start.12 = (f32[40,32]{1,0:T(8,128)S(1)}, f32[40,32]{1,0:T(8,128)S(1)}, u32[]{:S(2)}, u32[]{:S(2)}) collective-permute-start(f32[40,32]{1,0:T(8,128)S(1)} %add_add_fusion.1), channel_id=1, source_target_pairs={{0,32},{1,161},{2,34},{3,163},{4,36},{5,165},{6,38},{7,167},{8,40}... | collective-permute-start | bytes 15368 | tf_op jit(solution)/shard_map/ppermute | solution.py:189
  112.6 5.2 %collective-permute-start.13 = (f32[40,32]{1,0:T(8,128)S(1)}, f32[40,32]{1,0:T(8,128)S(1)}, u32[]{:S(2)}, u32[]{:S(2)}) collective-permute-start(f32[40,32]{1,0:T(8,128)S(1)} %add_add_fusion.1), channel_id=1, source_target_pairs={{0,64},{1,193},{2,66},{3,195},{4,68},{5,197},{6,70},{7,199},{8,72}... | collective-permute-start | bytes 15368 | tf_op jit(solution)/shard_map/ppermute | solution.py:189
  115.2 5.9 %collective-permute-start.14 = (f32[40,32]{1,0:T(8,128)S(1)}, f32[40,32]{1,0:T(8,128)S(1)}, u32[]{:S(2)}, u32[]{:S(2)}) collective-permute-start(f32[40,32]{1,0:T(8,128)S(1)} %add_add_fusion.1), channel_id=1, source_target_pairs={{0,96},{1,225},{2,98},{3,227},{4,100},{5,229},{6,102},{7,231},{8,1... | collective-permute-start | bytes 15368 | tf_op jit(solution)/shard_map/ppermute | solution.py:189
  121.1 2.6 %collective-permute-start.15 = (f32[40,32]{1,0:T(8,128)S(1)}, f32[40,32]{1,0:T(8,128)S(1)}, u32[]{:S(2)}, u32[]{:S(2)}) collective-permute-start(f32[40,32]{1,0:T(8,128)S(1)} %add_add_fusion), channel_id=1, source_target_pairs={{0,1},{1,0},{2,3},{3,2},{4,5},{5,4},{6,7},{7,6},{8,9},{9,8},{10,11... | collective-permute-start | bytes 15368 | tf_op jit(solution)/shard_map/ppermute | solution.py:189
